TPU v7x, 1024 devices: a whole 4x4x32 slice. The times are simulated.
1024 devices in a mesh: seq: 128 (over z, y_hi, core), head: 8 (over x, y_lo).
Axes of the slice: x: 4, y: 4 (y_hi: 2, y_lo: 2; y = y_hi * 2 + y_lo), z: 32, core: 2. Of those that a mesh axis runs over, the one named last changes fastest.
Arguments:
- queries: bfloat16 [16384, 4096], P('seq', 'head'), may hold values from -192 to 192
- keys: bfloat16 [16384, 1024], P('seq', 'head'), may hold values from -5 to 5
- values: bfloat16 [16384, 1024], P('seq', 'head'), may hold values from -24 to 24
- segments: int32 [16384], replicated, may hold values from 0 to 5, never falling along the last dimension, each value on 1 to 5461 neighbouring positions
- out_weight: bfloat16 [4096, 8192], P(None, 'head'), may hold values from -0.09375 to 0.09375
Outputs:
- mixed: bfloat16 [16384, 8192], P('seq', 'head')
All inputs are finite; a program needn't handle non-finite values.
Results may differ from a plain program's by a relative error of at most 0.007.
Values may be sent and summed in bfloat16 or wider, within the bound.
No kernel may reach another device: no remote copies, remote signals or barrier semaphores. Data moves between devices by JAX's collectives and lax.ppermute only.
A program may use at most 32 MiB of HBM per device.

v0:
```python
import jax
import jax.numpy as jnp
from jax import lax
from jax.sharding import PartitionSpec as P

HD = 128
WIN_BLK = 31


masked_score = -1e30


def passed_along(block, axis, distance):
    devices = range(lax.axis_size(axis))
    route = [(i - distance, i) for i in devices if i - distance in devices]
    return lax.ppermute(block, axis, route)


def sent_to_all(value, axis):
    copies = jnp.broadcast_to(value, (lax.axis_size(axis), *value.shape))
    return lax.all_to_all(copies, axis, split_axis=0, concat_axis=0, tiled=True)


def joined_along(parts, dim):
    shape = list(parts.shape[1:])
    shape[dim] *= parts.shape[0]
    return jnp.moveaxis(parts, 0, dim).reshape(shape)


def collect(value, axis, dim):
    parts = sent_to_all(value, axis)
    return joined_along(parts, dim)


def allowed_keys(segments, query_pos, query_seg, key_first, key_count, window_len):
    key_pos = key_first + jnp.arange(key_count, dtype=jnp.int32)
    clipped = jnp.clip(key_pos, 0, segments.shape[0] - 1)
    key_seg = jnp.take(segments, clipped)
    allowed = key_pos[None, :] <= query_pos[:, None]
    allowed = allowed & (query_pos[:, None] - key_pos[None, :] < window_len)
    allowed = allowed & (key_pos[None, :] >= 0)
    return allowed & (key_seg[None, :] == query_seg[:, None])


def absorb(carry_state, query_heads, key_piece, value_piece, allowed):
    row_max, row_sum, accum = carry_state
    key_count = key_piece.shape[0]
    kv_heads = query_heads.shape[1]
    key_heads = key_piece.reshape(key_count, kv_heads, HD)
    value_heads = value_piece.reshape(key_count, kv_heads, HD)
    scores = jnp.einsum(
        "tagd,sad->agts", query_heads, key_heads, preferred_element_type=jnp.float32
    )
    scores = jnp.where(allowed[None, None], scores * HD ** (-0.5), masked_score)
    new_max = jnp.maximum(row_max, jnp.max(scores, axis=-1))
    weights = jnp.exp(scores - new_max[..., None])
    factor = jnp.exp(row_max - new_max)
    new_sum = row_sum * factor + jnp.sum(weights, axis=-1)
    update = jnp.einsum(
        "agts,sad->agtd",
        weights.astype(jnp.bfloat16),
        value_heads,
        preferred_element_type=jnp.float32,
    )
    return (new_max, new_sum, accum * factor[..., None] + update)


def on_device(queries, keys, values, segments, out_weight):
    row_count = queries.shape[0]
    kv_width = keys.shape[1]
    kv_heads = kv_width // HD
    group_size = queries.shape[1] // kv_width
    cycle_size = lax.axis_size("seq")
    position = lax.axis_index("seq")
    window_len = WIN_BLK * row_count
    reach_blocks = min(WIN_BLK, cycle_size - 1)
    own_first = position * row_count
    query_pos = own_first + jnp.arange(row_count, dtype=jnp.int32)
    query_seg = lax.dynamic_slice_in_dim(segments, own_first, row_count, 0)
    query_heads = queries.reshape(row_count, kv_heads, group_size, HD)
    start_state = (
        jnp.full((kv_heads, group_size, row_count), masked_score, jnp.float32),
        jnp.zeros((kv_heads, group_size, row_count), jnp.float32),
        jnp.zeros((kv_heads, group_size, row_count, HD), jnp.float32),
    )

    def take_block(carry_state, key_piece, value_piece, key_first):
        allowed = allowed_keys(
            segments, query_pos, query_seg, key_first, key_piece.shape[0], window_len
        )
        return lax.cond(
            jnp.any(allowed),
            lambda inner_state: absorb(inner_state, query_heads, key_piece, value_piece, allowed),
            lambda inner_state: inner_state,
            carry_state,
        )

    carry_state = take_block(start_state, keys, values, own_first)
    near_keys, near_values = passed_along((keys, values), "seq", 1)
    carry_state = take_block(carry_state, near_keys, near_values, own_first - row_count)
    pair_keys = jnp.concatenate([near_keys, keys], axis=0)
    pair_values = jnp.concatenate([near_values, values], axis=0)

    def pair_turn(turn_index, loop_carry):
        moving_keys, moving_values, inner_state = loop_carry
        moving_keys, moving_values = passed_along((moving_keys, moving_values), "seq", 2)
        key_first = own_first - (2 * turn_index + 3) * row_count
        inner_state = take_block(inner_state, moving_keys, moving_values, key_first)
        return (moving_keys, moving_values, inner_state)

    finished = lax.fori_loop(0, reach_blocks // 2, pair_turn, (pair_keys, pair_values, carry_state))
    carry_state = finished[2]
    row_max, row_sum, accum = carry_state
    attended = (accum / row_sum[..., None]).transpose(2, 0, 1, 3)
    attended = attended.reshape(row_count, queries.shape[1]).astype(jnp.bfloat16)
    mixed = jnp.dot(collect(attended, "head", 1), out_weight, preferred_element_type=jnp.float32)
    return mixed.astype(jnp.bfloat16)


def solution(mesh):
    return jax.shard_map(
        on_device,
        mesh=mesh,
        in_specs=(P("seq", "head"), P("seq", "head"), P("seq", "head"), P(), P(None, "head")),
        out_specs=P("seq", "head"),
        check_vma=False,
    )
```

profile of v0, /device:TPU:112, one launch (start us, length us, event | category | flops | bytes accessed | tf_op | source)
XLA Modules:
  0.0 242.0 jit_solution(9079854282287933171)
XLA Ops:
  1.9 4.9 %collective-permute-start.3 = (bf16[128,128]{1,0:T(8,128)(2,1)}, bf16[128,128]{1,0:T(8,128)(2,1)S(1)}, u32[]{:S(2)}, u32[]{:S(2)}) collective-permute-start(bf16[128,128]{1,0:T(8,128)(2,1)} %param.17), channel_id=1, source_target_pairs={{0,8},{8,16},{16,24},{24,32},{32,40},{40,48},{48,56},{56,64},{64,7... | collective-permute-start | bytes 98312 | tf_op jit(solution)/shard_map/ppermute | solution.py:16
  18.7 201.0 %while.23 = (s32[]{:T(128)}, bf16[256,128]{1,0:T(8,128)(2,1)S(1)}, bf16[256,128]{1,0:T(8,128)(2,1)S(1)}, f32[1,4,128]{2,1,0:T(4,128)S(1)}, f32[1,4,128]{2,1,0:T(...) while((s32[]{:T(128)}, bf16[256,128]{1,0:T(8,128)(2,1)S(1)}, ...), condition=%wide.region_16.18_spmd.clone.clone, body=%wide.region_10.17_spmd.clone.clone.sunk | while | flops 68426376 | bytes 3260811 | solution.py:111
  18.7 5.1 %collective-permute-start.1 = (bf16[256,128]{1,0:T(8,128)(2,1)S(1)}, bf16[256,128]{1,0:T(8,128)(2,1)S(1)}, u32[]{:S(2)}, u32[]{:S(2)}) collective-permute-start(bf16[256,128]{1,0:T(8,128)(2,1)S(1)} %get-tuple-element.515), channel_id=1, source_target_pairs={{0,16},{8,24},{16,32},{24,40},{32,48},{40,56},{48,64},{56,72},{64,... | collective-permute-start | bytes 196616 | tf_op jit(solution)/shard_map/while/body/eval_jaxpr/ppermute | solution.py:16
  23.8 3.6 %collective-permute-start = (bf16[256,128]{1,0:T(8,128)(2,1)S(1)}, bf16[256,128]{1,0:T(8,128)(2,1)S(1)}, u32[]{:S(2)}, u32[]{:S(2)}) collective-permute-start(bf16[256,128]{1,0:T(8,128)(2,1)S(1)} %get-tuple-element.514), channel_id=1, source_target_pairs={{0,16},{8,24},{16,32},{24,40},{32,48},{40,56},{48,64},{56,72},{64,... | collective-permute-start | bytes 196616 | tf_op jit(solution)/shard_map/while/body/eval_jaxpr/ppermute | solution.py:16
  32.3 5.7 %collective-permute-start.1 = (bf16[256,128]{1,0:T(8,128)(2,1)S(1)}, bf16[256,128]{1,0:T(8,128)(2,1)S(1)}, u32[]{:S(2)}, u32[]{:S(2)}) collective-permute-start(bf16[256,128]{1,0:T(8,128)(2,1)S(1)} %get-tuple-element.515), channel_id=1, source_target_pairs={{0,16},{8,24},{16,32},{24,40},{32,48},{40,56},{48,64},{56,72},{64,... | collective-permute-start | bytes 196616 | tf_op jit(solution)/shard_map/while/body/eval_jaxpr/ppermute | solution.py:16
  38.0 3.0 %collective-permute-start = (bf16[256,128]{1,0:T(8,128)(2,1)S(1)}, bf16[256,128]{1,0:T(8,128)(2,1)S(1)}, u32[]{:S(2)}, u32[]{:S(2)}) collective-permute-start(bf16[256,128]{1,0:T(8,128)(2,1)S(1)} %get-tuple-element.514), channel_id=1, source_target_pairs={{0,16},{8,24},{16,32},{24,40},{32,48},{40,56},{48,64},{56,72},{64,... | collective-permute-start | bytes 196616 | tf_op jit(solution)/shard_map/while/body/eval_jaxpr/ppermute | solution.py:16
  46.4 5.1 %collective-permute-start.1 = (bf16[256,128]{1,0:T(8,128)(2,1)S(1)}, bf16[256,128]{1,0:T(8,128)(2,1)S(1)}, u32[]{:S(2)}, u32[]{:S(2)}) collective-permute-start(bf16[256,128]{1,0:T(8,128)(2,1)S(1)} %get-tuple-element.515), channel_id=1, source_target_pairs={{0,16},{8,24},{16,32},{24,40},{32,48},{40,56},{48,64},{56,72},{64,... | collective-permute-start | bytes 196616 | tf_op jit(solution)/shard_map/while/body/eval_jaxpr/ppermute | solution.py:16
  60.0 4.6 %collective-permute-start.1 = (bf16[256,128]{1,0:T(8,128)(2,1)S(1)}, bf16[256,128]{1,0:T(8,128)(2,1)S(1)}, u32[]{:S(2)}, u32[]{:S(2)}) collective-permute-start(bf16[256,128]{1,0:T(8,128)(2,1)S(1)} %get-tuple-element.515), channel_id=1, source_target_pairs={{0,16},{8,24},{16,32},{24,40},{32,48},{40,56},{48,64},{56,72},{64,... | collective-permute-start | bytes 196616 | tf_op jit(solution)/shard_map/while/body/eval_jaxpr/ppermute | solution.py:16
  64.6 3.2 %collective-permute-start = (bf16[256,128]{1,0:T(8,128)(2,1)S(1)}, bf16[256,128]{1,0:T(8,128)(2,1)S(1)}, u32[]{:S(2)}, u32[]{:S(2)}) collective-permute-start(bf16[256,128]{1,0:T(8,128)(2,1)S(1)} %get-tuple-element.514), channel_id=1, source_target_pairs={{0,16},{8,24},{16,32},{24,40},{32,48},{40,56},{48,64},{56,72},{64,... | collective-permute-start | bytes 196616 | tf_op jit(solution)/shard_map/while/body/eval_jaxpr/ppermute | solution.py:16
  72.3 6.0 %collective-permute-start.1 = (bf16[256,128]{1,0:T(8,128)(2,1)S(1)}, bf16[256,128]{1,0:T(8,128)(2,1)S(1)}, u32[]{:S(2)}, u32[]{:S(2)}) collective-permute-start(bf16[256,128]{1,0:T(8,128)(2,1)S(1)} %get-tuple-element.515), channel_id=1, source_target_pairs={{0,16},{8,24},{16,32},{24,40},{32,48},{40,56},{48,64},{56,72},{64,... | collective-permute-start | bytes 196616 | tf_op jit(solution)/shard_map/while/body/eval_jaxpr/ppermute | solution.py:16
  78.3 3.0 %collective-permute-start = (bf16[256,128]{1,0:T(8,128)(2,1)S(1)}, bf16[256,128]{1,0:T(8,128)(2,1)S(1)}, u32[]{:S(2)}, u32[]{:S(2)}) collective-permute-start(bf16[256,128]{1,0:T(8,128)(2,1)S(1)} %get-tuple-element.514), channel_id=1, source_target_pairs={{0,16},{8,24},{16,32},{24,40},{32,48},{40,56},{48,64},{56,72},{64,... | collective-permute-start | bytes 196616 | tf_op jit(solution)/shard_map/while/body/eval_jaxpr/ppermute | solution.py:16
  86.0 5.1 %collective-permute-start.1 = (bf16[256,128]{1,0:T(8,128)(2,1)S(1)}, bf16[256,128]{1,0:T(8,128)(2,1)S(1)}, u32[]{:S(2)}, u32[]{:S(2)}) collective-permute-start(bf16[256,128]{1,0:T(8,128)(2,1)S(1)} %get-tuple-element.515), channel_id=1, source_target_pairs={{0,16},{8,24},{16,32},{24,40},{32,48},{40,56},{48,64},{56,72},{64,... | collective-permute-start | bytes 196616 | tf_op jit(solution)/shard_map/while/body/eval_jaxpr/ppermute | solution.py:16
  91.1 4.3 %collective-permute-start = (bf16[256,128]{1,0:T(8,128)(2,1)S(1)}, bf16[256,128]{1,0:T(8,128)(2,1)S(1)}, u32[]{:S(2)}, u32[]{:S(2)}) collective-permute-start(bf16[256,128]{1,0:T(8,128)(2,1)S(1)} %get-tuple-element.514), channel_id=1, source_target_pairs={{0,16},{8,24},{16,32},{24,40},{32,48},{40,56},{48,64},{56,72},{64,... | collective-permute-start | bytes 196616 | tf_op jit(solution)/shard_map/while/body/eval_jaxpr/ppermute | solution.py:16
  99.1 6.2 %collective-permute-start.1 = (bf16[256,128]{1,0:T(8,128)(2,1)S(1)}, bf16[256,128]{1,0:T(8,128)(2,1)S(1)}, u32[]{:S(2)}, u32[]{:S(2)}) collective-permute-start(bf16[256,128]{1,0:T(8,128)(2,1)S(1)} %get-tuple-element.515), channel_id=1, source_target_pairs={{0,16},{8,24},{16,32},{24,40},{32,48},{40,56},{48,64},{56,72},{64,... | collective-permute-start | bytes 196616 | tf_op jit(solution)/shard_map/while/body/eval_jaxpr/ppermute | solution.py:16
  105.3 2.9 %collective-permute-start = (bf16[256,128]{1,0:T(8,128)(2,1)S(1)}, bf16[256,128]{1,0:T(8,128)(2,1)S(1)}, u32[]{:S(2)}, u32[]{:S(2)}) collective-permute-start(bf16[256,128]{1,0:T(8,128)(2,1)S(1)} %get-tuple-element.514), channel_id=1, source_target_pairs={{0,16},{8,24},{16,32},{24,40},{32,48},{40,56},{48,64},{56,72},{64,... | collective-permute-start | bytes 196616 | tf_op jit(solution)/shard_map/while/body/eval_jaxpr/ppermute | solution.py:16
  113.3 4.7 %collective-permute-start.1 = (bf16[256,128]{1,0:T(8,128)(2,1)S(1)}, bf16[256,128]{1,0:T(8,128)(2,1)S(1)}, u32[]{:S(2)}, u32[]{:S(2)}) collective-permute-start(bf16[256,128]{1,0:T(8,128)(2,1)S(1)} %get-tuple-element.515), channel_id=1, source_target_pairs={{0,16},{8,24},{16,32},{24,40},{32,48},{40,56},{48,64},{56,72},{64,... | collective-permute-start | bytes 196616 | tf_op jit(solution)/shard_map/while/body/eval_jaxpr/ppermute | solution.py:16
  118.0 3.0 %collective-permute-start = (bf16[256,128]{1,0:T(8,128)(2,1)S(1)}, bf16[256,128]{1,0:T(8,128)(2,1)S(1)}, u32[]{:S(2)}, u32[]{:S(2)}) collective-permute-start(bf16[256,128]{1,0:T(8,128)(2,1)S(1)} %get-tuple-element.514), channel_id=1, source_target_pairs={{0,16},{8,24},{16,32},{24,40},{32,48},{40,56},{48,64},{56,72},{64,... | collective-permute-start | bytes 196616 | tf_op jit(solution)/shard_map/while/body/eval_jaxpr/ppermute | solution.py:16
  125.7 5.1 %collective-permute-start.1 = (bf16[256,128]{1,0:T(8,128)(2,1)S(1)}, bf16[256,128]{1,0:T(8,128)(2,1)S(1)}, u32[]{:S(2)}, u32[]{:S(2)}) collective-permute-start(bf16[256,128]{1,0:T(8,128)(2,1)S(1)} %get-tuple-element.515), channel_id=1, source_target_pairs={{0,16},{8,24},{16,32},{24,40},{32,48},{40,56},{48,64},{56,72},{64,... | collective-permute-start | bytes 196616 | tf_op jit(solution)/shard_map/while/body/eval_jaxpr/ppermute | solution.py:16
  130.8 3.5 %collective-permute-start = (bf16[256,128]{1,0:T(8,128)(2,1)S(1)}, bf16[256,128]{1,0:T(8,128)(2,1)S(1)}, u32[]{:S(2)}, u32[]{:S(2)}) collective-permute-start(bf16[256,128]{1,0:T(8,128)(2,1)S(1)} %get-tuple-element.514), channel_id=1, source_target_pairs={{0,16},{8,24},{16,32},{24,40},{32,48},{40,56},{48,64},{56,72},{64,... | collective-permute-start | bytes 196616 | tf_op jit(solution)/shard_map/while/body/eval_jaxpr/ppermute | solution.py:16
  138.7 5.5 %collective-permute-start.1 = (bf16[256,128]{1,0:T(8,128)(2,1)S(1)}, bf16[256,128]{1,0:T(8,128)(2,1)S(1)}, u32[]{:S(2)}, u32[]{:S(2)}) collective-permute-start(bf16[256,128]{1,0:T(8,128)(2,1)S(1)} %get-tuple-element.515), channel_id=1, source_target_pairs={{0,16},{8,24},{16,32},{24,40},{32,48},{40,56},{48,64},{56,72},{64,... | collective-permute-start | bytes 196616 | tf_op jit(solution)/shard_map/while/body/eval_jaxpr/ppermute | solution.py:16
  144.2 3.3 %collective-permute-start = (bf16[256,128]{1,0:T(8,128)(2,1)S(1)}, bf16[256,128]{1,0:T(8,128)(2,1)S(1)}, u32[]{:S(2)}, u32[]{:S(2)}) collective-permute-start(bf16[256,128]{1,0:T(8,128)(2,1)S(1)} %get-tuple-element.514), channel_id=1, source_target_pairs={{0,16},{8,24},{16,32},{24,40},{32,48},{40,56},{48,64},{56,72},{64,... | collective-permute-start | bytes 196616 | tf_op jit(solution)/shard_map/while/body/eval_jaxpr/ppermute | solution.py:16
  151.9 6.1 %collective-permute-start.1 = (bf16[256,128]{1,0:T(8,128)(2,1)S(1)}, bf16[256,128]{1,0:T(8,128)(2,1)S(1)}, u32[]{:S(2)}, u32[]{:S(2)}) collective-permute-start(bf16[256,128]{1,0:T(8,128)(2,1)S(1)} %get-tuple-element.515), channel_id=1, source_target_pairs={{0,16},{8,24},{16,32},{24,40},{32,48},{40,56},{48,64},{56,72},{64,... | collective-permute-start | bytes 196616 | tf_op jit(solution)/shard_map/while/body/eval_jaxpr/ppermute | solution.py:16
  165.7 4.7 %collective-permute-start.1 = (bf16[256,128]{1,0:T(8,128)(2,1)S(1)}, bf16[256,128]{1,0:T(8,128)(2,1)S(1)}, u32[]{:S(2)}, u32[]{:S(2)}) collective-permute-start(bf16[256,128]{1,0:T(8,128)(2,1)S(1)} %get-tuple-element.515), channel_id=1, source_target_pairs={{0,16},{8,24},{16,32},{24,40},{32,48},{40,56},{48,64},{56,72},{64,... | collective-permute-start | bytes 196616 | tf_op jit(solution)/shard_map/while/body/eval_jaxpr/ppermute | solution.py:16
  170.4 3.4 %collective-permute-start = (bf16[256,128]{1,0:T(8,128)(2,1)S(1)}, bf16[256,128]{1,0:T(8,128)(2,1)S(1)}, u32[]{:S(2)}, u32[]{:S(2)}) collective-permute-start(bf16[256,128]{1,0:T(8,128)(2,1)S(1)} %get-tuple-element.514), channel_id=1, source_target_pairs={{0,16},{8,24},{16,32},{24,40},{32,48},{40,56},{48,64},{56,72},{64,... | collective-permute-start | bytes 196616 | tf_op jit(solution)/shard_map/while/body/eval_jaxpr/ppermute | solution.py:16
  178.1 5.5 %collective-permute-start.1 = (bf16[256,128]{1,0:T(8,128)(2,1)S(1)}, bf16[256,128]{1,0:T(8,128)(2,1)S(1)}, u32[]{:S(2)}, u32[]{:S(2)}) collective-permute-start(bf16[256,128]{1,0:T(8,128)(2,1)S(1)} %get-tuple-element.515), channel_id=1, source_target_pairs={{0,16},{8,24},{16,32},{24,40},{32,48},{40,56},{48,64},{56,72},{64,... | collective-permute-start | bytes 196616 | tf_op jit(solution)/shard_map/while/body/eval_jaxpr/ppermute | solution.py:16
  183.6 3.2 %collective-permute-start = (bf16[256,128]{1,0:T(8,128)(2,1)S(1)}, bf16[256,128]{1,0:T(8,128)(2,1)S(1)}, u32[]{:S(2)}, u32[]{:S(2)}) collective-permute-start(bf16[256,128]{1,0:T(8,128)(2,1)S(1)} %get-tuple-element.514), channel_id=1, source_target_pairs={{0,16},{8,24},{16,32},{24,40},{32,48},{40,56},{48,64},{56,72},{64,... | collective-permute-start | bytes 196616 | tf_op jit(solution)/shard_map/while/body/eval_jaxpr/ppermute | solution.py:16
  191.3 5.3 %collective-permute-start.1 = (bf16[256,128]{1,0:T(8,128)(2,1)S(1)}, bf16[256,128]{1,0:T(8,128)(2,1)S(1)}, u32[]{:S(2)}, u32[]{:S(2)}) collective-permute-start(bf16[256,128]{1,0:T(8,128)(2,1)S(1)} %get-tuple-element.515), channel_id=1, source_target_pairs={{0,16},{8,24},{16,32},{24,40},{32,48},{40,56},{48,64},{56,72},{64,... | collective-permute-start | bytes 196616 | tf_op jit(solution)/shard_map/while/body/eval_jaxpr/ppermute | solution.py:16
  196.6 3.2 %collective-permute-start = (bf16[256,128]{1,0:T(8,128)(2,1)S(1)}, bf16[256,128]{1,0:T(8,128)(2,1)S(1)}, u32[]{:S(2)}, u32[]{:S(2)}) collective-permute-start(bf16[256,128]{1,0:T(8,128)(2,1)S(1)} %get-tuple-element.514), channel_id=1, source_target_pairs={{0,16},{8,24},{16,32},{24,40},{32,48},{40,56},{48,64},{56,72},{64,... | collective-permute-start | bytes 196616 | tf_op jit(solution)/shard_map/while/body/eval_jaxpr/ppermute | solution.py:16
  204.6 5.5 %collective-permute-start.1 = (bf16[256,128]{1,0:T(8,128)(2,1)S(1)}, bf16[256,128]{1,0:T(8,128)(2,1)S(1)}, u32[]{:S(2)}, u32[]{:S(2)}) collective-permute-start(bf16[256,128]{1,0:T(8,128)(2,1)S(1)} %get-tuple-element.515), channel_id=1, source_target_pairs={{0,16},{8,24},{16,32},{24,40},{32,48},{40,56},{48,64},{56,72},{64,... | collective-permute-start | bytes 196616 | tf_op jit(solution)/shard_map/while/body/eval_jaxpr/ppermute | solution.py:16
  210.1 3.7 %collective-permute-start = (bf16[256,128]{1,0:T(8,128)(2,1)S(1)}, bf16[256,128]{1,0:T(8,128)(2,1)S(1)}, u32[]{:S(2)}, u32[]{:S(2)}) collective-permute-start(bf16[256,128]{1,0:T(8,128)(2,1)S(1)} %get-tuple-element.514), channel_id=1, source_target_pairs={{0,16},{8,24},{16,32},{24,40},{32,48},{40,56},{48,64},{56,72},{64,... | collective-permute-start | bytes 196616 | tf_op jit(solution)/shard_map/while/body/eval_jaxpr/ppermute | solution.py:16
  220.0 16.5 %all_to_all.5 = bf16[8,128,512]{1,2,0:T(8,128)(2,1)S(1)} all-to-all(bf16[8,128,512]{1,2,0:T(8,128)(2,1)S(1)} %broadcast_in_dim.110), channel_id=1, replica_groups=mesh['seq'=128,'head'=8] {'head'}, dimensions={0} | all-to-all | bytes 2097152 | tf_op jit(solution)/shard_map/all_to_all | solution.py:21
  236.6 5.4 %convolution_convert_fusion = bf16[128,1024]{1,0:T(8,128)(2,1)} fusion(bf16[128,4096]{0,1:T(8,128)(2,1)S(1)} %bitcast.112, bf16[4096,1024]{1,0:T(8,128)(2,1)} %param.19), kind=kOutput, calls=%fused_computation.66 | convolution fusion | flops 1073872896 | bytes 9699328 | tf_op jit(solution)/shard_map/dot_general | solution.py:116
  (234 shorter events, 84.8 us)
Async XLA Ops:
  0.0 16.6 %collective-permute-start.2 = (bf16[128,128]{1,0:T(8,128)(2,1)}, bf16[128,128]{1,0:T(8,128)(2,1)S(1)}, u32[]{:S(2)}, u32[]{:S(2)}) collective-permute-start(bf16[128,128]{1,0:T(8,128)(2,1)} %param.16), channel_id=1, source_target_pairs={{0,8},{8,16},{16,24},{24,32},{32,40},{40,48},{48,56},{56,64},{64,7... | collective-permute-start | bytes 98312 | tf_op jit(solution)/shard_map/ppermute | solution.py:16
  1.9 14.7 %collective-permute-start.3 = (bf16[128,128]{1,0:T(8,128)(2,1)}, bf16[128,128]{1,0:T(8,128)(2,1)S(1)}, u32[]{:S(2)}, u32[]{:S(2)}) collective-permute-start(bf16[128,128]{1,0:T(8,128)(2,1)} %param.17), channel_id=1, source_target_pairs={{0,8},{8,16},{16,24},{24,32},{32,40},{40,48},{48,56},{56,64},{64,7... | collective-permute-start | bytes 98312 | tf_op jit(solution)/shard_map/ppermute | solution.py:16
  18.7 12.2 %collective-permute-start.1 = (bf16[256,128]{1,0:T(8,128)(2,1)S(1)}, bf16[256,128]{1,0:T(8,128)(2,1)S(1)}, u32[]{:S(2)}, u32[]{:S(2)}) collective-permute-start(bf16[256,128]{1,0:T(8,128)(2,1)S(1)} %get-tuple-element.515), channel_id=1, source_target_pairs={{0,16},{8,24},{16,32},{24,40},{32,48},{40,56},{48,64},{56,72},{64,... | collective-permute-start | bytes 196616 | tf_op jit(solution)/shard_map/while/body/eval_jaxpr/ppermute | solution.py:16
  23.8 7.7 %collective-permute-start = (bf16[256,128]{1,0:T(8,128)(2,1)S(1)}, bf16[256,128]{1,0:T(8,128)(2,1)S(1)}, u32[]{:S(2)}, u32[]{:S(2)}) collective-permute-start(bf16[256,128]{1,0:T(8,128)(2,1)S(1)} %get-tuple-element.514), channel_id=1, source_target_pairs={{0,16},{8,24},{16,32},{24,40},{32,48},{40,56},{48,64},{56,72},{64,... | collective-permute-start | bytes 196616 | tf_op jit(solution)/shard_map/while/body/eval_jaxpr/ppermute | solution.py:16
  32.3 12.2 %collective-permute-start.1 = (bf16[256,128]{1,0:T(8,128)(2,1)S(1)}, bf16[256,128]{1,0:T(8,128)(2,1)S(1)}, u32[]{:S(2)}, u32[]{:S(2)}) collective-permute-start(bf16[256,128]{1,0:T(8,128)(2,1)S(1)} %get-tuple-element.515), channel_id=1, source_target_pairs={{0,16},{8,24},{16,32},{24,40},{32,48},{40,56},{48,64},{56,72},{64,... | collective-permute-start | bytes 196616 | tf_op jit(solution)/shard_map/while/body/eval_jaxpr/ppermute | solution.py:16
  38.0 7.7 %collective-permute-start = (bf16[256,128]{1,0:T(8,128)(2,1)S(1)}, bf16[256,128]{1,0:T(8,128)(2,1)S(1)}, u32[]{:S(2)}, u32[]{:S(2)}) collective-permute-start(bf16[256,128]{1,0:T(8,128)(2,1)S(1)} %get-tuple-element.514), channel_id=1, source_target_pairs={{0,16},{8,24},{16,32},{24,40},{32,48},{40,56},{48,64},{56,72},{64,... | collective-permute-start | bytes 196616 | tf_op jit(solution)/shard_map/while/body/eval_jaxpr/ppermute | solution.py:16
  46.4 11.1 %collective-permute-start.1 = (bf16[256,128]{1,0:T(8,128)(2,1)S(1)}, bf16[256,128]{1,0:T(8,128)(2,1)S(1)}, u32[]{:S(2)}, u32[]{:S(2)}) collective-permute-start(bf16[256,128]{1,0:T(8,128)(2,1)S(1)} %get-tuple-element.515), channel_id=1, source_target_pairs={{0,16},{8,24},{16,32},{24,40},{32,48},{40,56},{48,64},{56,72},{64,... | collective-permute-start | bytes 196616 | tf_op jit(solution)/shard_map/while/body/eval_jaxpr/ppermute | solution.py:16
  51.5 7.7 %collective-permute-start = (bf16[256,128]{1,0:T(8,128)(2,1)S(1)}, bf16[256,128]{1,0:T(8,128)(2,1)S(1)}, u32[]{:S(2)}, u32[]{:S(2)}) collective-permute-start(bf16[256,128]{1,0:T(8,128)(2,1)S(1)} %get-tuple-element.514), channel_id=1, source_target_pairs={{0,16},{8,24},{16,32},{24,40},{32,48},{40,56},{48,64},{56,72},{64,... | collective-permute-start | bytes 196616 | tf_op jit(solution)/shard_map/while/body/eval_jaxpr/ppermute | solution.py:16
  60.0 11.3 %collective-permute-start.1 = (bf16[256,128]{1,0:T(8,128)(2,1)S(1)}, bf16[256,128]{1,0:T(8,128)(2,1)S(1)}, u32[]{:S(2)}, u32[]{:S(2)}) collective-permute-start(bf16[256,128]{1,0:T(8,128)(2,1)S(1)} %get-tuple-element.515), channel_id=1, source_target_pairs={{0,16},{8,24},{16,32},{24,40},{32,48},{40,56},{48,64},{56,72},{64,... | collective-permute-start | bytes 196616 | tf_op jit(solution)/shard_map/while/body/eval_jaxpr/ppermute | solution.py:16
  64.6 7.7 %collective-permute-start = (bf16[256,128]{1,0:T(8,128)(2,1)S(1)}, bf16[256,128]{1,0:T(8,128)(2,1)S(1)}, u32[]{:S(2)}, u32[]{:S(2)}) collective-permute-start(bf16[256,128]{1,0:T(8,128)(2,1)S(1)} %get-tuple-element.514), channel_id=1, source_target_pairs={{0,16},{8,24},{16,32},{24,40},{32,48},{40,56},{48,64},{56,72},{64,... | collective-permute-start | bytes 196616 | tf_op jit(solution)/shard_map/while/body/eval_jaxpr/ppermute | solution.py:16
  72.3 12.6 %collective-permute-start.1 = (bf16[256,128]{1,0:T(8,128)(2,1)S(1)}, bf16[256,128]{1,0:T(8,128)(2,1)S(1)}, u32[]{:S(2)}, u32[]{:S(2)}) collective-permute-start(bf16[256,128]{1,0:T(8,128)(2,1)S(1)} %get-tuple-element.515), channel_id=1, source_target_pairs={{0,16},{8,24},{16,32},{24,40},{32,48},{40,56},{48,64},{56,72},{64,... | collective-permute-start | bytes 196616 | tf_op jit(solution)/shard_map/while/body/eval_jaxpr/ppermute | solution.py:16
  78.3 7.7 %collective-permute-start = (bf16[256,128]{1,0:T(8,128)(2,1)S(1)}, bf16[256,128]{1,0:T(8,128)(2,1)S(1)}, u32[]{:S(2)}, u32[]{:S(2)}) collective-permute-start(bf16[256,128]{1,0:T(8,128)(2,1)S(1)} %get-tuple-element.514), channel_id=1, source_target_pairs={{0,16},{8,24},{16,32},{24,40},{32,48},{40,56},{48,64},{56,72},{64,... | collective-permute-start | bytes 196616 | tf_op jit(solution)/shard_map/while/body/eval_jaxpr/ppermute | solution.py:16
  86.0 13.0 %collective-permute-start.1 = (bf16[256,128]{1,0:T(8,128)(2,1)S(1)}, bf16[256,128]{1,0:T(8,128)(2,1)S(1)}, u32[]{:S(2)}, u32[]{:S(2)}) collective-permute-start(bf16[256,128]{1,0:T(8,128)(2,1)S(1)} %get-tuple-element.515), channel_id=1, source_target_pairs={{0,16},{8,24},{16,32},{24,40},{32,48},{40,56},{48,64},{56,72},{64,... | collective-permute-start | bytes 196616 | tf_op jit(solution)/shard_map/while/body/eval_jaxpr/ppermute | solution.py:16
  91.1 7.9 %collective-permute-start = (bf16[256,128]{1,0:T(8,128)(2,1)S(1)}, bf16[256,128]{1,0:T(8,128)(2,1)S(1)}, u32[]{:S(2)}, u32[]{:S(2)}) collective-permute-start(bf16[256,128]{1,0:T(8,128)(2,1)S(1)} %get-tuple-element.514), channel_id=1, source_target_pairs={{0,16},{8,24},{16,32},{24,40},{32,48},{40,56},{48,64},{56,72},{64,... | collective-permute-start | bytes 196616 | tf_op jit(solution)/shard_map/while/body/eval_jaxpr/ppermute | solution.py:16
  99.1 12.6 %collective-permute-start.1 = (bf16[256,128]{1,0:T(8,128)(2,1)S(1)}, bf16[256,128]{1,0:T(8,128)(2,1)S(1)}, u32[]{:S(2)}, u32[]{:S(2)}) collective-permute-start(bf16[256,128]{1,0:T(8,128)(2,1)S(1)} %get-tuple-element.515), channel_id=1, source_target_pairs={{0,16},{8,24},{16,32},{24,40},{32,48},{40,56},{48,64},{56,72},{64,... | collective-permute-start | bytes 196616 | tf_op jit(solution)/shard_map/while/body/eval_jaxpr/ppermute | solution.py:16
  105.3 8.0 %collective-permute-start = (bf16[256,128]{1,0:T(8,128)(2,1)S(1)}, bf16[256,128]{1,0:T(8,128)(2,1)S(1)}, u32[]{:S(2)}, u32[]{:S(2)}) collective-permute-start(bf16[256,128]{1,0:T(8,128)(2,1)S(1)} %get-tuple-element.514), channel_id=1, source_target_pairs={{0,16},{8,24},{16,32},{24,40},{32,48},{40,56},{48,64},{56,72},{64,... | collective-permute-start | bytes 196616 | tf_op jit(solution)/shard_map/while/body/eval_jaxpr/ppermute | solution.py:16
  113.3 11.2 %collective-permute-start.1 = (bf16[256,128]{1,0:T(8,128)(2,1)S(1)}, bf16[256,128]{1,0:T(8,128)(2,1)S(1)}, u32[]{:S(2)}, u32[]{:S(2)}) collective-permute-start(bf16[256,128]{1,0:T(8,128)(2,1)S(1)} %get-tuple-element.515), channel_id=1, source_target_pairs={{0,16},{8,24},{16,32},{24,40},{32,48},{40,56},{48,64},{56,72},{64,... | collective-permute-start | bytes 196616 | tf_op jit(solution)/shard_map/while/body/eval_jaxpr/ppermute | solution.py:16
  118.0 7.7 %collective-permute-start = (bf16[256,128]{1,0:T(8,128)(2,1)S(1)}, bf16[256,128]{1,0:T(8,128)(2,1)S(1)}, u32[]{:S(2)}, u32[]{:S(2)}) collective-permute-start(bf16[256,128]{1,0:T(8,128)(2,1)S(1)} %get-tuple-element.514), channel_id=1, source_target_pairs={{0,16},{8,24},{16,32},{24,40},{32,48},{40,56},{48,64},{56,72},{64,... | collective-permute-start | bytes 196616 | tf_op jit(solution)/shard_map/while/body/eval_jaxpr/ppermute | solution.py:16
  125.7 12.2 %collective-permute-start.1 = (bf16[256,128]{1,0:T(8,128)(2,1)S(1)}, bf16[256,128]{1,0:T(8,128)(2,1)S(1)}, u32[]{:S(2)}, u32[]{:S(2)}) collective-permute-start(bf16[256,128]{1,0:T(8,128)(2,1)S(1)} %get-tuple-element.515), channel_id=1, source_target_pairs={{0,16},{8,24},{16,32},{24,40},{32,48},{40,56},{48,64},{56,72},{64,... | collective-permute-start | bytes 196616 | tf_op jit(solution)/shard_map/while/body/eval_jaxpr/ppermute | solution.py:16
  130.8 7.8 %collective-permute-start = (bf16[256,128]{1,0:T(8,128)(2,1)S(1)}, bf16[256,128]{1,0:T(8,128)(2,1)S(1)}, u32[]{:S(2)}, u32[]{:S(2)}) collective-permute-start(bf16[256,128]{1,0:T(8,128)(2,1)S(1)} %get-tuple-element.514), channel_id=1, source_target_pairs={{0,16},{8,24},{16,32},{24,40},{32,48},{40,56},{48,64},{56,72},{64,... | collective-permute-start | bytes 196616 | tf_op jit(solution)/shard_map/while/body/eval_jaxpr/ppermute | solution.py:16
  138.7 12.3 %collective-permute-start.1 = (bf16[256,128]{1,0:T(8,128)(2,1)S(1)}, bf16[256,128]{1,0:T(8,128)(2,1)S(1)}, u32[]{:S(2)}, u32[]{:S(2)}) collective-permute-start(bf16[256,128]{1,0:T(8,128)(2,1)S(1)} %get-tuple-element.515), channel_id=1, source_target_pairs={{0,16},{8,24},{16,32},{24,40},{32,48},{40,56},{48,64},{56,72},{64,... | collective-permute-start | bytes 196616 | tf_op jit(solution)/shard_map/while/body/eval_jaxpr/ppermute | solution.py:16
  144.2 7.7 %collective-permute-start = (bf16[256,128]{1,0:T(8,128)(2,1)S(1)}, bf16[256,128]{1,0:T(8,128)(2,1)S(1)}, u32[]{:S(2)}, u32[]{:S(2)}) collective-permute-start(bf16[256,128]{1,0:T(8,128)(2,1)S(1)} %get-tuple-element.514), channel_id=1, source_target_pairs={{0,16},{8,24},{16,32},{24,40},{32,48},{40,56},{48,64},{56,72},{64,... | collective-permute-start | bytes 196616 | tf_op jit(solution)/shard_map/while/body/eval_jaxpr/ppermute | solution.py:16
  151.9 12.2 %collective-permute-start.1 = (bf16[256,128]{1,0:T(8,128)(2,1)S(1)}, bf16[256,128]{1,0:T(8,128)(2,1)S(1)}, u32[]{:S(2)}, u32[]{:S(2)}) collective-permute-start(bf16[256,128]{1,0:T(8,128)(2,1)S(1)} %get-tuple-element.515), channel_id=1, source_target_pairs={{0,16},{8,24},{16,32},{24,40},{32,48},{40,56},{48,64},{56,72},{64,... | collective-permute-start | bytes 196616 | tf_op jit(solution)/shard_map/while/body/eval_jaxpr/ppermute | solution.py:16
  158.0 7.7 %collective-permute-start = (bf16[256,128]{1,0:T(8,128)(2,1)S(1)}, bf16[256,128]{1,0:T(8,128)(2,1)S(1)}, u32[]{:S(2)}, u32[]{:S(2)}) collective-permute-start(bf16[256,128]{1,0:T(8,128)(2,1)S(1)} %get-tuple-element.514), channel_id=1, source_target_pairs={{0,16},{8,24},{16,32},{24,40},{32,48},{40,56},{48,64},{56,72},{64,... | collective-permute-start | bytes 196616 | tf_op jit(solution)/shard_map/while/body/eval_jaxpr/ppermute | solution.py:16
  165.7 11.7 %collective-permute-start.1 = (bf16[256,128]{1,0:T(8,128)(2,1)S(1)}, bf16[256,128]{1,0:T(8,128)(2,1)S(1)}, u32[]{:S(2)}, u32[]{:S(2)}) collective-permute-start(bf16[256,128]{1,0:T(8,128)(2,1)S(1)} %get-tuple-element.515), channel_id=1, source_target_pairs={{0,16},{8,24},{16,32},{24,40},{32,48},{40,56},{48,64},{56,72},{64,... | collective-permute-start | bytes 196616 | tf_op jit(solution)/shard_map/while/body/eval_jaxpr/ppermute | solution.py:16
  170.4 7.7 %collective-permute-start = (bf16[256,128]{1,0:T(8,128)(2,1)S(1)}, bf16[256,128]{1,0:T(8,128)(2,1)S(1)}, u32[]{:S(2)}, u32[]{:S(2)}) collective-permute-start(bf16[256,128]{1,0:T(8,128)(2,1)S(1)} %get-tuple-element.514), channel_id=1, source_target_pairs={{0,16},{8,24},{16,32},{24,40},{32,48},{40,56},{48,64},{56,72},{64,... | collective-permute-start | bytes 196616 | tf_op jit(solution)/shard_map/while/body/eval_jaxpr/ppermute | solution.py:16
  178.1 12.3 %collective-permute-start.1 = (bf16[256,128]{1,0:T(8,128)(2,1)S(1)}, bf16[256,128]{1,0:T(8,128)(2,1)S(1)}, u32[]{:S(2)}, u32[]{:S(2)}) collective-permute-start(bf16[256,128]{1,0:T(8,128)(2,1)S(1)} %get-tuple-element.515), channel_id=1, source_target_pairs={{0,16},{8,24},{16,32},{24,40},{32,48},{40,56},{48,64},{56,72},{64,... | collective-permute-start | bytes 196616 | tf_op jit(solution)/shard_map/while/body/eval_jaxpr/ppermute | solution.py:16
  183.6 7.7 %collective-permute-start = (bf16[256,128]{1,0:T(8,128)(2,1)S(1)}, bf16[256,128]{1,0:T(8,128)(2,1)S(1)}, u32[]{:S(2)}, u32[]{:S(2)}) collective-permute-start(bf16[256,128]{1,0:T(8,128)(2,1)S(1)} %get-tuple-element.514), channel_id=1, source_target_pairs={{0,16},{8,24},{16,32},{24,40},{32,48},{40,56},{48,64},{56,72},{64,... | collective-permute-start | bytes 196616 | tf_op jit(solution)/shard_map/while/body/eval_jaxpr/ppermute | solution.py:16
  191.3 12.0 %collective-permute-start.1 = (bf16[256,128]{1,0:T(8,128)(2,1)S(1)}, bf16[256,128]{1,0:T(8,128)(2,1)S(1)}, u32[]{:S(2)}, u32[]{:S(2)}) collective-permute-start(bf16[256,128]{1,0:T(8,128)(2,1)S(1)} %get-tuple-element.515), channel_id=1, source_target_pairs={{0,16},{8,24},{16,32},{24,40},{32,48},{40,56},{48,64},{56,72},{64,... | collective-permute-start | bytes 196616 | tf_op jit(solution)/shard_map/while/body/eval_jaxpr/ppermute | solution.py:16
  196.6 8.0 %collective-permute-start = (bf16[256,128]{1,0:T(8,128)(2,1)S(1)}, bf16[256,128]{1,0:T(8,128)(2,1)S(1)}, u32[]{:S(2)}, u32[]{:S(2)}) collective-permute-start(bf16[256,128]{1,0:T(8,128)(2,1)S(1)} %get-tuple-element.514), channel_id=1, source_target_pairs={{0,16},{8,24},{16,32},{24,40},{32,48},{40,56},{48,64},{56,72},{64,... | collective-permute-start | bytes 196616 | tf_op jit(solution)/shard_map/while/body/eval_jaxpr/ppermute | solution.py:16
  204.6 12.7 %collective-permute-start.1 = (bf16[256,128]{1,0:T(8,128)(2,1)S(1)}, bf16[256,128]{1,0:T(8,128)(2,1)S(1)}, u32[]{:S(2)}, u32[]{:S(2)}) collective-permute-start(bf16[256,128]{1,0:T(8,128)(2,1)S(1)} %get-tuple-element.515), channel_id=1, source_target_pairs={{0,16},{8,24},{16,32},{24,40},{32,48},{40,56},{48,64},{56,72},{64,... | collective-permute-start | bytes 196616 | tf_op jit(solution)/shard_map/while/body/eval_jaxpr/ppermute | solution.py:16
  210.1 9.5 %collective-permute-start = (bf16[256,128]{1,0:T(8,128)(2,1)S(1)}, bf16[256,128]{1,0:T(8,128)(2,1)S(1)}, u32[]{:S(2)}, u32[]{:S(2)}) collective-permute-start(bf16[256,128]{1,0:T(8,128)(2,1)S(1)} %get-tuple-element.514), channel_id=1, source_target_pairs={{0,16},{8,24},{16,32},{24,40},{32,48},{40,56},{48,64},{56,72},{64,... | collective-permute-start | bytes 196616 | tf_op jit(solution)/shard_map/while/body/eval_jaxpr/ppermute | solution.py:16
where the time goes:
time: 244 us; the launch traced here: 242 us
  starting transfers between devices  136 us (56%)
  local copies, waits for them, and re-layouts  37.1 us (15%)
  blocking collectives  16.5 us (7%)
  waiting for transfers between devices  16.3 us (7%)
  other arithmetic  15.5 us (6%)
  loops' own time  9.99 us (4%)
  matrix products  9.49 us (4%)
    ppermute x32, starting transfers between devices, passed_along(): return lax.ppermute(block, axis, route)  136 us
    gather x17, local copies, waits for them, and re-layouts, allowed_keys(): key_seg = jnp.take(segments, clipped)  34.7 us
    all_to_all x1, blocking collectives, sent_to_all(): return lax.all_to_all(copies, axis, split_axis=0, concat_axis=0, tiled=True)  16.5 us
    ppermute x32, waiting for transfers between devices, passed_along(): return lax.ppermute(block, axis, route)  16.3 us
    reduce_or x16, other arithmetic, take_block(): jnp.any(allowed)  12.9 us
    another operation x1, loops' own time, on_device(): lax.fori_loop(0, reach_blocks // 2, pair_turn, (pair_keys, pair_values, c...  9.8 us
    dot_general x1, matrix products, on_device(): jnp.dot(collect(attended, 'head', 1), out_weight, preferred_element_type=...  5.42 us
  transfers between devices with their start and end apart: 32, of which 14 were waited for; matrix products, arithmetic and copies ran while one was open for 22% of the time, Pallas kernels for 0%

commit v1 on v0

v1 whole, which is shorter than its diff:
```python
import functools

import jax
import jax.numpy as jnp
from jax import lax
from jax.experimental import pallas as pl
from jax.experimental.pallas import tpu as pltpu
from jax.sharding import Mesh, PartitionSpec as P

HD = 128
BLK = 128
GROUP = 4
LANES = 4
WINDOW = 31 * BLK
PLANE = LANES * BLK
ROWS = GROUP * BLK
PIECES = 16
HEADS = 8
SEGMENT_VALUES = 6
SCALE2 = float(HD**-0.5 * 1.4426950408889634)
MASKED = -1e30
VMEM = 24 * 1024 * 1024


def shift(block, distance):
    planes = lax.axis_size("z")
    return lax.ppermute(block, "z", [(i, i + distance) for i in range(planes - distance)])


def first_allowed(segments, plane):
    own = lax.dynamic_slice_in_dim(segments, plane * PLANE, PLANE, 0)
    position = plane * PLANE + jnp.arange(PLANE, dtype=jnp.int32)
    start = jnp.zeros((PLANE,), jnp.int32)
    for value in range(1, SEGMENT_VALUES):
        before = jnp.sum((segments < value).astype(jnp.int32))
        start = jnp.where(own == value, before, start)
    return jnp.maximum(start, position - (WINDOW - 1)).reshape(LANES, 1, BLK)


def attend(where_ref, q_ref, low_ref, blocks, distances, old_max):
    token_block = pl.program_id(0)
    own_key, plane_first = where_ref[0], where_ref[1]
    queries = jnp.concatenate([q_ref[0, :, g * HD : (g + 1) * HD] for g in range(GROUP)], axis=0)
    keys = jnp.concatenate([k for k in blocks], axis=0)
    scores = lax.dot_general(keys, queries, (((1,), (1,)), ((), ())), preferred_element_type=jnp.float32)
    low = jnp.concatenate([low_ref[0]] * GROUP, axis=1)
    sub = lax.broadcasted_iota(jnp.int32, (BLK, ROWS), 0)
    parts = []
    for n, distance in enumerate(distances):
        piece = scores[n * BLK : (n + 1) * BLK] * SCALE2
        first = own_key - distance * PLANE
        allowed = sub >= low - first
        if distance == 0:
            token = lax.broadcasted_iota(jnp.int32, (1, ROWS), 1) % BLK
            allowed = allowed & (sub <= plane_first + token_block * BLK + token - first)
        parts.append(jnp.where(allowed, piece, MASKED))
    top = functools.reduce(jnp.maximum, parts)
    top = jnp.max(top, axis=0, keepdims=True)
    if old_max is not None:
        top = jnp.maximum(top, old_max)
    weights = [jnp.exp2(piece - top) for piece in parts]
    total = jnp.sum(functools.reduce(jnp.add, weights), axis=0, keepdims=True)
    return top, total, jnp.concatenate([w.astype(jnp.bfloat16) for w in weights], axis=0)


def put_values(values_t, blocks):
    for n, block in enumerate(blocks):
        values_t[:, n * BLK : (n + 1) * BLK] = block.astype(jnp.float32).T.astype(jnp.bfloat16)


NEAR = (0, 1, 2, 3, 6)
FAR = (4, 7, 5, 8)


def near_kernel(where_ref, q_ref, low_ref, kv0, kv1, kv2, kv3, kv6, acc_ref, stat_ref, values_t):
    refs = (kv0, kv1, kv2, kv3, kv6)

    @pl.when(pl.program_id(0) == 0)
    def _():
        put_values(values_t, [r[:, HD:] for r in refs])

    top, total, weights = attend(where_ref, q_ref, low_ref, [r[:, :HD] for r in refs], NEAR, None)
    acc_ref[0] = jnp.dot(values_t[...], weights, preferred_element_type=jnp.float32)
    stat_ref[0, 0:1] = top
    stat_ref[0, 1:2] = total


def far_kernel(where_ref, q_ref, low_ref, one, two, acc_ref, stat_ref, out_ref, values_t):
    refs = (one, two)

    @pl.when(pl.program_id(0) == 0)
    def _():
        put_values(values_t, [r[i * BLK : (i + 1) * BLK, HD:] for r in refs for i in range(2)])

    old_max, old_total = stat_ref[0, 0:1], stat_ref[0, 1:2]
    keys = [r[:, :HD] for r in refs]
    top, total, weights = attend(where_ref, q_ref, low_ref, keys, FAR, old_max)
    factor = jnp.exp2(old_max - top)
    total = total + old_total * factor
    acc = acc_ref[0] * factor + jnp.dot(values_t[...], weights, preferred_element_type=jnp.float32)
    out_ref[0, :HD] = (acc / total).astype(jnp.bfloat16)
    spread = top + jnp.log2(total)
    high = spread.astype(jnp.bfloat16)
    rest = spread - high.astype(jnp.float32)
    middle = rest.astype(jnp.bfloat16)
    rest = rest - middle.astype(jnp.float32)
    row = lax.broadcasted_iota(jnp.int32, (PIECES, ROWS), 0)
    pieces = jnp.where(row == 0, high.astype(jnp.float32), jnp.where(row == 1, middle.astype(jnp.float32), jnp.where(row == 2, rest, 0.0)))
    out_ref[0, HD:] = pieces.astype(jnp.bfloat16)


def combine_kernel(parts_ref, out_ref):
    spread = []
    for p in range(LANES):
        pieces = parts_ref[p, HD:].astype(jnp.float32)
        spread.append(pieces[0:1] + pieces[1:2] + pieces[2:3])
    top = functools.reduce(jnp.maximum, spread)
    shares = [jnp.exp2(s - top) for s in spread]
    inverse = 1.0 / functools.reduce(jnp.add, shares)
    total = functools.reduce(
        jnp.add, [parts_ref[p, :HD].astype(jnp.float32) * (shares[p] * inverse) for p in range(LANES)]
    )
    for g in range(GROUP):
        head = total[:, g * BLK : (g + 1) * BLK].T.astype(jnp.bfloat16)
        for h in range(HEADS):
            out_ref[h, :, g * HD : (g + 1) * HD] = head


def project_kernel(rows_ref, weight_ref, out_ref, acc):
    step = pl.program_id(0)
    product = jnp.dot(rows_ref[0], weight_ref[...], preferred_element_type=jnp.float32)

    @pl.when(step == 0)
    def _():
        acc[...] = product

    @pl.when(step > 0)
    def _():
        acc[...] += product

    @pl.when(step == pl.num_programs(0) - 1)
    def _():
        out_ref[...] = acc[...].astype(jnp.bfloat16)


def whole(*shape):
    return pl.BlockSpec(shape, lambda i: (0,) * len(shape))


def stepped(*shape):
    return pl.BlockSpec((1, *shape), lambda i: (i,) + (0,) * len(shape))


def on_device(queries, keys, values, segments, out_weight):
    plane = lax.axis_index("z")
    lane = lax.axis_index("p")
    own = jnp.concatenate([keys, values], axis=1)
    from3, from6 = shift(own, 3), shift(own, 6)
    from1, from2 = shift(own, 1), shift(own, 2)
    pair = jnp.concatenate([from3, from6], axis=0)
    one, two = shift(pair, 1), shift(pair, 2)

    low = first_allowed(segments, plane)
    where = jnp.stack([plane * PLANE + lane * BLK, plane * PLANE]).astype(jnp.int32)
    plane_queries = lax.all_gather(queries, "p")

    smem = pl.BlockSpec(memory_space=pltpu.SMEM)
    params = pltpu.CompilerParams(vmem_limit_bytes=VMEM)
    acc, stat = pl.pallas_call(
        near_kernel,
        grid=(LANES,),
        out_shape=(
            jax.ShapeDtypeStruct((LANES, HD, ROWS), jnp.float32),
            jax.ShapeDtypeStruct((LANES, 8, ROWS), jnp.float32),
        ),
        in_specs=[smem, stepped(BLK, GROUP * HD), stepped(1, BLK)] + [whole(BLK, 2 * HD)] * 5,
        out_specs=(stepped(HD, ROWS), stepped(8, ROWS)),
        scratch_shapes=[pltpu.VMEM((HD, 5 * BLK), jnp.bfloat16)],
        compiler_params=params,
        cost_estimate=pl.CostEstimate(flops=4 * 2048 * 640 * 128, bytes_accessed=3 << 20, transcendentals=2048 * 640),
        name="near",
    )(where, plane_queries, low, own, from1, from2, from3, from6)
    partial = pl.pallas_call(
        far_kernel,
        grid=(LANES,),
        out_shape=jax.ShapeDtypeStruct((LANES, HD + PIECES, ROWS), jnp.bfloat16),
        in_specs=[smem, stepped(BLK, GROUP * HD), stepped(1, BLK)]
        + [whole(2 * BLK, 2 * HD)] * 2
        + [stepped(HD, ROWS), stepped(8, ROWS)],
        out_specs=stepped(HD + PIECES, ROWS),
        scratch_shapes=[pltpu.VMEM((HD, 4 * BLK), jnp.bfloat16)],
        compiler_params=params,
        cost_estimate=pl.CostEstimate(flops=4 * 2048 * 512 * 128, bytes_accessed=3 << 20, transcendentals=2048 * 512),
        name="far",
    )(where, plane_queries, low, one, two, acc, stat)
    parts = lax.all_to_all(partial, "p", 0, 0, tiled=True)
    copies = pl.pallas_call(
        combine_kernel,
        out_shape=jax.ShapeDtypeStruct((HEADS, BLK, GROUP * HD), jnp.bfloat16),
        compiler_params=params,
        cost_estimate=pl.CostEstimate(flops=4 * 128 * 512, bytes_accessed=2 << 20, transcendentals=2048),
        name="combine",
    )(parts)
    attended = lax.all_to_all(copies, "h", 0, 0, tiled=True)
    width = out_weight.shape[1]
    return pl.pallas_call(
        project_kernel,
        grid=(HEADS,),
        out_shape=jax.ShapeDtypeStruct((BLK, width), jnp.bfloat16),
        in_specs=[stepped(BLK, GROUP * HD), pl.BlockSpec((GROUP * HD, width), lambda i: (i, 0))],
        out_specs=whole(BLK, width),
        scratch_shapes=[pltpu.VMEM((BLK, width), jnp.float32)],
        compiler_params=params,
        cost_estimate=pl.CostEstimate(flops=2 * 128 * 4096 * 1024, bytes_accessed=9 << 20, transcendentals=0),
        name="project",
    )(attended, out_weight)


def solution(mesh):
    planes = mesh.shape["seq"] // LANES
    fine = Mesh(mesh.devices.reshape(planes, LANES, mesh.shape["head"]), ("z", "p", "h"))
    return jax.shard_map(
        on_device,
        mesh=fine,
        in_specs=(P(("z", "p"), "h"), P(("z", "p"), "h"), P(("z", "p"), "h"), P(), P(None, "h")),
        out_specs=P(("z", "p"), "h"),
        check_vma=False,
    )
```

time: 244 us -> 104 us (0.43)
  the two profiles are of different devices: /device:TPU:112 before, /device:TPU:96 now
where the time goes in v1:
time: 104 us; the launch traced here: 103 us
  blocking collectives  43 us (41%)
  starting transfers between devices  38.2 us (37%)
  Pallas kernels  11.2 us (11%)
  other arithmetic  6.04 us (6%)
  waiting for transfers between devices  3.34 us (3%)
  local copies, waits for them, and re-layouts  1.55 us (1%)
    ppermute x6, starting transfers between devices, shift(): lax.ppermute(block, 'z', [(i, i + distance) for i in range(planes - dista...  38.2 us
    all_to_all x1, blocking collectives, on_device(): attended = lax.all_to_all(copies, 'h', 0, 0, tiled=True)  19.5 us
    all_to_all x1, blocking collectives, on_device(): parts = lax.all_to_all(partial, 'p', 0, 0, tiled=True)  14.4 us
    all_gather x1, blocking collectives, on_device(): plane_queries = lax.all_gather(queries, 'p')  9.07 us
    max x1, other arithmetic, first_allowed(): return jnp.maximum(start, position - (WINDOW - 1)).reshape(LANES, 1, BLK)  4.35 us
    pallas_call x1, Pallas kernels, on_device(): pl.pallas_call(near_kernel, grid=(LANES,), out_shape=(jax.ShapeDtypeStruc...  3.9 us
    pallas_call x1, Pallas kernels, on_device(): pl.pallas_call(project_kernel, grid=(HEADS,), out_shape=jax.ShapeDtypeStr...  3.66 us
    pallas_call x1, Pallas kernels, on_device(): pl.pallas_call(far_kernel, grid=(LANES,), out_shape=jax.ShapeDtypeStruct(...  3.38 us
  transfers between devices with their start and end apart: 6, of which 1 were waited for; matrix products, arithmetic and copies ran while one was open for 6% of the time, Pallas kernels for 4%

profile of v1, /device:TPU:96, one launch (start us, length us, event | category | flops | bytes accessed | tf_op | source)
XLA Modules:
  0.0 103.5 jit_solution(17696400790418777938)
XLA Ops:
  0.0 0.8 constant_dynamic-update-slice_fusion.1
  0.8 0.8 constant_dynamic-update-slice_fusion.kv0
  1.5 6.4 %collective-permute-start.5 = (bf16[128,256]{1,0:T(8,128)(2,1)S(1)}, bf16[128,256]{1,0:T(8,128)(2,1)S(1)}, u32[]{:S(2)}, u32[]{:S(2)}) collective-permute-start(bf16[128,256]{1,0:T(8,128)(2,1)S(1)} %constant_dynamic-update-slice_fusion.kv0), channel_id=1, source_target_pairs={{0,64},{32,96},{64,128},{96,160},{128,192},{160,224},{192,256},{22... | collective-permute-start | bytes 196616 | tf_op jit(solution)/shard_map/ppermute | solution.py:27
  7.9 3.8 %collective-permute-start.4 = (bf16[128,256]{1,0:T(8,128)(2,1)S(1)}, bf16[128,256]{1,0:T(8,128)(2,1)S(1)}, u32[]{:S(2)}, u32[]{:S(2)}) collective-permute-start(bf16[128,256]{1,0:T(8,128)(2,1)S(1)} %constant_dynamic-update-slice_fusion.kv0), channel_id=1, source_target_pairs={{0,32},{32,64},{64,96},{96,128},{128,160},{160,192},{192,224},{224... | collective-permute-start | bytes 196616 | tf_op jit(solution)/shard_map/ppermute | solution.py:27
  11.8 13.0 %collective-permute-start.1 = (bf16[128,256]{1,0:T(8,128)(2,1)S(1)}, bf16[128,256]{1,0:T(8,128)(2,1)S(1)}, u32[]{:S(2)}, u32[]{:S(2)}) collective-permute-start(bf16[128,256]{1,0:T(8,128)(2,1)S(1)} %constant_dynamic-update-slice_fusion.kv0), channel_id=1, source_target_pairs={{0,192},{32,224},{64,256},{96,288},{128,320},{160,352},{192,384},{... | collective-permute-start | bytes 196616 | tf_op jit(solution)/shard_map/ppermute | solution.py:27
  24.8 6.5 %collective-permute-start = (bf16[128,256]{1,0:T(8,128)(2,1)S(1)}, bf16[128,256]{1,0:T(8,128)(2,1)S(1)}, u32[]{:S(2)}, u32[]{:S(2)}) collective-permute-start(bf16[128,256]{1,0:T(8,128)(2,1)S(1)} %constant_dynamic-update-slice_fusion.kv0), channel_id=1, source_target_pairs={{0,96},{32,128},{64,160},{96,192},{128,224},{160,256},{192,288},{2... | collective-permute-start | bytes 196616 | tf_op jit(solution)/shard_map/ppermute | solution.py:27
  31.3 1.6 %convert_reduce_fusion.4 = (s32[]{:T(128)}, s32[]{:T(128)}, s32[]{:T(128)}, s32[]{:T(128)}, s32[]{:T(128)}) fusion(s32[16384]{0:T(1024)} %param.8), kind=kLoop, calls=%fused_computation.4 | loop fusion | flops 245755 | bytes 65556 | tf_op jit(solution)/shard_map/reduce_sum | solution.py:35
  32.9 9.1 %all-gather = bf16[512,512]{1,0:T(8,128)(2,1)S(1)} all-gather(bf16[128,512]{1,0:T(8,128)(2,1)} %param.5), channel_id=2, replica_groups=mesh['z'=32,'p'=4,'h'=8] {'p'}, dimensions={0}, use_global_device_ids=true | all-gather | bytes 655360 | tf_op jit(solution)/shard_map/all_gather | solution.py:165
  42.0 0.0 copy-start
  42.0 4.4 %add_maximum_fusion = s32[512]{0:T(512)S(1)} fusion(s32[16384]{0:T(1024)} %param.8, s32[]{:T(128)S(6)} %select_n.19, s32[]{:T(128)} %mul.4, s32[]{:T(128)} %get-tuple-element.12, s32[]{:T(128)} %get-tuple-element.13, s32[]{:T(128)} %get-tuple-element.10, s32[]{:T(128)} %get-tuple-element.11, s32[]{:T(128)} %get-tuple-element.9), kind=kLoop, calls=%fused_computation.9 | loop fusion | flops 6656 | bytes 4124 | tf_op jit(solution)/shard_map/max | solution.py:37
  46.4 0.0 collective-permute-done.kv3
  46.4 0.0 collective-permute-done.1.kv6
  46.4 5.5 %collective-permute-start.3 = (bf16[256,256]{1,0:T(8,128)(2,1)S(1)}, bf16[256,256]{1,0:T(8,128)(2,1)S(1)}, u32[]{:S(2)}, u32[]{:S(2)}) collective-permute-start(bf16[256,256]{1,0:T(8,128)(2,1)S(1)} %constant_dynamic-update-slice_fusion.2), channel_id=1, source_target_pairs={{0,64},{32,96},{64,128},{96,160},{128,192},{160,224},{192,256},{22... | collective-permute-start | bytes 393224 | tf_op jit(solution)/shard_map/ppermute | solution.py:27
  51.9 2.9 %collective-permute-start.2 = (bf16[256,256]{1,0:T(8,128)(2,1)S(1)}, bf16[256,256]{1,0:T(8,128)(2,1)S(1)}, u32[]{:S(2)}, u32[]{:S(2)}) collective-permute-start(bf16[256,256]{1,0:T(8,128)(2,1)S(1)} %constant_dynamic-update-slice_fusion.2), channel_id=1, source_target_pairs={{0,32},{32,64},{64,96},{96,128},{128,160},{160,192},{192,224},{224... | collective-permute-start | bytes 393224 | tf_op jit(solution)/shard_map/ppermute | solution.py:27
  54.8 0.1 pad_add_fusion.where_ref
  54.9 0.0 collective-permute-done.5.kv2
  54.9 0.0 collective-permute-done.4.kv1
  54.9 3.9 %near.1 = (f32[4,128,512]{2,1,0:T(8,128)S(1)}, f32[4,8,512]{2,1,0:T(8,128)S(1)}) custom-call(s32[2]{0:T(128)S(1)} %pad_add_fusion.where_ref, bf16[4,128,512]{2,1,0:T(8,128)(2,1)S(1)} %bitcast.4, s32[4,1,128]{2,1,0:T(1,128)S(1)} %bitcast.6, bf16[128,256]{1,0:T(8,128)(2,1)S(1)} %constant_dynamic-update-slice_fusion.kv0, ...), custom_call_target="tpu_custom_call" | custom-call | flops 671088640 | bytes 3145728 | tf_op jit(solution)/shard_map/near/pallas_call | solution.py:169
  58.8 0.0 collective-permute-done.3.two
  58.8 3.3 %collective-permute-done.2.one = bf16[256,256]{1,0:T(8,128)(2,1)S(1)} collective-permute-done((bf16[256,256]{1,0:T(8,128)(2,1)S(1)}, bf16[256,256]{1,0:T(8,128)(2,1)S(1)}, u32[]{:S(2)}, u32[]{:S(2)}) %collective-permute-start.2) | collective-permute-done | bytes 131104 | tf_op jit(solution)/shard_map/ppermute | solution.py:27
  62.2 3.4 %far.1 = bf16[4,144,512]{2,1,0:T(8,128)(2,1)S(1)} custom-call(s32[2]{0:T(128)S(1)} %pad_add_fusion.where_ref, bf16[4,128,512]{2,1,0:T(8,128)(2,1)S(1)} %bitcast.5, s32[4,1,128]{2,1,0:T(1,128)S(1)} %bitcast.7, bf16[256,256]{1,0:T(8,128)(2,1)S(1)} %collective-permute-done.2.one, bf16[256,256]{1,0:T(8,128)(2,1)S(1)} %collective-permute-done.3.two, ...), custom_call_target="tpu_custom_call" | custom-call | flops 536870912 | bytes 3145728 | tf_op jit(solution)/shard_map/far/pallas_call | solution.py:183
  65.6 14.4 %all_to_all.10.parts_ref = bf16[4,144,512]{2,1,0:T(8,128)(2,1)S(1)} all-to-all(bf16[4,144,512]{2,1,0:T(8,128)(2,1)S(1)} %far.1), channel_id=1, replica_groups=mesh['z'=32,'p'=4,'h'=8] {'p'}, dimensions={0} | all-to-all | bytes 1179648 | tf_op jit(solution)/shard_map/all_to_all | solution.py:196
  80.0 0.3 combine.1
  80.3 19.5 %all_to_all.11.rows_ref = bf16[8,128,512]{2,1,0:T(8,128)(2,1)S(1)} all-to-all(bf16[8,128,512]{2,1,0:T(8,128)(2,1)S(1)} %combine.1), channel_id=1, replica_groups=mesh['z'=32,'p'=4,'h'=8] {'h'}, dimensions={0} | all-to-all | bytes 2097152 | tf_op jit(solution)/shard_map/all_to_all | solution.py:204
  99.8 0.0 copy-done
  99.8 3.7 %project.1 = bf16[128,1024]{1,0:T(8,128)(2,1)} custom-call(bf16[8,128,512]{2,1,0:T(8,128)(2,1)S(1)} %all_to_all.11.rows_ref, bf16[4096,1024]{1,0:T(8,128)(2,1)S(1)} %copy-done), custom_call_target="tpu_custom_call" | custom-call | flops 1073741824 | bytes 9437184 | tf_op jit(solution)/shard_map/project/pallas_call | solution.py:206
  (2 shorter events, 0.0 us)
Async XLA Ops:
  1.5 53.4 %collective-permute-start.5 = (bf16[128,256]{1,0:T(8,128)(2,1)S(1)}, bf16[128,256]{1,0:T(8,128)(2,1)S(1)}, u32[]{:S(2)}, u32[]{:S(2)}) collective-permute-start(bf16[128,256]{1,0:T(8,128)(2,1)S(1)} %constant_dynamic-update-slice_fusion.kv0), channel_id=1, source_target_pairs={{0,64},{32,96},{64,128},{96,160},{128,192},{160,224},{192,256},{22... | collective-permute-start | bytes 196616 | tf_op jit(solution)/shard_map/ppermute | solution.py:27
  7.9 47.0 %collective-permute-start.4 = (bf16[128,256]{1,0:T(8,128)(2,1)S(1)}, bf16[128,256]{1,0:T(8,128)(2,1)S(1)}, u32[]{:S(2)}, u32[]{:S(2)}) collective-permute-start(bf16[128,256]{1,0:T(8,128)(2,1)S(1)} %constant_dynamic-update-slice_fusion.kv0), channel_id=1, source_target_pairs={{0,32},{32,64},{64,96},{96,128},{128,160},{160,192},{192,224},{224... | collective-permute-start | bytes 196616 | tf_op jit(solution)/shard_map/ppermute | solution.py:27
  11.8 34.6 %collective-permute-start.1 = (bf16[128,256]{1,0:T(8,128)(2,1)S(1)}, bf16[128,256]{1,0:T(8,128)(2,1)S(1)}, u32[]{:S(2)}, u32[]{:S(2)}) collective-permute-start(bf16[128,256]{1,0:T(8,128)(2,1)S(1)} %constant_dynamic-update-slice_fusion.kv0), channel_id=1, source_target_pairs={{0,192},{32,224},{64,256},{96,288},{128,320},{160,352},{192,384},{... | collective-permute-start | bytes 196616 | tf_op jit(solution)/shard_map/ppermute | solution.py:27
  24.8 21.6 %collective-permute-start = (bf16[128,256]{1,0:T(8,128)(2,1)S(1)}, bf16[128,256]{1,0:T(8,128)(2,1)S(1)}, u32[]{:S(2)}, u32[]{:S(2)}) collective-permute-start(bf16[128,256]{1,0:T(8,128)(2,1)S(1)} %constant_dynamic-update-slice_fusion.kv0), channel_id=1, source_target_pairs={{0,96},{32,128},{64,160},{96,192},{128,224},{160,256},{192,288},{2... | collective-permute-start | bytes 196616 | tf_op jit(solution)/shard_map/ppermute | solution.py:27
  42.0 57.8 %copy-start = (bf16[4096,1024]{1,0:T(8,128)(2,1)S(1)}, bf16[4096,1024]{1,0:T(8,128)(2,1)}, u32[]{:S(2)}) copy-start(bf16[4096,1024]{1,0:T(8,128)(2,1)} %weight_ref.1) | copy-start | bytes 25165828
  46.4 12.4 %collective-permute-start.3 = (bf16[256,256]{1,0:T(8,128)(2,1)S(1)}, bf16[256,256]{1,0:T(8,128)(2,1)S(1)}, u32[]{:S(2)}, u32[]{:S(2)}) collective-permute-start(bf16[256,256]{1,0:T(8,128)(2,1)S(1)} %constant_dynamic-update-slice_fusion.2), channel_id=1, source_target_pairs={{0,64},{32,96},{64,128},{96,160},{128,192},{160,224},{192,256},{22... | collective-permute-start | bytes 393224 | tf_op jit(solution)/shard_map/ppermute | solution.py:27
  51.9 10.3 %collective-permute-start.2 = (bf16[256,256]{1,0:T(8,128)(2,1)S(1)}, bf16[256,256]{1,0:T(8,128)(2,1)S(1)}, u32[]{:S(2)}, u32[]{:S(2)}) collective-permute-start(bf16[256,256]{1,0:T(8,128)(2,1)S(1)} %constant_dynamic-update-slice_fusion.2), channel_id=1, source_target_pairs={{0,32},{32,64},{64,96},{96,128},{128,160},{160,192},{192,224},{224... | collective-permute-start | bytes 393224 | tf_op jit(solution)/shard_map/ppermute | solution.py:27

commit v2 on v0

v2 whole, which is shorter than its diff:
```python
import functools

import jax
import jax.numpy as jnp
from jax import lax
from jax.experimental import pallas as pl
from jax.experimental.pallas import tpu as pltpu
from jax.sharding import Mesh, PartitionSpec as P

HD = 128
BLK = 128
GROUP = 4
PAIR = 2
LANES = 4
WINDOW = 31 * BLK
PLANE = LANES * BLK
ROWS = GROUP * BLK
PIECES = 16
HEADS = 8
SEGMENT_VALUES = 6
SCALE2 = float(HD**-0.5 * 1.4426950408889634)
MASKED = -1e30
VMEM = 24 * 1024 * 1024
PARAMS = pltpu.CompilerParams(vmem_limit_bytes=VMEM)
SMEM = pl.BlockSpec(memory_space=pltpu.SMEM)
VREF = pl.BlockSpec(memory_space=pltpu.VMEM)
STATE = (
    jax.ShapeDtypeStruct((LANES, HD, ROWS), jnp.float32),
    jax.ShapeDtypeStruct((LANES, 8, ROWS), jnp.float32),
)


def shift(block, distance):
    planes = lax.axis_size("z")
    return lax.ppermute(block, "z", [(i, i + distance) for i in range(planes - distance)])


def pack_kernel(key_ref, value_ref, out_ref, sems):
    key_copy = pltpu.make_async_copy(key_ref, out_ref.at[:, pl.ds(0, HD)], sems.at[0])
    value_copy = pltpu.make_async_copy(value_ref, out_ref.at[:, pl.ds(HD, HD)], sems.at[1])
    key_copy.start()
    value_copy.start()
    key_copy.wait()
    value_copy.wait()


def trio_kernel(own_ref, from3_ref, from6_ref, out_ref):
    for n, ref in enumerate((own_ref, from3_ref, from6_ref)):
        out_ref[n * BLK : (n + 1) * BLK] = ref[...]


def low_kernel(where_ref, segment_ref, out_ref):
    segments = segment_ref[...]
    before = [jnp.sum((segments < v).astype(jnp.int32)) for v in range(1, SEGMENT_VALUES)]
    token = lax.broadcasted_iota(jnp.int32, (1, BLK), 1)
    for p in range(LANES):
        own = segment_ref[pl.ds(where_ref[1] * LANES + p, 1), :]
        start = jnp.zeros((1, BLK), jnp.int32)
        for v in range(1, SEGMENT_VALUES):
            start = jnp.where(own == v, before[v - 1], start)
        position = where_ref[1] * PLANE + p * BLK + token
        out_ref[p : p + 1] = jnp.maximum(start, position - (WINDOW - 1))
    out_ref[LANES:] = jnp.zeros((8 - LANES, BLK), jnp.int32)


def attend_kernel(distances, first, last, where_ref, mine_ref, other_ref, low_ref, kv_ref, *refs):
    old, refs = ((), refs) if first else (refs[:2], refs[2:])
    own_key, plane_first, side = where_ref[0], where_ref[1] * PLANE, where_ref[2]
    keys = kv_ref[:, :HD]
    values_t = kv_ref[:, HD:].astype(jnp.float32).T.astype(jnp.bfloat16)
    sub = lax.broadcasted_iota(jnp.int32, (BLK, ROWS), 0)
    for index in range(LANES):
        query_ref, core = (mine_ref, other_ref)[index // PAIR], index % PAIR
        block = core + PAIR * (side if index < PAIR else 1 - side)
        rows = slice(core * BLK, (core + 1) * BLK)
        queries = jnp.concatenate([query_ref[rows, g * HD : (g + 1) * HD] for g in range(GROUP)], axis=0)
        scores = lax.dot_general(keys, queries, (((1,), (1,)), ((), ())), preferred_element_type=jnp.float32)
        low = jnp.concatenate([low_ref[pl.ds(block, 1), :]] * GROUP, axis=1)
        parts = []
        for n, distance in enumerate(distances):
            key_first = own_key - distance * PLANE
            allowed = sub >= low - key_first
            if distance == 0:
                token = lax.broadcasted_iota(jnp.int32, (1, ROWS), 1) % BLK
                allowed = allowed & (sub <= plane_first + block * BLK + token - key_first)
            parts.append(jnp.where(allowed, scores[n * BLK : (n + 1) * BLK] * SCALE2, MASKED))
        top = jnp.max(functools.reduce(jnp.maximum, parts), axis=0, keepdims=True)
        if not first:
            old_top = old[1][index, 0:1]
            top = jnp.maximum(top, old_top)
        weights = [jnp.exp2(piece - top) for piece in parts]
        total = jnp.sum(functools.reduce(jnp.add, weights), axis=0, keepdims=True)
        weights = jnp.concatenate([w.astype(jnp.bfloat16) for w in weights], axis=0)
        acc = jnp.dot(values_t, weights, preferred_element_type=jnp.float32)
        if not first:
            factor = jnp.exp2(old_top - top)
            total = total + old[1][index, 1:2] * factor
            acc = acc + old[0][index] * factor
        if not last:
            refs[0][index] = acc
            refs[1][index, 0:1] = top
            refs[1][index, 1:2] = total
            continue
        refs[0][block, :HD] = (acc / total).astype(jnp.bfloat16)
        spread = top + jnp.log2(total)
        high = spread.astype(jnp.bfloat16)
        rest = spread - high.astype(jnp.float32)
        middle = rest.astype(jnp.bfloat16)
        rest = rest - middle.astype(jnp.float32)
        row = lax.broadcasted_iota(jnp.int32, (PIECES, ROWS), 0)
        pieces = jnp.where(row == 0, high.astype(jnp.float32), jnp.where(row == 1, middle.astype(jnp.float32), jnp.where(row == 2, rest, 0.0)))
        refs[0][block, HD:] = pieces.astype(jnp.bfloat16)


def attend(name, distances, first, last, *args):
    out = jax.ShapeDtypeStruct((LANES, HD + PIECES, ROWS), jnp.bfloat16) if last else STATE
    pairs = LANES * ROWS * len(distances) * BLK
    return pl.pallas_call(
        functools.partial(attend_kernel, distances, first, last),
        out_shape=out,
        in_specs=[SMEM] + [VREF] * (len(args) - 1),
        out_specs=VREF if last else (VREF, VREF),
        compiler_params=PARAMS,
        cost_estimate=pl.CostEstimate(flops=4 * pairs * HD, bytes_accessed=3 << 20, transcendentals=pairs),
        name=name,
    )(*args)


def combine_kernel(parts_ref, out_ref):
    spread = []
    for p in range(LANES):
        pieces = parts_ref[p, HD:].astype(jnp.float32)
        spread.append(pieces[0:1] + pieces[1:2] + pieces[2:3])
    top = functools.reduce(jnp.maximum, spread)
    shares = [jnp.exp2(s - top) for s in spread]
    inverse = 1.0 / functools.reduce(jnp.add, shares)
    total = functools.reduce(
        jnp.add, [parts_ref[p, :HD].astype(jnp.float32) * (shares[p] * inverse) for p in range(LANES)]
    )
    for g in range(GROUP):
        head = total[:, g * BLK : (g + 1) * BLK].T.astype(jnp.bfloat16)
        for h in range(HEADS):
            out_ref[h, :, g * HD : (g + 1) * HD] = head


def project_kernel(rows_ref, weight_ref, out_ref):
    depth = rows_ref.shape[2]
    acc = functools.reduce(
        jnp.add,
        [
            jnp.dot(rows_ref[h], weight_ref[h * depth : (h + 1) * depth, :], preferred_element_type=jnp.float32)
            for h in range(HEADS)
        ],
    )
    out_ref[...] = acc.astype(jnp.bfloat16)


def small(kernel, name, shape, dtype, *args, smem=0, params=PARAMS):
    return pl.pallas_call(
        kernel,
        out_shape=jax.ShapeDtypeStruct(shape, dtype),
        in_specs=[SMEM] * smem + [VREF] * (len(args) - smem),
        out_specs=VREF,
        compiler_params=params,
        cost_estimate=pl.CostEstimate(flops=1 << 20, bytes_accessed=1 << 19, transcendentals=0),
        name=name,
    )(*args)


def pack(keys, values):
    return pl.pallas_call(
        pack_kernel,
        out_shape=jax.ShapeDtypeStruct((BLK, 2 * HD), keys.dtype),
        in_specs=[pl.BlockSpec(memory_space=pltpu.HBM)] * 2,
        out_specs=VREF,
        scratch_shapes=[pltpu.SemaphoreType.DMA((2,))],
        compiler_params=PARAMS,
        cost_estimate=pl.CostEstimate(flops=0, bytes_accessed=1 << 17, transcendentals=0),
        name="pack",
    )(keys, values)


def on_device(queries, keys, values, segments, out_weight):
    plane, side, core = lax.axis_index("z"), lax.axis_index("y"), lax.axis_index("c")
    where = jnp.stack([plane * PLANE + (side * PAIR + core) * BLK, plane, side]).astype(jnp.int32)
    own = pack(keys, values)
    from6 = shift(own, 6)
    from3 = shift(own, 3)
    queries, _ = lax.optimization_barrier((queries, own))
    mine = lax.all_gather(queries, "c", tiled=True)
    ready, _, _ = lax.optimization_barrier((mine, from3, from6))
    other = lax.ppermute(ready, "y", [(0, 1), (1, 0)])
    low = small(low_kernel, "low", (8, BLK), jnp.int32, where, segments.reshape(-1, BLK), smem=1)
    trio = small(trio_kernel, "trio", (3 * BLK, 2 * HD), keys.dtype, own, from3, from6)
    one, two = shift(trio, 1), shift(trio, 2)
    common = (where, mine, other, low)
    state = attend("near", (0, 3, 6), True, False, *common, trio)
    state = attend("middle", (1, 4, 7), False, False, *common, one, *state)
    partial = attend("far", (2, 5, 8), False, True, *common, two, *state)
    parts = lax.all_to_all(partial, ("y", "c"), 0, 0, tiled=True)
    copies = small(combine_kernel, "combine", (HEADS, BLK, GROUP * HD), jnp.bfloat16, parts)
    attended = lax.all_to_all(copies, "h", 0, 0, tiled=True)
    return small(project_kernel, "project", (BLK, out_weight.shape[1]), jnp.bfloat16, attended, out_weight)


def solution(mesh):
    planes = mesh.shape["seq"] // LANES
    heads = mesh.shape["head"]
    fine = Mesh(mesh.devices.reshape(planes, LANES // PAIR, PAIR, heads), ("z", "y", "c", "h"))
    tokens = ("z", "y", "c")
    return jax.shard_map(
        on_device,
        mesh=fine,
        in_specs=(P(tokens, "h"), P(tokens, "h"), P(tokens, "h"), P(), P(None, "h")),
        out_specs=P(tokens, "h"),
        check_vma=False,
    )
```

time: 244 us -> 86.3 us (0.35)
  the two profiles are of different devices: /device:TPU:112 before, /device:TPU:384 now
where the time goes in v2:
time: 86.3 us; the launch traced here: 85.9 us
  blocking collectives  35.1 us (41%)
  starting transfers between devices  26.6 us (31%)
  waiting for transfers between devices  11.2 us (13%)
  Pallas kernels  10.2 us (12%)
  local copies, waits for them, and re-layouts  2.51 us (3%)
    ppermute x4, starting transfers between devices, shift(): lax.ppermute(block, 'z', [(i, i + distance) for i in range(planes - dista...  21.5 us
    all_to_all x1, blocking collectives, on_device(): attended = lax.all_to_all(copies, 'h', 0, 0, tiled=True)  19.5 us
    all_to_all x1, blocking collectives, on_device(): parts = lax.all_to_all(partial, ('y', 'c'), 0, 0, tiled=True)  13.4 us
    ppermute x4, waiting for transfers between devices, shift(): lax.ppermute(block, 'z', [(i, i + distance) for i in range(planes - dista...  11.2 us
    pallas_call x3, Pallas kernels, attend(): pl.pallas_call(functools.partial(attend_kernel, distances, first, last),...  7.2 us
    ppermute x1, starting transfers between devices, on_device(): other = lax.ppermute(ready, 'y', [(0, 1), (1, 0)])  5.12 us
    pallas_call x4, Pallas kernels, small(): pl.pallas_call(kernel, out_shape=jax.ShapeDtypeStruct(shape, dtype), in_s...  2.98 us
    unnamed x8, local copies, waits for them, and re-layouts  2.51 us
  transfers between devices with their start and end apart: 5, of which 3 were waited for; matrix products, arithmetic and copies ran while one was open for 0% of the time, Pallas kernels for 6%

profile of v2, /device:TPU:384, one launch (start us, length us, event | category | flops | bytes accessed | tf_op | source)
XLA Modules:
  0.0 85.9 jit_solution(16976167906322788777)
XLA Ops:
  0.0 0.0 copy-start.2
  0.0 0.8 copy-done.2
  0.8 0.0 copy-start.3
  0.8 0.8 copy-done.3
  1.6 10.0 %collective-permute-start.1 = (bf16[128,256]{1,0:T(8,128)(2,1)S(1)}, bf16[128,256]{1,0:T(8,128)(2,1)S(1)}, u32[]{:S(2)}, u32[]{:S(2)}) collective-permute-start(bf16[128,256]{1,0:T(8,128)(2,1)S(1)} %pack.1.own_ref), channel_id=1, source_target_pairs={{0,192},{32,224},{64,256},{96,288},{128,320},{160,352},{192,384},{... | collective-permute-start | bytes 196616 | tf_op jit(solution)/shard_map/ppermute | solution.py:35
  11.6 3.8 %collective-permute-start = (bf16[128,256]{1,0:T(8,128)(2,1)S(1)}, bf16[128,256]{1,0:T(8,128)(2,1)S(1)}, u32[]{:S(2)}, u32[]{:S(2)}) collective-permute-start(bf16[128,256]{1,0:T(8,128)(2,1)S(1)} %pack.1.own_ref), channel_id=1, source_target_pairs={{0,96},{32,128},{64,160},{96,192},{128,224},{160,256},{192,288},{2... | collective-permute-start | bytes 196616 | tf_op jit(solution)/shard_map/ppermute | solution.py:35
  15.4 2.2 %all_gather.3.mine_ref = bf16[256,512]{1,0:T(8,128)(2,1)S(1)} all-gather(bf16[128,512]{1,0:T(8,128)(2,1)} %param.5), channel_id=1, replica_groups=mesh['z'=32,'y'=2,'c'=2,'h'=8] {'c'}, dimensions={0}, use_global_device_ids=true | all-gather | bytes 393216 | tf_op jit(solution)/shard_map/all_gather | solution.py:190
  17.6 3.5 %collective-permute-done.1.from6_ref = bf16[128,256]{1,0:T(8,128)(2,1)S(1)} collective-permute-done((bf16[128,256]{1,0:T(8,128)(2,1)S(1)}, bf16[128,256]{1,0:T(8,128)(2,1)S(1)}, u32[]{:S(2)}, u32[]{:S(2)}) %collective-permute-start.1) | collective-permute-done | bytes 65568 | tf_op jit(solution)/shard_map/ppermute | solution.py:35
  21.1 4.0 %collective-permute-done.from3_ref = bf16[128,256]{1,0:T(8,128)(2,1)S(1)} collective-permute-done((bf16[128,256]{1,0:T(8,128)(2,1)S(1)}, bf16[128,256]{1,0:T(8,128)(2,1)S(1)}, u32[]{:S(2)}, u32[]{:S(2)}) %collective-permute-start) | collective-permute-done | bytes 65568 | tf_op jit(solution)/shard_map/ppermute | solution.py:35
  25.1 5.1 %collective-permute-start.2 = (bf16[256,512]{1,0:T(8,128)(2,1)S(1)}, bf16[256,512]{1,0:T(8,128)(2,1)S(1)}, u32[]{:S(2)}, u32[]{:S(2)}) collective-permute-start(bf16[256,512]{1,0:T(8,128)(2,1)S(1)} %all_gather.3.mine_ref), channel_id=1, source_target_pairs={{0,16},{16,0},{1,17},{17,1},{2,18},{18,2},{3,19},{19,3},{4,20},{20... | collective-permute-start | bytes 786440 | tf_op jit(solution)/shard_map/ppermute | solution.py:192
  30.3 3.4 %collective-permute-start.4 = (bf16[384,256]{1,0:T(8,128)(2,1)S(1)}, bf16[384,256]{1,0:T(8,128)(2,1)S(1)}, u32[]{:S(2)}, u32[]{:S(2)}) collective-permute-start(bf16[384,256]{1,0:T(8,128)(2,1)S(1)} %trio.1.kv_ref), channel_id=1, source_target_pairs={{0,32},{32,64},{64,96},{96,128},{128,160},{160,192},{192,224},{224... | collective-permute-start | bytes 589832 | tf_op jit(solution)/shard_map/ppermute | solution.py:35
  33.7 4.2 %collective-permute-start.3 = (bf16[384,256]{1,0:T(8,128)(2,1)S(1)}, bf16[384,256]{1,0:T(8,128)(2,1)S(1)}, u32[]{:S(2)}, u32[]{:S(2)}) collective-permute-start(bf16[384,256]{1,0:T(8,128)(2,1)S(1)} %trio.1.kv_ref), channel_id=1, source_target_pairs={{0,64},{32,96},{64,128},{96,160},{128,192},{160,224},{192,256},{22... | collective-permute-start | bytes 589832 | tf_op jit(solution)/shard_map/ppermute | solution.py:35
  37.9 0.0 copy-start
  37.9 0.1 pad_add_fusion.where_ref
  38.0 0.0 copy-start.1
  38.0 1.0 %copy-done.1 = s32[16384]{0:T(1024)S(1)} copy-done((s32[16384]{0:T(1024)S(1)}, s32[16384]{0:T(1024)}, u32[]{:S(2)}) %copy-start.1) | copy-done | bytes 65560
  39.0 0.7 low.1.low_ref
  39.7 0.0 collective-permute-done.2.other_ref
  39.7 2.4 %near.1 = (f32[4,128,512]{2,1,0:T(8,128)S(1)}, f32[4,8,512]{2,1,0:T(8,128)S(1)}) custom-call(s32[3]{0:T(128)S(1)} %pad_add_fusion.where_ref, bf16[256,512]{1,0:T(8,128)(2,1)S(1)} %all_gather.3.mine_ref, bf16[256,512]{1,0:T(8,128)(2,1)S(1)} %collective-permute-done.2.other_ref, s32[8,128]{1,0:T(8,128)S(1)} %low.1.low_ref, bf16[384,256]{1,0:T(8,128)(2,1)S(1)} %trio.1.kv_ref), custom_call_target="tpu_custom_call" | custom-call | flops 402653184 | bytes 3145728 | tf_op jit(solution)/shard_map/near/pallas_call | solution.py:118
  42.1 0.0 collective-permute-done.4.kv_ref
  42.2 2.4 %middle.1 = (f32[4,128,512]{2,1,0:T(8,128)S(1)}, f32[4,8,512]{2,1,0:T(8,128)S(1)}) custom-call(s32[3]{0:T(128)S(1)} %pad_add_fusion.where_ref, bf16[256,512]{1,0:T(8,128)(2,1)S(1)} %all_gather.3.mine_ref, bf16[256,512]{1,0:T(8,128)(2,1)S(1)} %collective-permute-done.2.other_ref, s32[8,128]{1,0:T(8,128)S(1)} %low.1.low_ref, ...), custom_call_target="tpu_custom_call" | custom-call | flops 402653184 | bytes 3145728 | tf_op jit(solution)/shard_map/middle/pallas_call | solution.py:118
  44.5 3.7 %collective-permute-done.3.kv_ref = bf16[384,256]{1,0:T(8,128)(2,1)S(1)} collective-permute-done((bf16[384,256]{1,0:T(8,128)(2,1)S(1)}, bf16[384,256]{1,0:T(8,128)(2,1)S(1)}, u32[]{:S(2)}, u32[]{:S(2)}) %collective-permute-start.3) | collective-permute-done | bytes 196640 | tf_op jit(solution)/shard_map/ppermute | solution.py:35
  48.3 2.4 %far.1 = bf16[4,144,512]{2,1,0:T(8,128)(2,1)S(1)} custom-call(s32[3]{0:T(128)S(1)} %pad_add_fusion.where_ref, bf16[256,512]{1,0:T(8,128)(2,1)S(1)} %all_gather.3.mine_ref, bf16[256,512]{1,0:T(8,128)(2,1)S(1)} %collective-permute-done.2.other_ref, s32[8,128]{1,0:T(8,128)S(1)} %low.1.low_ref, bf16[384,256]{1,0:T(8,128)(2,1)S(1)} %collective-permute-done.3.kv_ref, ...), custom_call_target="tpu_custom_call" | custom-call | flops 402653184 | bytes 3145728 | tf_op jit(solution)/shard_map/far/pallas_call | solution.py:118
  50.7 13.4 %all_to_all.10.parts_ref = bf16[4,144,512]{2,1,0:T(8,128)(2,1)S(1)} all-to-all(bf16[4,144,512]{2,1,0:T(8,128)(2,1)S(1)} %far.1), channel_id=1, replica_groups=mesh['z'=32,'y'=2,'c'=2,'h'=8] {'y','c'}, dimensions={0} | all-to-all | bytes 1179648 | tf_op jit(solution)/shard_map/all_to_all | solution.py:200
  64.1 0.3 combine.1
  64.4 19.5 %all_to_all.11.rows_ref = bf16[8,128,512]{2,1,0:T(8,128)(2,1)S(1)} all-to-all(bf16[8,128,512]{2,1,0:T(8,128)(2,1)S(1)} %combine.1), channel_id=1, replica_groups=mesh['z'=32,'y'=2,'c'=2,'h'=8] {'h'}, dimensions={0} | all-to-all | bytes 2097152 | tf_op jit(solution)/shard_map/all_to_all | solution.py:202
  83.9 0.0 copy-done
  83.9 2.0 %project.1 = bf16[128,1024]{1,0:T(8,128)(2,1)} custom-call(bf16[8,128,512]{2,1,0:T(8,128)(2,1)S(1)} %all_to_all.11.rows_ref, bf16[4096,1024]{1,0:T(8,128)(2,1)S(1)} %copy-done), custom_call_target="tpu_custom_call" | custom-call | flops 1048576 | bytes 524288 | tf_op jit(solution)/shard_map/project/pallas_call | solution.py:159
  (2 shorter events, 0.0 us)
Async XLA Ops:
  0.0 0.8 copy-start.2
  0.8 0.8 copy-start.3
  1.6 19.5 %collective-permute-start.1 = (bf16[128,256]{1,0:T(8,128)(2,1)S(1)}, bf16[128,256]{1,0:T(8,128)(2,1)S(1)}, u32[]{:S(2)}, u32[]{:S(2)}) collective-permute-start(bf16[128,256]{1,0:T(8,128)(2,1)S(1)} %pack.1.own_ref), channel_id=1, source_target_pairs={{0,192},{32,224},{64,256},{96,288},{128,320},{160,352},{192,384},{... | collective-permute-start | bytes 196616 | tf_op jit(solution)/shard_map/ppermute | solution.py:35
  11.6 13.6 %collective-permute-start = (bf16[128,256]{1,0:T(8,128)(2,1)S(1)}, bf16[128,256]{1,0:T(8,128)(2,1)S(1)}, u32[]{:S(2)}, u32[]{:S(2)}) collective-permute-start(bf16[128,256]{1,0:T(8,128)(2,1)S(1)} %pack.1.own_ref), channel_id=1, source_target_pairs={{0,96},{32,128},{64,160},{96,192},{128,224},{160,256},{192,288},{2... | collective-permute-start | bytes 196616 | tf_op jit(solution)/shard_map/ppermute | solution.py:35
  25.1 14.6 %collective-permute-start.2 = (bf16[256,512]{1,0:T(8,128)(2,1)S(1)}, bf16[256,512]{1,0:T(8,128)(2,1)S(1)}, u32[]{:S(2)}, u32[]{:S(2)}) collective-permute-start(bf16[256,512]{1,0:T(8,128)(2,1)S(1)} %all_gather.3.mine_ref), channel_id=1, source_target_pairs={{0,16},{16,0},{1,17},{17,1},{2,18},{18,2},{3,19},{19,3},{4,20},{20... | collective-permute-start | bytes 786440 | tf_op jit(solution)/shard_map/ppermute | solution.py:192
  30.3 11.9 %collective-permute-start.4 = (bf16[384,256]{1,0:T(8,128)(2,1)S(1)}, bf16[384,256]{1,0:T(8,128)(2,1)S(1)}, u32[]{:S(2)}, u32[]{:S(2)}) collective-permute-start(bf16[384,256]{1,0:T(8,128)(2,1)S(1)} %trio.1.kv_ref), channel_id=1, source_target_pairs={{0,32},{32,64},{64,96},{96,128},{128,160},{160,192},{192,224},{224... | collective-permute-start | bytes 589832 | tf_op jit(solution)/shard_map/ppermute | solution.py:35
  33.7 14.6 %collective-permute-start.3 = (bf16[384,256]{1,0:T(8,128)(2,1)S(1)}, bf16[384,256]{1,0:T(8,128)(2,1)S(1)}, u32[]{:S(2)}, u32[]{:S(2)}) collective-permute-start(bf16[384,256]{1,0:T(8,128)(2,1)S(1)} %trio.1.kv_ref), channel_id=1, source_target_pairs={{0,64},{32,96},{64,128},{96,160},{128,192},{160,224},{192,256},{22... | collective-permute-start | bytes 589832 | tf_op jit(solution)/shard_map/ppermute | solution.py:35
  37.9 46.0 %copy-start = (bf16[4096,1024]{1,0:T(8,128)(2,1)S(1)}, bf16[4096,1024]{1,0:T(8,128)(2,1)}, u32[]{:S(2)}) copy-start(bf16[4096,1024]{1,0:T(8,128)(2,1)} %weight_ref.1) | copy-start | bytes 25165828
  38.0 1.0 %copy-start.1 = (s32[16384]{0:T(1024)S(1)}, s32[16384]{0:T(1024)}, u32[]{:S(2)}) copy-start(s32[16384]{0:T(1024)} %param.8) | copy-start | bytes 196612

commit v3 on v2

--- a/solution.py
+++ b/solution.py
@@ -30,9 +30,12 @@
 )
 
 
-def shift(block, distance):
-    planes = lax.axis_size("z")
-    return lax.ppermute(block, "z", [(i, i + distance) for i in range(planes - distance)])
+def shift_by_core(block, distances):
+    planes, cores = lax.axis_size("z"), lax.axis_size("c")
+    route = [
+        (z * cores + c, (z + distances[c]) * cores + c) for c in range(cores) for z in range(planes - distances[c])
+    ]
+    return lax.ppermute(block, ("z", "c"), route)
 
 
 def pack_kernel(key_ref, value_ref, out_ref, sems):
@@ -44,9 +47,10 @@
     value_copy.wait()
 
 
-def trio_kernel(own_ref, from3_ref, from6_ref, out_ref):
-    for n, ref in enumerate((own_ref, from3_ref, from6_ref)):
-        out_ref[n * BLK : (n + 1) * BLK] = ref[...]
+def join_kernel(own_ref, come_ref, out_ref):
+    rows = own_ref.shape[0]
+    out_ref[:rows] = own_ref[...]
+    out_ref[rows:] = come_ref[...]
 
 
 def low_kernel(where_ref, segment_ref, out_ref):
@@ -54,20 +58,30 @@
     before = [jnp.sum((segments < v).astype(jnp.int32)) for v in range(1, SEGMENT_VALUES)]
     token = lax.broadcasted_iota(jnp.int32, (1, BLK), 1)
     for p in range(LANES):
-        own = segment_ref[pl.ds(where_ref[1] * LANES + p, 1), :]
+        own = segment_ref[pl.ds(where_ref[0] * LANES + p, 1), :]
         start = jnp.zeros((1, BLK), jnp.int32)
         for v in range(1, SEGMENT_VALUES):
             start = jnp.where(own == v, before[v - 1], start)
-        position = where_ref[1] * PLANE + p * BLK + token
+        position = where_ref[0] * PLANE + p * BLK + token
         out_ref[p : p + 1] = jnp.maximum(start, position - (WINDOW - 1))
     out_ref[LANES:] = jnp.zeros((8 - LANES, BLK), jnp.int32)
 
 
-def attend_kernel(distances, first, last, where_ref, mine_ref, other_ref, low_ref, kv_ref, *refs):
-    old, refs = ((), refs) if first else (refs[:2], refs[2:])
-    own_key, plane_first, side = where_ref[0], where_ref[1] * PLANE, where_ref[2]
-    keys = kv_ref[:, :HD]
-    values_t = kv_ref[:, HD:].astype(jnp.float32).T.astype(jnp.bfloat16)
+def attend_kernel(near, where_ref, mine_ref, other_ref, low_ref, kv_ref, *refs):
+    old, refs = ((), refs) if near else (refs[:2], refs[2:])
+    plane, side, own_core = where_ref[0], where_ref[1], where_ref[2]
+    plane_first = plane * PLANE
+    side_first = plane_first + side * (PAIR * BLK)
+    if near:
+        firsts = [side_first + own_core * BLK - d * PLANE for d in (0, 3, 6)]
+        held = jnp.concatenate(
+            [kv_ref[pl.ds(pl.multiple_of((n * PAIR + own_core) * BLK, BLK), BLK), :] for n in range(3)], axis=0
+        )
+    else:
+        firsts = [side_first + lane * BLK - (d + own_core) * PLANE for d in (1, 4, 7) for lane in range(PAIR)]
+        held = kv_ref[...]
+    keys = held[:, :HD]
+    values_t = held[:, HD:].astype(jnp.float32).T.astype(jnp.bfloat16)
     sub = lax.broadcasted_iota(jnp.int32, (BLK, ROWS), 0)
     for index in range(LANES):
         query_ref, core = (mine_ref, other_ref)[index // PAIR], index % PAIR
@@ -77,26 +91,25 @@
         scores = lax.dot_general(keys, queries, (((1,), (1,)), ((), ())), preferred_element_type=jnp.float32)
         low = jnp.concatenate([low_ref[pl.ds(block, 1), :]] * GROUP, axis=1)
         parts = []
-        for n, distance in enumerate(distances):
-            key_first = own_key - distance * PLANE
+        for n, key_first in enumerate(firsts):
             allowed = sub >= low - key_first
-            if distance == 0:
+            if near and n == 0:
                 token = lax.broadcasted_iota(jnp.int32, (1, ROWS), 1) % BLK
                 allowed = allowed & (sub <= plane_first + block * BLK + token - key_first)
             parts.append(jnp.where(allowed, scores[n * BLK : (n + 1) * BLK] * SCALE2, MASKED))
         top = jnp.max(functools.reduce(jnp.maximum, parts), axis=0, keepdims=True)
-        if not first:
+        if not near:
             old_top = old[1][index, 0:1]
             top = jnp.maximum(top, old_top)
         weights = [jnp.exp2(piece - top) for piece in parts]
         total = jnp.sum(functools.reduce(jnp.add, weights), axis=0, keepdims=True)
         weights = jnp.concatenate([w.astype(jnp.bfloat16) for w in weights], axis=0)
         acc = jnp.dot(values_t, weights, preferred_element_type=jnp.float32)
-        if not first:
+        if not near:
             factor = jnp.exp2(old_top - top)
             total = total + old[1][index, 1:2] * factor
             acc = acc + old[0][index] * factor
-        if not last:
+        if near:
             refs[0][index] = acc
             refs[1][index, 0:1] = top
             refs[1][index, 1:2] = total
@@ -112,14 +125,14 @@
         refs[0][block, HD:] = pieces.astype(jnp.bfloat16)
 
 
-def attend(name, distances, first, last, *args):
-    out = jax.ShapeDtypeStruct((LANES, HD + PIECES, ROWS), jnp.bfloat16) if last else STATE
-    pairs = LANES * ROWS * len(distances) * BLK
+def attend(name, near, *args):
+    out = STATE if near else jax.ShapeDtypeStruct((LANES, HD + PIECES, ROWS), jnp.bfloat16)
+    pairs = LANES * ROWS * (3 if near else 6) * BLK
     return pl.pallas_call(
-        functools.partial(attend_kernel, distances, first, last),
+        functools.partial(attend_kernel, near),
         out_shape=out,
         in_specs=[SMEM] + [VREF] * (len(args) - 1),
-        out_specs=VREF if last else (VREF, VREF),
+        out_specs=(VREF, VREF) if near else VREF,
         compiler_params=PARAMS,
         cost_estimate=pl.CostEstimate(flops=4 * pairs * HD, bytes_accessed=3 << 20, transcendentals=pairs),
         name=name,
@@ -182,21 +195,18 @@
 
 def on_device(queries, keys, values, segments, out_weight):
     plane, side, core = lax.axis_index("z"), lax.axis_index("y"), lax.axis_index("c")
-    where = jnp.stack([plane * PLANE + (side * PAIR + core) * BLK, plane, side]).astype(jnp.int32)
-    own = pack(keys, values)
-    from6 = shift(own, 6)
-    from3 = shift(own, 3)
+    where = jnp.stack([plane, side, core]).astype(jnp.int32)
+    own = lax.all_gather(pack(keys, values), "c", tiled=True)
+    low = small(low_kernel, "low", (8, BLK), jnp.int32, where, segments.reshape(-1, BLK), smem=1)
+    come, low = lax.optimization_barrier((shift_by_core(own, (3, 6)), low))
+    come = lax.all_gather(come, "c", tiled=True)
     queries, _ = lax.optimization_barrier((queries, own))
     mine = lax.all_gather(queries, "c", tiled=True)
-    ready, _, _ = lax.optimization_barrier((mine, from3, from6))
-    other = lax.ppermute(ready, "y", [(0, 1), (1, 0)])
-    low = small(low_kernel, "low", (8, BLK), jnp.int32, where, segments.reshape(-1, BLK), smem=1)
-    trio = small(trio_kernel, "trio", (3 * BLK, 2 * HD), keys.dtype, own, from3, from6)
-    one, two = shift(trio, 1), shift(trio, 2)
-    common = (where, mine, other, low)
-    state = attend("near", (0, 3, 6), True, False, *common, trio)
-    state = attend("middle", (1, 4, 7), False, False, *common, one, *state)
-    partial = attend("far", (2, 5, 8), False, True, *common, two, *state)
+    held = small(join_kernel, "join", (6 * BLK, 2 * HD), keys.dtype, own, come)
+    far = shift_by_core(held, (1, 2))
+    other = lax.ppermute(mine, "y", [(0, 1), (1, 0)])
+    state = attend("near", True, where, mine, other, low, held)
+    partial = attend("far", False, where, mine, other, low, far, *state)
     parts = lax.all_to_all(partial, ("y", "c"), 0, 0, tiled=True)
     copies = small(combine_kernel, "combine", (HEADS, BLK, GROUP * HD), jnp.bfloat16, parts)
     attended = lax.all_to_all(copies, "h", 0, 0, tiled=True)

time: 86.3 us -> 89.4 us (1.036)
  the two profiles are of different devices: /device:TPU:384 before, /device:TPU:352 now
where the time goes in v3:
time: 89.4 us; the launch traced here: 89 us
  blocking collectives  44.4 us (50%)
  waiting for transfers between devices  17.8 us (20%)
  starting transfers between devices  15.2 us (17%)
  Pallas kernels  8.94 us (10%)
  local copies, waits for them, and re-layouts  2.51 us (3%)
    all_to_all x1, blocking collectives, on_device(): attended = lax.all_to_all(copies, 'h', 0, 0, tiled=True)  19.5 us
    all_to_all x1, blocking collectives, on_device(): parts = lax.all_to_all(partial, ('y', 'c'), 0, 0, tiled=True)  15.2 us
    ppermute x2, waiting for transfers between devices, shift_by_core(): return lax.ppermute(block, ('z', 'c'), route)  10.8 us
    ppermute x2, starting transfers between devices, shift_by_core(): return lax.ppermute(block, ('z', 'c'), route)  10.2 us
    ppermute x1, waiting for transfers between devices, on_device(): other = lax.ppermute(mine, 'y', [(0, 1), (1, 0)])  6.98 us
    pallas_call x2, Pallas kernels, attend(): pl.pallas_call(functools.partial(attend_kernel, near), out_shape=out, in_...  5.91 us
    all_gather x1, blocking collectives, on_device(): mine = lax.all_gather(queries, 'c', tiled=True)  5.53 us
    ppermute x1, starting transfers between devices, on_device(): other = lax.ppermute(mine, 'y', [(0, 1), (1, 0)])  4.98 us
  transfers between devices with their start and end apart: 3, of which 2 were waited for; matrix products, arithmetic and copies ran while one was open for 0% of the time, Pallas kernels for 4%

profile of v3, /device:TPU:352, one launch (start us, length us, event | category | flops | bytes accessed | tf_op | source)
XLA Modules:
  0.0 89.0 jit_solution(14456966765048052173)
XLA Ops:
  0.0 0.0 copy-start.2
  0.0 0.8 copy-done.2
  0.8 0.0 copy-start.3
  0.8 0.8 copy-done.3
  1.6 1.9 %all_gather.9.own_ref = bf16[256,256]{1,0:T(8,128)(2,1)S(1)} all-gather(bf16[128,256]{1,0:T(8,128)(2,1)S(1)} %pack.1), channel_id=1, replica_groups=mesh['z'=32,'y'=2,'c'=2,'h'=8] {'c'}, dimensions={0}, use_global_device_ids=true | all-gather | bytes 196608 | tf_op jit(solution)/shard_map/all_gather | solution.py:199
  3.5 7.7 %collective-permute-start.1 = (bf16[256,256]{1,0:T(8,128)(2,1)S(1)}, bf16[256,256]{1,0:T(8,128)(2,1)S(1)}, u32[]{:S(2)}, u32[]{:S(2)}) collective-permute-start(bf16[256,256]{1,0:T(8,128)(2,1)S(1)} %all_gather.9.own_ref), channel_id=1, source_target_pairs={{0,96},{32,128},{64,160},{96,192},{128,224},{160,256},{192,288},{2... | collective-permute-start | bytes 393224 | tf_op jit(solution)/shard_map/ppermute | solution.py:38
  11.2 0.0 copy-start
  11.2 0.1 pad_add_fusion.where_ref
  11.3 0.0 copy-start.1
  11.3 1.0 %copy-done.1 = s32[16384]{0:T(1024)S(1)} copy-done((s32[16384]{0:T(1024)S(1)}, s32[16384]{0:T(1024)}, u32[]{:S(2)}) %copy-start.1) | copy-done | bytes 65560
  12.3 0.7 low.1.low_ref
  13.0 10.8 %collective-permute-done.1 = bf16[256,256]{1,0:T(8,128)(2,1)S(1)} collective-permute-done((bf16[256,256]{1,0:T(8,128)(2,1)S(1)}, bf16[256,256]{1,0:T(8,128)(2,1)S(1)}, u32[]{:S(2)}, u32[]{:S(2)}) %collective-permute-start.1) | collective-permute-done | bytes 131104 | tf_op jit(solution)/shard_map/ppermute | solution.py:38
  23.8 2.3 %all_gather.11.come_ref = bf16[512,256]{1,0:T(8,128)(2,1)S(1)} all-gather(bf16[256,256]{1,0:T(8,128)(2,1)S(1)} %collective-permute-done.1), channel_id=1, replica_groups=mesh['z'=32,'y'=2,'c'=2,'h'=8] {'c'}, dimensions={0}, use_global_device_ids=true | all-gather | bytes 393216 | tf_op jit(solution)/shard_map/all_gather | solution.py:202
  26.2 2.5 %collective-permute-start.2 = (bf16[768,256]{1,0:T(8,128)(2,1)S(1)}, bf16[768,256]{1,0:T(8,128)(2,1)S(1)}, u32[]{:S(2)}, u32[]{:S(2)}) collective-permute-start(bf16[768,256]{1,0:T(8,128)(2,1)S(1)} %join.1.kv_ref), channel_id=1, source_target_pairs={{0,32},{32,64},{64,96},{96,128},{128,160},{160,192},{192,224},{224... | collective-permute-start | bytes 1179656 | tf_op jit(solution)/shard_map/ppermute | solution.py:38
  28.6 5.5 %all_gather.10.mine_ref = bf16[256,512]{1,0:T(8,128)(2,1)S(1)} all-gather(bf16[128,512]{1,0:T(8,128)(2,1)} %param.5), channel_id=1, replica_groups=mesh['z'=32,'y'=2,'c'=2,'h'=8] {'c'}, dimensions={0}, use_global_device_ids=true | all-gather | bytes 393216 | tf_op jit(solution)/shard_map/all_gather | solution.py:204
  34.2 5.0 %collective-permute-start = (bf16[256,512]{1,0:T(8,128)(2,1)S(1)}, bf16[256,512]{1,0:T(8,128)(2,1)S(1)}, u32[]{:S(2)}, u32[]{:S(2)}) collective-permute-start(bf16[256,512]{1,0:T(8,128)(2,1)S(1)} %all_gather.10.mine_ref), channel_id=1, source_target_pairs={{0,16},{16,0},{1,17},{17,1},{2,18},{18,2},{3,19},{19,3},{4,20},{20... | collective-permute-start | bytes 786440 | tf_op jit(solution)/shard_map/ppermute | solution.py:207
  39.2 7.0 %collective-permute-done.other_ref = bf16[256,512]{1,0:T(8,128)(2,1)S(1)} collective-permute-done((bf16[256,512]{1,0:T(8,128)(2,1)S(1)}, bf16[256,512]{1,0:T(8,128)(2,1)S(1)}, u32[]{:S(2)}, u32[]{:S(2)}) %collective-permute-start) | collective-permute-done | bytes 262176 | tf_op jit(solution)/shard_map/ppermute | solution.py:207
  46.1 2.4 %near.1 = (f32[4,128,512]{2,1,0:T(8,128)S(1)}, f32[4,8,512]{2,1,0:T(8,128)S(1)}) custom-call(s32[3]{0:T(128)S(1)} %pad_add_fusion.where_ref, bf16[256,512]{1,0:T(8,128)(2,1)S(1)} %all_gather.10.mine_ref, bf16[256,512]{1,0:T(8,128)(2,1)S(1)} %collective-permute-done.other_ref, s32[8,128]{1,0:T(8,128)S(1)} %low.1.low_ref, bf16[768,256]{1,0:T(8,128)(2,1)S(1)} %join.1.kv_ref), custom_call_target="tpu_custom_call" | custom-call | flops 402653184 | bytes 3145728 | tf_op jit(solution)/shard_map/near/pallas_call | solution.py:131
  48.5 0.0 collective-permute-done.2.kv_ref
  48.6 3.5 %far.1 = bf16[4,144,512]{2,1,0:T(8,128)(2,1)S(1)} custom-call(s32[3]{0:T(128)S(1)} %pad_add_fusion.where_ref, bf16[256,512]{1,0:T(8,128)(2,1)S(1)} %all_gather.10.mine_ref, bf16[256,512]{1,0:T(8,128)(2,1)S(1)} %collective-permute-done.other_ref, s32[8,128]{1,0:T(8,128)S(1)} %low.1.low_ref, bf16[768,256]{1,0:T(8,128)(2,1)S(1)} %collective-permute-done.2.kv_ref, ...), custom_call_target="tpu_custom_call" | custom-call | flops 805306368 | bytes 3145728 | tf_op jit(solution)/shard_map/far/pallas_call | solution.py:131
  52.1 15.2 %all_to_all.10.parts_ref = bf16[4,144,512]{2,1,0:T(8,128)(2,1)S(1)} all-to-all(bf16[4,144,512]{2,1,0:T(8,128)(2,1)S(1)} %far.1), channel_id=1, replica_groups=mesh['z'=32,'y'=2,'c'=2,'h'=8] {'y','c'}, dimensions={0} | all-to-all | bytes 1179648 | tf_op jit(solution)/shard_map/all_to_all | solution.py:210
  67.2 0.3 combine.1
  67.5 19.5 %all_to_all.11.rows_ref = bf16[8,128,512]{2,1,0:T(8,128)(2,1)S(1)} all-to-all(bf16[8,128,512]{2,1,0:T(8,128)(2,1)S(1)} %combine.1), channel_id=1, replica_groups=mesh['z'=32,'y'=2,'c'=2,'h'=8] {'h'}, dimensions={0} | all-to-all | bytes 2097152 | tf_op jit(solution)/shard_map/all_to_all | solution.py:212
  87.0 0.0 copy-done
  87.0 2.0 %project.1 = bf16[128,1024]{1,0:T(8,128)(2,1)} custom-call(bf16[8,128,512]{2,1,0:T(8,128)(2,1)S(1)} %all_to_all.11.rows_ref, bf16[4096,1024]{1,0:T(8,128)(2,1)S(1)} %copy-done), custom_call_target="tpu_custom_call" | custom-call | flops 1048576 | bytes 524288 | tf_op jit(solution)/shard_map/project/pallas_call | solution.py:172
  (2 shorter events, 0.1 us)
Async XLA Ops:
  0.0 0.8 copy-start.2
  0.8 0.8 copy-start.3
  3.5 20.4 %collective-permute-start.1 = (bf16[256,256]{1,0:T(8,128)(2,1)S(1)}, bf16[256,256]{1,0:T(8,128)(2,1)S(1)}, u32[]{:S(2)}, u32[]{:S(2)}) collective-permute-start(bf16[256,256]{1,0:T(8,128)(2,1)S(1)} %all_gather.9.own_ref), channel_id=1, source_target_pairs={{0,96},{32,128},{64,160},{96,192},{128,224},{160,256},{192,288},{2... | collective-permute-start | bytes 393224 | tf_op jit(solution)/shard_map/ppermute | solution.py:38
  11.2 75.8 %copy-start = (bf16[4096,1024]{1,0:T(8,128)(2,1)S(1)}, bf16[4096,1024]{1,0:T(8,128)(2,1)}, u32[]{:S(2)}) copy-start(bf16[4096,1024]{1,0:T(8,128)(2,1)} %weight_ref.1) | copy-start | bytes 25165828
  11.3 1.0 %copy-start.1 = (s32[16384]{0:T(1024)S(1)}, s32[16384]{0:T(1024)}, u32[]{:S(2)}) copy-start(s32[16384]{0:T(1024)} %param.8) | copy-start | bytes 196612
  26.2 22.4 %collective-permute-start.2 = (bf16[768,256]{1,0:T(8,128)(2,1)S(1)}, bf16[768,256]{1,0:T(8,128)(2,1)S(1)}, u32[]{:S(2)}, u32[]{:S(2)}) collective-permute-start(bf16[768,256]{1,0:T(8,128)(2,1)S(1)} %join.1.kv_ref), channel_id=1, source_target_pairs={{0,32},{32,64},{64,96},{96,128},{128,160},{160,192},{192,224},{224... | collective-permute-start | bytes 1179656 | tf_op jit(solution)/shard_map/ppermute | solution.py:38
  34.2 12.0 %collective-permute-start = (bf16[256,512]{1,0:T(8,128)(2,1)S(1)}, bf16[256,512]{1,0:T(8,128)(2,1)S(1)}, u32[]{:S(2)}, u32[]{:S(2)}) collective-permute-start(bf16[256,512]{1,0:T(8,128)(2,1)S(1)} %all_gather.10.mine_ref), channel_id=1, source_target_pairs={{0,16},{16,0},{1,17},{17,1},{2,18},{18,2},{3,19},{19,3},{4,20},{20... | collective-permute-start | bytes 786440 | tf_op jit(solution)/shard_map/ppermute | solution.py:207

commit v4 on v2

--- a/solution.py
+++ b/solution.py
@@ -10,7 +10,6 @@
 HD = 128
 BLK = 128
 GROUP = 4
-PAIR = 2
 LANES = 4
 WINDOW = 31 * BLK
 PLANE = LANES * BLK
@@ -20,6 +19,7 @@
 SEGMENT_VALUES = 6
 SCALE2 = float(HD**-0.5 * 1.4426950408889634)
 MASKED = -1e30
+UNROLL = LANES
 VMEM = 24 * 1024 * 1024
 PARAMS = pltpu.CompilerParams(vmem_limit_bytes=VMEM)
 SMEM = pl.BlockSpec(memory_space=pltpu.SMEM)
@@ -54,39 +54,39 @@
     before = [jnp.sum((segments < v).astype(jnp.int32)) for v in range(1, SEGMENT_VALUES)]
     token = lax.broadcasted_iota(jnp.int32, (1, BLK), 1)
     for p in range(LANES):
-        own = segment_ref[pl.ds(where_ref[1] * LANES + p, 1), :]
+        own = segment_ref[pl.ds(where_ref[0] * LANES + p, 1), :]
         start = jnp.zeros((1, BLK), jnp.int32)
         for v in range(1, SEGMENT_VALUES):
             start = jnp.where(own == v, before[v - 1], start)
-        position = where_ref[1] * PLANE + p * BLK + token
+        position = where_ref[0] * PLANE + p * BLK + token
         out_ref[p : p + 1] = jnp.maximum(start, position - (WINDOW - 1))
     out_ref[LANES:] = jnp.zeros((8 - LANES, BLK), jnp.int32)
 
 
-def attend_kernel(distances, first, last, where_ref, mine_ref, other_ref, low_ref, kv_ref, *refs):
+def attend_kernel(distances, first, last, where_ref, query_ref, low_ref, kv_ref, *refs):
     old, refs = ((), refs) if first else (refs[:2], refs[2:])
-    own_key, plane_first, side = where_ref[0], where_ref[1] * PLANE, where_ref[2]
+    plane_first = where_ref[0] * PLANE
+    own_first = plane_first + where_ref[1] * BLK
     keys = kv_ref[:, :HD]
     values_t = kv_ref[:, HD:].astype(jnp.float32).T.astype(jnp.bfloat16)
     sub = lax.broadcasted_iota(jnp.int32, (BLK, ROWS), 0)
-    for index in range(LANES):
-        query_ref, core = (mine_ref, other_ref)[index // PAIR], index % PAIR
-        block = core + PAIR * (side if index < PAIR else 1 - side)
-        rows = slice(core * BLK, (core + 1) * BLK)
+    token = lax.broadcasted_iota(jnp.int32, (1, ROWS), 1) % BLK
+
+    def one_block(block, carry):
+        rows = pl.ds(pl.multiple_of(block * BLK, BLK), BLK)
         queries = jnp.concatenate([query_ref[rows, g * HD : (g + 1) * HD] for g in range(GROUP)], axis=0)
         scores = lax.dot_general(keys, queries, (((1,), (1,)), ((), ())), preferred_element_type=jnp.float32)
         low = jnp.concatenate([low_ref[pl.ds(block, 1), :]] * GROUP, axis=1)
         parts = []
         for n, distance in enumerate(distances):
-            key_first = own_key - distance * PLANE
+            key_first = own_first - distance * PLANE
             allowed = sub >= low - key_first
             if distance == 0:
-                token = lax.broadcasted_iota(jnp.int32, (1, ROWS), 1) % BLK
                 allowed = allowed & (sub <= plane_first + block * BLK + token - key_first)
             parts.append(jnp.where(allowed, scores[n * BLK : (n + 1) * BLK] * SCALE2, MASKED))
         top = jnp.max(functools.reduce(jnp.maximum, parts), axis=0, keepdims=True)
         if not first:
-            old_top = old[1][index, 0:1]
+            old_top = old[1][block, 0:1]
             top = jnp.maximum(top, old_top)
         weights = [jnp.exp2(piece - top) for piece in parts]
         total = jnp.sum(functools.reduce(jnp.add, weights), axis=0, keepdims=True)
@@ -94,22 +94,24 @@
         acc = jnp.dot(values_t, weights, preferred_element_type=jnp.float32)
         if not first:
             factor = jnp.exp2(old_top - top)
-            total = total + old[1][index, 1:2] * factor
-            acc = acc + old[0][index] * factor
+            total = total + old[1][block, 1:2] * factor
+            acc = acc + old[0][block] * factor
         if not last:
-            refs[0][index] = acc
-            refs[1][index, 0:1] = top
-            refs[1][index, 1:2] = total
-            continue
-        refs[0][block, :HD] = (acc / total).astype(jnp.bfloat16)
+            refs[0][block] = acc
+            refs[1][block, 0:1] = top
+            refs[1][block, 1:2] = total
+            return carry
+        refs[0][block, :HD] = (acc * (1.0 / total)).astype(jnp.bfloat16)
         spread = top + jnp.log2(total)
-        high = spread.astype(jnp.bfloat16)
-        rest = spread - high.astype(jnp.float32)
-        middle = rest.astype(jnp.bfloat16)
-        rest = rest - middle.astype(jnp.float32)
+        high = spread.astype(jnp.bfloat16).astype(jnp.float32)
+        rest = spread - high
+        middle = rest.astype(jnp.bfloat16).astype(jnp.float32)
         row = lax.broadcasted_iota(jnp.int32, (PIECES, ROWS), 0)
-        pieces = jnp.where(row == 0, high.astype(jnp.float32), jnp.where(row == 1, middle.astype(jnp.float32), jnp.where(row == 2, rest, 0.0)))
+        pieces = jnp.where(row == 0, high, jnp.where(row == 1, middle, jnp.where(row == 2, rest - middle, 0.0)))
         refs[0][block, HD:] = pieces.astype(jnp.bfloat16)
+        return carry
+
+    lax.fori_loop(0, LANES, one_block, 0, unroll=UNROLL)
 
 
 def attend(name, distances, first, last, *args):
@@ -181,23 +183,21 @@
 
 
 def on_device(queries, keys, values, segments, out_weight):
-    plane, side, core = lax.axis_index("z"), lax.axis_index("y"), lax.axis_index("c")
-    where = jnp.stack([plane * PLANE + (side * PAIR + core) * BLK, plane, side]).astype(jnp.int32)
+    plane, lane = lax.axis_index("z"), lax.axis_index("p")
+    where = jnp.stack([plane, lane]).astype(jnp.int32)
+    low = small(low_kernel, "low", (8, BLK), jnp.int32, where, segments.reshape(-1, BLK), smem=1)
     own = pack(keys, values)
-    from6 = shift(own, 6)
-    from3 = shift(own, 3)
     queries, _ = lax.optimization_barrier((queries, own))
-    mine = lax.all_gather(queries, "c", tiled=True)
-    ready, _, _ = lax.optimization_barrier((mine, from3, from6))
-    other = lax.ppermute(ready, "y", [(0, 1), (1, 0)])
-    low = small(low_kernel, "low", (8, BLK), jnp.int32, where, segments.reshape(-1, BLK), smem=1)
+    plane_queries = lax.all_gather(queries, "p", tiled=True)
+    from3, low = lax.optimization_barrier((shift(own, 3), low))
+    from6, plane_queries = lax.optimization_barrier((shift(from3, 3), plane_queries))
     trio = small(trio_kernel, "trio", (3 * BLK, 2 * HD), keys.dtype, own, from3, from6)
     one, two = shift(trio, 1), shift(trio, 2)
-    common = (where, mine, other, low)
+    common = (where, plane_queries, low)
     state = attend("near", (0, 3, 6), True, False, *common, trio)
     state = attend("middle", (1, 4, 7), False, False, *common, one, *state)
     partial = attend("far", (2, 5, 8), False, True, *common, two, *state)
-    parts = lax.all_to_all(partial, ("y", "c"), 0, 0, tiled=True)
+    parts = lax.all_to_all(partial, "p", 0, 0, tiled=True)
     copies = small(combine_kernel, "combine", (HEADS, BLK, GROUP * HD), jnp.bfloat16, parts)
     attended = lax.all_to_all(copies, "h", 0, 0, tiled=True)
     return small(project_kernel, "project", (BLK, out_weight.shape[1]), jnp.bfloat16, attended, out_weight)
@@ -205,9 +205,8 @@
 
 def solution(mesh):
     planes = mesh.shape["seq"] // LANES
-    heads = mesh.shape["head"]
-    fine = Mesh(mesh.devices.reshape(planes, LANES // PAIR, PAIR, heads), ("z", "y", "c", "h"))
-    tokens = ("z", "y", "c")
+    fine = Mesh(mesh.devices.reshape(planes, LANES, mesh.shape["head"]), ("z", "p", "h"))
+    tokens = ("z", "p")
     return jax.shard_map(
         on_device,
         mesh=fine,

time: 86.3 us -> 87.1 us (level)
  the two profiles are of different devices: /device:TPU:384 before, /device:TPU:256 now
where the time goes in v4:
time: 87.1 us; the launch traced here: 86.7 us
  blocking collectives  43 us (49%)
  starting transfers between devices  23.6 us (27%)
  Pallas kernels  10.2 us (12%)
  waiting for transfers between devices  7.23 us (8%)
  local copies, waits for them, and re-layouts  2.51 us (3%)
    ppermute x4, starting transfers between devices, shift(): lax.ppermute(block, 'z', [(i, i + distance) for i in range(planes - dista...  23.6 us
    all_to_all x1, blocking collectives, on_device(): attended = lax.all_to_all(copies, 'h', 0, 0, tiled=True)  19.5 us
    all_to_all x1, blocking collectives, on_device(): parts = lax.all_to_all(partial, 'p', 0, 0, tiled=True)  14.4 us
    all_gather x1, blocking collectives, on_device(): plane_queries = lax.all_gather(queries, 'p', tiled=True)  9.06 us
    ppermute x4, waiting for transfers between devices, shift(): lax.ppermute(block, 'z', [(i, i + distance) for i in range(planes - dista...  7.23 us
    pallas_call x3, Pallas kernels, attend(): pl.pallas_call(functools.partial(attend_kernel, distances, first, last),...  7.2 us
    pallas_call x4, Pallas kernels, small(): pl.pallas_call(kernel, out_shape=jax.ShapeDtypeStruct(shape, dtype), in_s...  2.98 us
    unnamed x8, local copies, waits for them, and re-layouts  2.51 us
  transfers between devices with their start and end apart: 4, of which 2 were waited for; matrix products, arithmetic and copies ran while one was open for 0% of the time, Pallas kernels for 6%

profile of v4, /device:TPU:256, one launch (start us, length us, event | category | flops | bytes accessed | tf_op | source)
XLA Modules:
  0.0 86.7 jit_solution(17437510473719787639)
XLA Ops:
  0.0 0.0 copy-start.2
  0.0 0.8 copy-done.2
  0.8 0.0 copy-start.3
  0.8 0.8 copy-done.3
  1.6 6.5 %collective-permute-start = (bf16[128,256]{1,0:T(8,128)(2,1)S(1)}, bf16[128,256]{1,0:T(8,128)(2,1)S(1)}, u32[]{:S(2)}, u32[]{:S(2)}) collective-permute-start(bf16[128,256]{1,0:T(8,128)(2,1)S(1)} %pack.1.own_ref), channel_id=1, source_target_pairs={{0,96},{32,128},{64,160},{96,192},{128,224},{160,256},{192,288},{2... | collective-permute-start | bytes 196616 | tf_op jit(solution)/shard_map/ppermute | solution.py:35
  8.1 0.0 copy-start
  8.1 0.1 pad_add_fusion.where_ref
  8.2 0.0 copy-start.1
  8.2 1.0 %copy-done.1 = s32[16384]{0:T(1024)S(1)} copy-done((s32[16384]{0:T(1024)S(1)}, s32[16384]{0:T(1024)}, u32[]{:S(2)}) %copy-start.1) | copy-done | bytes 65560
  9.2 0.7 low.1.low_ref
  9.9 2.2 %collective-permute-done.from3_ref = bf16[128,256]{1,0:T(8,128)(2,1)S(1)} collective-permute-done((bf16[128,256]{1,0:T(8,128)(2,1)S(1)}, bf16[128,256]{1,0:T(8,128)(2,1)S(1)}, u32[]{:S(2)}, u32[]{:S(2)}) %collective-permute-start) | collective-permute-done | bytes 65568 | tf_op jit(solution)/shard_map/ppermute | solution.py:35
  12.1 7.0 %collective-permute-start.1 = (bf16[128,256]{1,0:T(8,128)(2,1)S(1)}, bf16[128,256]{1,0:T(8,128)(2,1)S(1)}, u32[]{:S(2)}, u32[]{:S(2)}) collective-permute-start(bf16[128,256]{1,0:T(8,128)(2,1)S(1)} %collective-permute-done.from3_ref), channel_id=1, source_target_pairs={{0,96},{32,128},{64,160},{96,192},{128,224},{160,256},{192,288},{2... | collective-permute-start | bytes 196616 | tf_op jit(solution)/shard_map/ppermute | solution.py:35
  19.1 9.1 %all_gather.3.query_ref = bf16[512,512]{1,0:T(8,128)(2,1)S(1)} all-gather(bf16[128,512]{1,0:T(8,128)(2,1)} %param.5), channel_id=1, replica_groups=mesh['z'=32,'p'=4,'h'=8] {'p'}, dimensions={0}, use_global_device_ids=true | all-gather | bytes 655360 | tf_op jit(solution)/shard_map/all_gather | solution.py:191
  28.2 0.0 collective-permute-done.1.from6_ref
  28.2 4.8 %collective-permute-start.3 = (bf16[384,256]{1,0:T(8,128)(2,1)S(1)}, bf16[384,256]{1,0:T(8,128)(2,1)S(1)}, u32[]{:S(2)}, u32[]{:S(2)}) collective-permute-start(bf16[384,256]{1,0:T(8,128)(2,1)S(1)} %trio.1.kv_ref), channel_id=1, source_target_pairs={{0,32},{32,64},{64,96},{96,128},{128,160},{160,192},{192,224},{224... | collective-permute-start | bytes 589832 | tf_op jit(solution)/shard_map/ppermute | solution.py:35
  33.0 5.3 %collective-permute-start.2 = (bf16[384,256]{1,0:T(8,128)(2,1)S(1)}, bf16[384,256]{1,0:T(8,128)(2,1)S(1)}, u32[]{:S(2)}, u32[]{:S(2)}) collective-permute-start(bf16[384,256]{1,0:T(8,128)(2,1)S(1)} %trio.1.kv_ref), channel_id=1, source_target_pairs={{0,64},{32,96},{64,128},{96,160},{128,192},{160,224},{192,256},{22... | collective-permute-start | bytes 589832 | tf_op jit(solution)/shard_map/ppermute | solution.py:35
  38.3 2.4 %near.1 = (f32[4,128,512]{2,1,0:T(8,128)S(1)}, f32[4,8,512]{2,1,0:T(8,128)S(1)}) custom-call(s32[2]{0:T(128)S(1)} %pad_add_fusion.where_ref, bf16[512,512]{1,0:T(8,128)(2,1)S(1)} %all_gather.3.query_ref, s32[8,128]{1,0:T(8,128)S(1)} %low.1.low_ref, bf16[384,256]{1,0:T(8,128)(2,1)S(1)} %trio.1.kv_ref), custom_call_target="tpu_custom_call" | custom-call | flops 402653184 | bytes 3145728 | tf_op jit(solution)/shard_map/near/pallas_call | solution.py:120
  40.7 0.0 collective-permute-done.3.kv_ref
  40.7 2.4 %middle.1 = (f32[4,128,512]{2,1,0:T(8,128)S(1)}, f32[4,8,512]{2,1,0:T(8,128)S(1)}) custom-call(s32[2]{0:T(128)S(1)} %pad_add_fusion.where_ref, bf16[512,512]{1,0:T(8,128)(2,1)S(1)} %all_gather.3.query_ref, s32[8,128]{1,0:T(8,128)S(1)} %low.1.low_ref, bf16[384,256]{1,0:T(8,128)(2,1)S(1)} %collective-permute-done.3.kv_ref, ...), custom_call_target="tpu_custom_call" | custom-call | flops 402653184 | bytes 3145728 | tf_op jit(solution)/shard_map/middle/pallas_call | solution.py:120
  43.1 5.0 %collective-permute-done.2.kv_ref = bf16[384,256]{1,0:T(8,128)(2,1)S(1)} collective-permute-done((bf16[384,256]{1,0:T(8,128)(2,1)S(1)}, bf16[384,256]{1,0:T(8,128)(2,1)S(1)}, u32[]{:S(2)}, u32[]{:S(2)}) %collective-permute-start.2) | collective-permute-done | bytes 196640 | tf_op jit(solution)/shard_map/ppermute | solution.py:35
  48.1 2.4 %far.1 = bf16[4,144,512]{2,1,0:T(8,128)(2,1)S(1)} custom-call(s32[2]{0:T(128)S(1)} %pad_add_fusion.where_ref, bf16[512,512]{1,0:T(8,128)(2,1)S(1)} %all_gather.3.query_ref, s32[8,128]{1,0:T(8,128)S(1)} %low.1.low_ref, bf16[384,256]{1,0:T(8,128)(2,1)S(1)} %collective-permute-done.2.kv_ref, f32[4,128,512]{2,1,0:T(8,128)S(1)} %get-tuple-element.21.refs_0_, ...), custom_call_target="tpu_custom_call" | custom-call | flops 402653184 | bytes 3145728 | tf_op jit(solution)/shard_map/far/pallas_call | solution.py:120
  50.5 14.4 %all_to_all.10.parts_ref = bf16[4,144,512]{2,1,0:T(8,128)(2,1)S(1)} all-to-all(bf16[4,144,512]{2,1,0:T(8,128)(2,1)S(1)} %far.1), channel_id=1, replica_groups=mesh['z'=32,'p'=4,'h'=8] {'p'}, dimensions={0} | all-to-all | bytes 1179648 | tf_op jit(solution)/shard_map/all_to_all | solution.py:200
  64.9 0.3 combine.1
  65.2 19.5 %all_to_all.11.rows_ref = bf16[8,128,512]{2,1,0:T(8,128)(2,1)S(1)} all-to-all(bf16[8,128,512]{2,1,0:T(8,128)(2,1)S(1)} %combine.1), channel_id=1, replica_groups=mesh['z'=32,'p'=4,'h'=8] {'h'}, dimensions={0} | all-to-all | bytes 2097152 | tf_op jit(solution)/shard_map/all_to_all | solution.py:202
  84.7 0.0 copy-done
  84.7 2.0 %project.1 = bf16[128,1024]{1,0:T(8,128)(2,1)} custom-call(bf16[8,128,512]{2,1,0:T(8,128)(2,1)S(1)} %all_to_all.11.rows_ref, bf16[4096,1024]{1,0:T(8,128)(2,1)S(1)} %copy-done), custom_call_target="tpu_custom_call" | custom-call | flops 1048576 | bytes 524288 | tf_op jit(solution)/shard_map/project/pallas_call | solution.py:161
  (2 shorter events, 0.0 us)
Async XLA Ops:
  0.0 0.8 copy-start.2
  0.8 0.8 copy-start.3
  1.6 10.6 %collective-permute-start = (bf16[128,256]{1,0:T(8,128)(2,1)S(1)}, bf16[128,256]{1,0:T(8,128)(2,1)S(1)}, u32[]{:S(2)}, u32[]{:S(2)}) collective-permute-start(bf16[128,256]{1,0:T(8,128)(2,1)S(1)} %pack.1.own_ref), channel_id=1, source_target_pairs={{0,96},{32,128},{64,160},{96,192},{128,224},{160,256},{192,288},{2... | collective-permute-start | bytes 196616 | tf_op jit(solution)/shard_map/ppermute | solution.py:35
  8.1 76.6 %copy-start = (bf16[4096,1024]{1,0:T(8,128)(2,1)S(1)}, bf16[4096,1024]{1,0:T(8,128)(2,1)}, u32[]{:S(2)}) copy-start(bf16[4096,1024]{1,0:T(8,128)(2,1)} %weight_ref.1) | copy-start | bytes 25165828
  8.2 1.0 %copy-start.1 = (s32[16384]{0:T(1024)S(1)}, s32[16384]{0:T(1024)}, u32[]{:S(2)}) copy-start(s32[16384]{0:T(1024)} %param.8) | copy-start | bytes 196612
  12.1 16.1 %collective-permute-start.1 = (bf16[128,256]{1,0:T(8,128)(2,1)S(1)}, bf16[128,256]{1,0:T(8,128)(2,1)S(1)}, u32[]{:S(2)}, u32[]{:S(2)}) collective-permute-start(bf16[128,256]{1,0:T(8,128)(2,1)S(1)} %collective-permute-done.from3_ref), channel_id=1, source_target_pairs={{0,96},{32,128},{64,160},{96,192},{128,224},{160,256},{192,288},{2... | collective-permute-start | bytes 196616 | tf_op jit(solution)/shard_map/ppermute | solution.py:35
  28.2 12.5 %collective-permute-start.3 = (bf16[384,256]{1,0:T(8,128)(2,1)S(1)}, bf16[384,256]{1,0:T(8,128)(2,1)S(1)}, u32[]{:S(2)}, u32[]{:S(2)}) collective-permute-start(bf16[384,256]{1,0:T(8,128)(2,1)S(1)} %trio.1.kv_ref), channel_id=1, source_target_pairs={{0,32},{32,64},{64,96},{96,128},{128,160},{160,192},{192,224},{224... | collective-permute-start | bytes 589832 | tf_op jit(solution)/shard_map/ppermute | solution.py:35
  33.0 15.1 %collective-permute-start.2 = (bf16[384,256]{1,0:T(8,128)(2,1)S(1)}, bf16[384,256]{1,0:T(8,128)(2,1)S(1)}, u32[]{:S(2)}, u32[]{:S(2)}) collective-permute-start(bf16[384,256]{1,0:T(8,128)(2,1)S(1)} %trio.1.kv_ref), channel_id=1, source_target_pairs={{0,64},{32,96},{64,128},{96,160},{128,192},{160,224},{192,256},{22... | collective-permute-start | bytes 589832 | tf_op jit(solution)/shard_map/ppermute | solution.py:35

commit v5 on v4

--- a/solution.py
+++ b/solution.py
@@ -10,6 +10,7 @@
 HD = 128
 BLK = 128
 GROUP = 4
+PAIR = 2
 LANES = 4
 WINDOW = 31 * BLK
 PLANE = LANES * BLK
@@ -30,23 +31,17 @@
 )
 
 
-def shift(block, distance):
-    planes = lax.axis_size("z")
-    return lax.ppermute(block, "z", [(i, i + distance) for i in range(planes - distance)])
-
-
-def pack_kernel(key_ref, value_ref, out_ref, sems):
-    key_copy = pltpu.make_async_copy(key_ref, out_ref.at[:, pl.ds(0, HD)], sems.at[0])
-    value_copy = pltpu.make_async_copy(value_ref, out_ref.at[:, pl.ds(HD, HD)], sems.at[1])
-    key_copy.start()
-    value_copy.start()
-    key_copy.wait()
-    value_copy.wait()
-
-
-def trio_kernel(own_ref, from3_ref, from6_ref, out_ref):
-    for n, ref in enumerate((own_ref, from3_ref, from6_ref)):
-        out_ref[n * BLK : (n + 1) * BLK] = ref[...]
+def shift_by_core(block, distances):
+    planes, cores = lax.axis_size("z"), lax.axis_size("c")
+    route = [
+        (z * cores + c, (z + distances[c]) * cores + c) for c in range(cores) for z in range(planes - distances[c])
+    ]
+    return lax.ppermute(block, ("z", "c"), route)
+
+
+def pack_kernel(key_ref, value_ref, out_ref):
+    out_ref[:, :HD] = key_ref[...]
+    out_ref[:, HD:] = value_ref[...]
 
 
 def low_kernel(where_ref, segment_ref, out_ref):
@@ -63,12 +58,28 @@
     out_ref[LANES:] = jnp.zeros((8 - LANES, BLK), jnp.int32)
 
 
-def attend_kernel(distances, first, last, where_ref, query_ref, low_ref, kv_ref, *refs):
-    old, refs = ((), refs) if first else (refs[:2], refs[2:])
-    plane_first = where_ref[0] * PLANE
-    own_first = plane_first + where_ref[1] * BLK
-    keys = kv_ref[:, :HD]
-    values_t = kv_ref[:, HD:].astype(jnp.float32).T.astype(jnp.bfloat16)
+def attend_kernel(near, where_ref, query_ref, low_ref, *refs):
+    first, last = near, not near
+    plane, lane = where_ref[0], where_ref[1]
+    core = lane % PAIR
+    plane_first = plane * PLANE
+    side_first = plane_first + (lane - core) * BLK
+    if near:
+        own_ref, *pairs = refs[:3]
+        old, refs = (), refs[3:]
+        own_row = pl.multiple_of(core * BLK, BLK)
+        blocks, firsts = [own_ref[pl.ds(own_row, BLK), :]], [side_first + own_row]
+        distances = (1 + core, 3 + 3 * core)
+    else:
+        pairs, old, refs = refs[:2], refs[2:4], refs[4:]
+        blocks, firsts = [], []
+        distances = (4 + 3 * core, 5 + 3 * core)
+    for ref, distance in zip(pairs, distances):
+        blocks.append(ref[...])
+        firsts += [side_first + n * BLK - distance * PLANE for n in range(PAIR)]
+    held = jnp.concatenate(blocks, axis=0)
+    keys = held[:, :HD]
+    values_t = held[:, HD:].astype(jnp.float32).T.astype(jnp.bfloat16)
     sub = lax.broadcasted_iota(jnp.int32, (BLK, ROWS), 0)
     token = lax.broadcasted_iota(jnp.int32, (1, ROWS), 1) % BLK
 
@@ -78,10 +89,9 @@
         scores = lax.dot_general(keys, queries, (((1,), (1,)), ((), ())), preferred_element_type=jnp.float32)
         low = jnp.concatenate([low_ref[pl.ds(block, 1), :]] * GROUP, axis=1)
         parts = []
-        for n, distance in enumerate(distances):
-            key_first = own_first - distance * PLANE
+        for n, key_first in enumerate(firsts):
             allowed = sub >= low - key_first
-            if distance == 0:
+            if near and n == 0:
                 allowed = allowed & (sub <= plane_first + block * BLK + token - key_first)
             parts.append(jnp.where(allowed, scores[n * BLK : (n + 1) * BLK] * SCALE2, MASKED))
         top = jnp.max(functools.reduce(jnp.maximum, parts), axis=0, keepdims=True)
@@ -114,17 +124,17 @@
     lax.fori_loop(0, LANES, one_block, 0, unroll=UNROLL)
 
 
-def attend(name, distances, first, last, *args):
-    out = jax.ShapeDtypeStruct((LANES, HD + PIECES, ROWS), jnp.bfloat16) if last else STATE
-    pairs = LANES * ROWS * len(distances) * BLK
+def attend(near, *args):
+    out = STATE if near else jax.ShapeDtypeStruct((LANES, HD + PIECES, ROWS), jnp.bfloat16)
+    pairs = LANES * ROWS * (5 if near else 4) * BLK
     return pl.pallas_call(
-        functools.partial(attend_kernel, distances, first, last),
+        functools.partial(attend_kernel, near),
         out_shape=out,
         in_specs=[SMEM] + [VREF] * (len(args) - 1),
-        out_specs=VREF if last else (VREF, VREF),
+        out_specs=(VREF, VREF) if near else VREF,
         compiler_params=PARAMS,
         cost_estimate=pl.CostEstimate(flops=4 * pairs * HD, bytes_accessed=3 << 20, transcendentals=pairs),
-        name=name,
+        name="near" if near else "far",
     )(*args)
 
 
@@ -169,35 +179,22 @@
     )(*args)
 
 
-def pack(keys, values):
-    return pl.pallas_call(
-        pack_kernel,
-        out_shape=jax.ShapeDtypeStruct((BLK, 2 * HD), keys.dtype),
-        in_specs=[pl.BlockSpec(memory_space=pltpu.HBM)] * 2,
-        out_specs=VREF,
-        scratch_shapes=[pltpu.SemaphoreType.DMA((2,))],
-        compiler_params=PARAMS,
-        cost_estimate=pl.CostEstimate(flops=0, bytes_accessed=1 << 17, transcendentals=0),
-        name="pack",
-    )(keys, values)
-
-
 def on_device(queries, keys, values, segments, out_weight):
-    plane, lane = lax.axis_index("z"), lax.axis_index("p")
+    plane, lane = lax.axis_index("z"), lax.axis_index(("y", "c"))
     where = jnp.stack([plane, lane]).astype(jnp.int32)
     low = small(low_kernel, "low", (8, BLK), jnp.int32, where, segments.reshape(-1, BLK), smem=1)
-    own = pack(keys, values)
+    pair_keys, pair_values = lax.all_gather((keys, values), "c", tiled=True)
+    own = small(pack_kernel, "pack", (PAIR * BLK, 2 * HD), keys.dtype, pair_keys, pair_values)
+    from36 = shift_by_core(own, (3, 6))
+    from12 = shift_by_core(own, (1, 2))
     queries, _ = lax.optimization_barrier((queries, own))
-    plane_queries = lax.all_gather(queries, "p", tiled=True)
-    from3, low = lax.optimization_barrier((shift(own, 3), low))
-    from6, plane_queries = lax.optimization_barrier((shift(from3, 3), plane_queries))
-    trio = small(trio_kernel, "trio", (3 * BLK, 2 * HD), keys.dtype, own, from3, from6)
-    one, two = shift(trio, 1), shift(trio, 2)
+    plane_queries = lax.all_gather(queries, ("y", "c"), tiled=True)
+    from36, plane_queries, low = lax.optimization_barrier((from36, plane_queries, low))
+    one, two = shift_by_core(from36, (1, 1)), shift_by_core(from36, (2, 2))
     common = (where, plane_queries, low)
-    state = attend("near", (0, 3, 6), True, False, *common, trio)
-    state = attend("middle", (1, 4, 7), False, False, *common, one, *state)
-    partial = attend("far", (2, 5, 8), False, True, *common, two, *state)
-    parts = lax.all_to_all(partial, "p", 0, 0, tiled=True)
+    state = attend(True, *common, own, from12, from36)
+    partial = attend(False, *common, one, two, *state)
+    parts = lax.all_to_all(partial, ("y", "c"), 0, 0, tiled=True)
     copies = small(combine_kernel, "combine", (HEADS, BLK, GROUP * HD), jnp.bfloat16, parts)
     attended = lax.all_to_all(copies, "h", 0, 0, tiled=True)
     return small(project_kernel, "project", (BLK, out_weight.shape[1]), jnp.bfloat16, attended, out_weight)
@@ -205,8 +202,9 @@
 
 def solution(mesh):
     planes = mesh.shape["seq"] // LANES
-    fine = Mesh(mesh.devices.reshape(planes, LANES, mesh.shape["head"]), ("z", "p", "h"))
-    tokens = ("z", "p")
+    heads = mesh.shape["head"]
+    fine = Mesh(mesh.devices.reshape(planes, LANES // PAIR, PAIR, heads), ("z", "y", "c", "h"))
+    tokens = ("z", "y", "c")
     return jax.shard_map(
         on_device,
         mesh=fine,

time: 87.1 us -> 86.8 us (level)
  the two profiles are of different devices: /device:TPU:256 before, /device:TPU:96 now
where the time goes in v5:
time: 86.8 us; the launch traced here: 86.5 us
  blocking collectives  52.2 us (60%)
  starting transfers between devices  21.9 us (25%)
  Pallas kernels  8.87 us (10%)
  waiting for transfers between devices  2.35 us (3%)
  local copies, waits for them, and re-layouts  0.99 us (1%)
    ppermute x4, starting transfers between devices, shift_by_core(): return lax.ppermute(block, ('z', 'c'), route)  21.9 us
    all_to_all x1, blocking collectives, on_device(): attended = lax.all_to_all(copies, 'h', 0, 0, tiled=True)  19.8 us
    all_gather x1, blocking collectives, on_device(): plane_queries = lax.all_gather(queries, ('y', 'c'), tiled=True)  14.9 us
    all_to_all x1, blocking collectives, on_device(): parts = lax.all_to_all(partial, ('y', 'c'), 0, 0, tiled=True)  13.4 us
    pallas_call x2, Pallas kernels, attend(): pl.pallas_call(functools.partial(attend_kernel, near), out_shape=out, in_...  5.88 us
    all_gather x2, blocking collectives, on_device(): pair_keys, pair_values = lax.all_gather((keys, values), 'c', tiled=True)  4.1 us
    pallas_call x4, Pallas kernels, small(): pl.pallas_call(kernel, out_shape=jax.ShapeDtypeStruct(shape, dtype), in_s...  2.99 us
    ppermute x4, waiting for transfers between devices, shift_by_core(): return lax.ppermute(block, ('z', 'c'), route)  2.35 us
  transfers between devices with their start and end apart: 4, of which 1 were waited for; matrix products, arithmetic and copies ran while one was open for 0% of the time, Pallas kernels for 4%

profile of v5, /device:TPU:96, one launch (start us, length us, event | category | flops | bytes accessed | tf_op | source)
XLA Modules:
  0.0 86.5 jit_solution(13919356817155993611)
XLA Ops:
  0.0 2.1 %all_gather.9.key_ref = bf16[256,128]{1,0:T(8,128)(2,1)S(1)} all-gather(bf16[128,128]{1,0:T(8,128)(2,1)} %param.6), channel_id=1, replica_groups=mesh['z'=32,'y'=2,'c'=2,'h'=8] {'c'}, dimensions={0}, use_global_device_ids=true | all-gather | bytes 98304 | tf_op jit(solution)/shard_map/all_gather | solution.py:186
  2.1 2.1 %all_gather.10.value_ref = bf16[256,128]{1,0:T(8,128)(2,1)S(1)} all-gather(bf16[128,128]{1,0:T(8,128)(2,1)} %param.7), channel_id=1, replica_groups=mesh['z'=32,'y'=2,'c'=2,'h'=8] {'c'}, dimensions={0}, use_global_device_ids=true | all-gather | bytes 98304 | tf_op jit(solution)/shard_map/all_gather | solution.py:186
  4.1 5.0 %collective-permute-start.3 = (bf16[256,256]{1,0:T(8,128)(2,1)S(1)}, bf16[256,256]{1,0:T(8,128)(2,1)S(1)}, u32[]{:S(2)}, u32[]{:S(2)}) collective-permute-start(bf16[256,256]{1,0:T(8,128)(2,1)S(1)} %pack.1.refs_0_), channel_id=1, source_target_pairs={{0,32},{32,64},{64,96},{96,128},{128,160},{160,192},{192,224},{224... | collective-permute-start | bytes 393224 | tf_op jit(solution)/shard_map/ppermute | solution.py:39
  9.2 6.5 %collective-permute-start = (bf16[256,256]{1,0:T(8,128)(2,1)S(1)}, bf16[256,256]{1,0:T(8,128)(2,1)S(1)}, u32[]{:S(2)}, u32[]{:S(2)}) collective-permute-start(bf16[256,256]{1,0:T(8,128)(2,1)S(1)} %pack.1.refs_0_), channel_id=1, source_target_pairs={{0,96},{32,128},{64,160},{96,192},{128,224},{160,256},{192,288},{2... | collective-permute-start | bytes 393224 | tf_op jit(solution)/shard_map/ppermute | solution.py:39
  15.7 14.9 %all_gather.11.query_ref = bf16[512,512]{1,0:T(8,128)(2,1)S(1)} all-gather(bf16[128,512]{1,0:T(8,128)(2,1)} %param.5), channel_id=1, replica_groups=mesh['z'=32,'y'=2,'c'=2,'h'=8] {'y','c'}, dimensions={0}, use_global_device_ids=true | all-gather | bytes 655360 | tf_op jit(solution)/shard_map/all_gather | solution.py:191
  30.6 0.0 copy-start
  30.6 0.1 pad_add_fusion.where_ref
  30.7 0.0 copy-start.1
  30.7 1.0 %copy-done.1 = s32[16384]{0:T(1024)S(1)} copy-done((s32[16384]{0:T(1024)S(1)}, s32[16384]{0:T(1024)}, u32[]{:S(2)}) %copy-start.1) | copy-done | bytes 65560
  31.7 0.7 low.1.low_ref
  32.4 0.0 collective-permute-done.refs_2_
  32.4 6.5 %collective-permute-start.2 = (bf16[256,256]{1,0:T(8,128)(2,1)S(1)}, bf16[256,256]{1,0:T(8,128)(2,1)S(1)}, u32[]{:S(2)}, u32[]{:S(2)}) collective-permute-start(bf16[256,256]{1,0:T(8,128)(2,1)S(1)} %collective-permute-done.refs_2_), channel_id=1, source_target_pairs={{0,64},{32,96},{64,128},{96,160},{128,192},{160,224},{192,256},{22... | collective-permute-start | bytes 393224 | tf_op jit(solution)/shard_map/ppermute | solution.py:39
  38.9 3.8 %collective-permute-start.1 = (bf16[256,256]{1,0:T(8,128)(2,1)S(1)}, bf16[256,256]{1,0:T(8,128)(2,1)S(1)}, u32[]{:S(2)}, u32[]{:S(2)}) collective-permute-start(bf16[256,256]{1,0:T(8,128)(2,1)S(1)} %collective-permute-done.refs_2_), channel_id=1, source_target_pairs={{0,32},{32,64},{64,96},{96,128},{128,160},{160,192},{192,224},{224... | collective-permute-start | bytes 393224 | tf_op jit(solution)/shard_map/ppermute | solution.py:39
  42.8 0.0 collective-permute-done.3.refs_1_
  42.8 3.2 %near.1 = (f32[4,128,512]{2,1,0:T(8,128)S(1)}, f32[4,8,512]{2,1,0:T(8,128)S(1)}) custom-call(s32[2]{0:T(128)S(1)} %pad_add_fusion.where_ref, bf16[512,512]{1,0:T(8,128)(2,1)S(1)} %all_gather.11.query_ref, s32[8,128]{1,0:T(8,128)S(1)} %low.1.low_ref, bf16[256,256]{1,0:T(8,128)(2,1)S(1)} %pack.1.refs_0_, bf16[256,256]{1,0:T(8,128)(2,1)S(1)} %collective-permute-done.3.refs_1_, ...), custom_call_target="tpu_custom_call" | custom-call | flops 671088640 | bytes 3145728 | tf_op jit(solution)/shard_map/near/pallas_call | solution.py:130
  46.0 0.0 collective-permute-done.2.refs_1_
  46.0 2.3 %collective-permute-done.1.refs_0_ = bf16[256,256]{1,0:T(8,128)(2,1)S(1)} collective-permute-done((bf16[256,256]{1,0:T(8,128)(2,1)S(1)}, bf16[256,256]{1,0:T(8,128)(2,1)S(1)}, u32[]{:S(2)}, u32[]{:S(2)}) %collective-permute-start.1) | collective-permute-done | bytes 131104 | tf_op jit(solution)/shard_map/ppermute | solution.py:39
  48.3 2.7 %far.1 = bf16[4,144,512]{2,1,0:T(8,128)(2,1)S(1)} custom-call(s32[2]{0:T(128)S(1)} %pad_add_fusion.where_ref, bf16[512,512]{1,0:T(8,128)(2,1)S(1)} %all_gather.11.query_ref, s32[8,128]{1,0:T(8,128)S(1)} %low.1.low_ref, bf16[256,256]{1,0:T(8,128)(2,1)S(1)} %collective-permute-done.1.refs_0_, bf16[256,256]{1,0:T(8,128)(2,1)S(1)} %collective-permute-done.2.refs_1_, ...), custom_call_target="tpu_custom_call" | custom-call | flops 536870912 | bytes 3145728 | tf_op jit(solution)/shard_map/far/pallas_call | solution.py:130
  51.0 13.4 %all_to_all.10.parts_ref = bf16[4,144,512]{2,1,0:T(8,128)(2,1)S(1)} all-to-all(bf16[4,144,512]{2,1,0:T(8,128)(2,1)S(1)} %far.1), channel_id=1, replica_groups=mesh['z'=32,'y'=2,'c'=2,'h'=8] {'y','c'}, dimensions={0} | all-to-all | bytes 1179648 | tf_op jit(solution)/shard_map/all_to_all | solution.py:197
  64.5 0.3 combine.1
  64.8 19.8 %all_to_all.11.rows_ref = bf16[8,128,512]{2,1,0:T(8,128)(2,1)S(1)} all-to-all(bf16[8,128,512]{2,1,0:T(8,128)(2,1)S(1)} %combine.1), channel_id=1, replica_groups=mesh['z'=32,'y'=2,'c'=2,'h'=8] {'h'}, dimensions={0} | all-to-all | bytes 2097152 | tf_op jit(solution)/shard_map/all_to_all | solution.py:199
  84.6 0.0 copy-done
  84.6 2.0 %project.1 = bf16[128,1024]{1,0:T(8,128)(2,1)} custom-call(bf16[8,128,512]{2,1,0:T(8,128)(2,1)S(1)} %all_to_all.11.rows_ref, bf16[4096,1024]{1,0:T(8,128)(2,1)S(1)} %copy-done), custom_call_target="tpu_custom_call" | custom-call | flops 1048576 | bytes 524288 | tf_op jit(solution)/shard_map/project/pallas_call | solution.py:171
  (1 shorter events, 0.0 us)
Async XLA Ops:
  4.1 38.6 %collective-permute-start.3 = (bf16[256,256]{1,0:T(8,128)(2,1)S(1)}, bf16[256,256]{1,0:T(8,128)(2,1)S(1)}, u32[]{:S(2)}, u32[]{:S(2)}) collective-permute-start(bf16[256,256]{1,0:T(8,128)(2,1)S(1)} %pack.1.refs_0_), channel_id=1, source_target_pairs={{0,32},{32,64},{64,96},{96,128},{128,160},{160,192},{192,224},{224... | collective-permute-start | bytes 393224 | tf_op jit(solution)/shard_map/ppermute | solution.py:39
  9.2 23.2 %collective-permute-start = (bf16[256,256]{1,0:T(8,128)(2,1)S(1)}, bf16[256,256]{1,0:T(8,128)(2,1)S(1)}, u32[]{:S(2)}, u32[]{:S(2)}) collective-permute-start(bf16[256,256]{1,0:T(8,128)(2,1)S(1)} %pack.1.refs_0_), channel_id=1, source_target_pairs={{0,96},{32,128},{64,160},{96,192},{128,224},{160,256},{192,288},{2... | collective-permute-start | bytes 393224 | tf_op jit(solution)/shard_map/ppermute | solution.py:39
  30.6 54.0 %copy-start = (bf16[4096,1024]{1,0:T(8,128)(2,1)S(1)}, bf16[4096,1024]{1,0:T(8,128)(2,1)}, u32[]{:S(2)}) copy-start(bf16[4096,1024]{1,0:T(8,128)(2,1)} %weight_ref.1) | copy-start | bytes 25165828
  30.7 1.0 %copy-start.1 = (s32[16384]{0:T(1024)S(1)}, s32[16384]{0:T(1024)}, u32[]{:S(2)}) copy-start(s32[16384]{0:T(1024)} %param.8) | copy-start | bytes 196612
  32.4 13.6 %collective-permute-start.2 = (bf16[256,256]{1,0:T(8,128)(2,1)S(1)}, bf16[256,256]{1,0:T(8,128)(2,1)S(1)}, u32[]{:S(2)}, u32[]{:S(2)}) collective-permute-start(bf16[256,256]{1,0:T(8,128)(2,1)S(1)} %collective-permute-done.refs_2_), channel_id=1, source_target_pairs={{0,64},{32,96},{64,128},{96,160},{128,192},{160,224},{192,256},{22... | collective-permute-start | bytes 393224 | tf_op jit(solution)/shard_map/ppermute | solution.py:39
  38.9 9.4 %collective-permute-start.1 = (bf16[256,256]{1,0:T(8,128)(2,1)S(1)}, bf16[256,256]{1,0:T(8,128)(2,1)S(1)}, u32[]{:S(2)}, u32[]{:S(2)}) collective-permute-start(bf16[256,256]{1,0:T(8,128)(2,1)S(1)} %collective-permute-done.refs_2_), channel_id=1, source_target_pairs={{0,32},{32,64},{64,96},{96,128},{128,160},{160,192},{192,224},{224... | collective-permute-start | bytes 393224 | tf_op jit(solution)/shard_map/ppermute | solution.py:39

commit v6 on v5

--- a/solution.py
+++ b/solution.py
@@ -20,7 +20,6 @@
 SEGMENT_VALUES = 6
 SCALE2 = float(HD**-0.5 * 1.4426950408889634)
 MASKED = -1e30
-UNROLL = LANES
 VMEM = 24 * 1024 * 1024
 PARAMS = pltpu.CompilerParams(vmem_limit_bytes=VMEM)
 SMEM = pl.BlockSpec(memory_space=pltpu.SMEM)
@@ -37,11 +36,6 @@
         (z * cores + c, (z + distances[c]) * cores + c) for c in range(cores) for z in range(planes - distances[c])
     ]
     return lax.ppermute(block, ("z", "c"), route)
-
-
-def pack_kernel(key_ref, value_ref, out_ref):
-    out_ref[:, :HD] = key_ref[...]
-    out_ref[:, HD:] = value_ref[...]
 
 
 def low_kernel(where_ref, segment_ref, out_ref):
@@ -58,7 +52,7 @@
     out_ref[LANES:] = jnp.zeros((8 - LANES, BLK), jnp.int32)
 
 
-def attend_kernel(near, where_ref, query_ref, low_ref, *refs):
+def attend_kernel(near, where_ref, mine_ref, other_ref, low_ref, *refs):
     first, last = near, not near
     plane, lane = where_ref[0], where_ref[1]
     core = lane % PAIR
@@ -67,24 +61,25 @@
     if near:
         own_ref, *pairs = refs[:3]
         old, refs = (), refs[3:]
-        own_row = pl.multiple_of(core * BLK, BLK)
-        blocks, firsts = [own_ref[pl.ds(own_row, BLK), :]], [side_first + own_row]
+        keys, values, firsts = [own_ref[2 * core]], [own_ref[2 * core + 1]], [side_first + core * BLK]
         distances = (1 + core, 3 + 3 * core)
     else:
         pairs, old, refs = refs[:2], refs[2:4], refs[4:]
-        blocks, firsts = [], []
+        keys, values, firsts = [], [], []
         distances = (4 + 3 * core, 5 + 3 * core)
     for ref, distance in zip(pairs, distances):
-        blocks.append(ref[...])
-        firsts += [side_first + n * BLK - distance * PLANE for n in range(PAIR)]
-    held = jnp.concatenate(blocks, axis=0)
-    keys = held[:, :HD]
-    values_t = held[:, HD:].astype(jnp.float32).T.astype(jnp.bfloat16)
+        for n in range(PAIR):
+            keys.append(ref[2 * n])
+            values.append(ref[2 * n + 1])
+            firsts.append(side_first + n * BLK - distance * PLANE)
+    keys = jnp.concatenate(keys, axis=0)
+    values_t = jnp.concatenate(values, axis=0).astype(jnp.float32).T.astype(jnp.bfloat16)
     sub = lax.broadcasted_iota(jnp.int32, (BLK, ROWS), 0)
     token = lax.broadcasted_iota(jnp.int32, (1, ROWS), 1) % BLK
-
-    def one_block(block, carry):
-        rows = pl.ds(pl.multiple_of(block * BLK, BLK), BLK)
+    for index in range(LANES):
+        query_ref, of_core = (mine_ref, other_ref)[index // PAIR], index % PAIR
+        block = of_core + ((lane - core) if index < PAIR else (PAIR - lane + core))
+        rows = slice(of_core * BLK, (of_core + 1) * BLK)
         queries = jnp.concatenate([query_ref[rows, g * HD : (g + 1) * HD] for g in range(GROUP)], axis=0)
         scores = lax.dot_general(keys, queries, (((1,), (1,)), ((), ())), preferred_element_type=jnp.float32)
         low = jnp.concatenate([low_ref[pl.ds(block, 1), :]] * GROUP, axis=1)
@@ -96,7 +91,7 @@
             parts.append(jnp.where(allowed, scores[n * BLK : (n + 1) * BLK] * SCALE2, MASKED))
         top = jnp.max(functools.reduce(jnp.maximum, parts), axis=0, keepdims=True)
         if not first:
-            old_top = old[1][block, 0:1]
+            old_top = old[1][index, 0:1]
             top = jnp.maximum(top, old_top)
         weights = [jnp.exp2(piece - top) for piece in parts]
         total = jnp.sum(functools.reduce(jnp.add, weights), axis=0, keepdims=True)
@@ -104,13 +99,13 @@
         acc = jnp.dot(values_t, weights, preferred_element_type=jnp.float32)
         if not first:
             factor = jnp.exp2(old_top - top)
-            total = total + old[1][block, 1:2] * factor
-            acc = acc + old[0][block] * factor
+            total = total + old[1][index, 1:2] * factor
+            acc = acc + old[0][index] * factor
         if not last:
-            refs[0][block] = acc
-            refs[1][block, 0:1] = top
-            refs[1][block, 1:2] = total
-            return carry
+            refs[0][index] = acc
+            refs[1][index, 0:1] = top
+            refs[1][index, 1:2] = total
+            continue
         refs[0][block, :HD] = (acc * (1.0 / total)).astype(jnp.bfloat16)
         spread = top + jnp.log2(total)
         high = spread.astype(jnp.bfloat16).astype(jnp.float32)
@@ -119,9 +114,6 @@
         row = lax.broadcasted_iota(jnp.int32, (PIECES, ROWS), 0)
         pieces = jnp.where(row == 0, high, jnp.where(row == 1, middle, jnp.where(row == 2, rest - middle, 0.0)))
         refs[0][block, HD:] = pieces.astype(jnp.bfloat16)
-        return carry
-
-    lax.fori_loop(0, LANES, one_block, 0, unroll=UNROLL)
 
 
 def attend(near, *args):
@@ -183,15 +175,16 @@
     plane, lane = lax.axis_index("z"), lax.axis_index(("y", "c"))
     where = jnp.stack([plane, lane]).astype(jnp.int32)
     low = small(low_kernel, "low", (8, BLK), jnp.int32, where, segments.reshape(-1, BLK), smem=1)
-    pair_keys, pair_values = lax.all_gather((keys, values), "c", tiled=True)
-    own = small(pack_kernel, "pack", (PAIR * BLK, 2 * HD), keys.dtype, pair_keys, pair_values)
+    is_key = lax.broadcasted_iota(jnp.int32, (2, BLK, HD), 0) == 0
+    own = lax.all_gather(jnp.where(is_key, keys[None], values[None]), "c", tiled=True)
     from36 = shift_by_core(own, (3, 6))
     from12 = shift_by_core(own, (1, 2))
     queries, _ = lax.optimization_barrier((queries, own))
-    plane_queries = lax.all_gather(queries, ("y", "c"), tiled=True)
-    from36, plane_queries, low = lax.optimization_barrier((from36, plane_queries, low))
+    mine = lax.all_gather(queries, "c", tiled=True)
+    from36, from12, mine, low = lax.optimization_barrier((from36, from12, mine, low))
+    other = lax.ppermute(mine, "y", [(0, 1), (1, 0)])
     one, two = shift_by_core(from36, (1, 1)), shift_by_core(from36, (2, 2))
-    common = (where, plane_queries, low)
+    common = (where, mine, other, low)
     state = attend(True, *common, own, from12, from36)
     partial = attend(False, *common, one, two, *state)
     parts = lax.all_to_all(partial, ("y", "c"), 0, 0, tiled=True)

time: 86.8 us -> 85 us (0.979)
  the two profiles are of different devices: /device:TPU:96 before, /device:TPU:384 now
where the time goes in v6:
time: 85 us; the launch traced here: 84.6 us
  blocking collectives  38.2 us (45%)
  starting transfers between devices  23.3 us (27%)
  waiting for transfers between devices  12.3 us (14%)
  Pallas kernels  8.85 us (10%)
  local copies, waits for them, and re-layouts  1 us (1%)
  other arithmetic  0.93 us (1%)
    ppermute x4, starting transfers between devices, shift_by_core(): return lax.ppermute(block, ('z', 'c'), route)  20.2 us
    all_to_all x1, blocking collectives, on_device(): attended = lax.all_to_all(copies, 'h', 0, 0, tiled=True)  19.5 us
    all_to_all x1, blocking collectives, on_device(): parts = lax.all_to_all(partial, ('y', 'c'), 0, 0, tiled=True)  13.4 us
    ppermute x4, waiting for transfers between devices, shift_by_core(): return lax.ppermute(block, ('z', 'c'), route)  12.1 us
    pallas_call x2, Pallas kernels, attend(): pl.pallas_call(functools.partial(attend_kernel, near), out_shape=out, in_...  5.88 us
    all_gather x1, blocking collectives, on_device(): mine = lax.all_gather(queries, 'c', tiled=True)  3.39 us
    ppermute x1, starting transfers between devices, on_device(): other = lax.ppermute(mine, 'y', [(0, 1), (1, 0)])  3.06 us
    pallas_call x3, Pallas kernels, small(): pl.pallas_call(kernel, out_shape=jax.ShapeDtypeStruct(shape, dtype), in_s...  2.97 us
  transfers between devices with their start and end apart: 5, of which 3 were waited for; matrix products, arithmetic and copies ran while one was open for 0% of the time, Pallas kernels for 5%

profile of v6, /device:TPU:384, one launch (start us, length us, event | category | flops | bytes accessed | tf_op | source)
XLA Modules:
  0.0 84.6 jit_solution(261182254538117646)
XLA Ops:
  0.0 0.9 %broadcast_select_fusion = bf16[2,128,128]{2,1,0:T(8,128)(2,1)S(1)} fusion(pred[2]{0:T(512)(128)(4,1)S(1)} %iota_compare_fusion, bf16[128,128]{1,0:T(8,128)(2,1)} %param.7, bf16[128,128]{1,0:T(8,128)(2,1)} %param.6), kind=kLoop, calls=%fused_computation | loop fusion | flops 32768 | bytes 131074 | tf_op jit(solution)/shard_map/jit(_where)/select_n | solution.py:179
  0.9 1.9 %all_gather.6.refs_0_ = bf16[4,128,128]{2,1,0:T(8,128)(2,1)S(1)} all-gather(bf16[2,128,128]{2,1,0:T(8,128)(2,1)S(1)} %broadcast_select_fusion), channel_id=1, replica_groups=mesh['z'=32,'y'=2,'c'=2,'h'=8] {'c'}, dimensions={0}, use_global_device_ids=true | all-gather | bytes 196608 | tf_op jit(solution)/shard_map/all_gather | solution.py:179
  2.7 3.8 %collective-permute-start.1 = (bf16[4,128,128]{2,1,0:T(8,128)(2,1)S(1)}, bf16[4,128,128]{2,1,0:T(8,128)(2,1)S(1)}, u32[]{:S(2)}, u32[]{:S(2)}) collective-permute-start(bf16[4,128,128]{2,1,0:T(8,128)(2,1)S(1)} %all_gather.6.refs_0_), channel_id=1, source_target_pairs={{0,32},{32,64},{64,96},{96,128},{128,160},{160,192},{192,224},{224... | collective-permute-start | bytes 393224 | tf_op jit(solution)/shard_map/ppermute | solution.py:38
  6.6 7.7 %collective-permute-start = (bf16[4,128,128]{2,1,0:T(8,128)(2,1)S(1)}, bf16[4,128,128]{2,1,0:T(8,128)(2,1)S(1)}, u32[]{:S(2)}, u32[]{:S(2)}) collective-permute-start(bf16[4,128,128]{2,1,0:T(8,128)(2,1)S(1)} %all_gather.6.refs_0_), channel_id=1, source_target_pairs={{0,96},{32,128},{64,160},{96,192},{128,224},{160,256},{192,288},{2... | collective-permute-start | bytes 393224 | tf_op jit(solution)/shard_map/ppermute | solution.py:38
  14.3 0.0 copy-start
  14.3 0.1 pad_add_fusion.where_ref
  14.4 0.0 copy-start.1
  14.4 1.0 %copy-done.1 = s32[16384]{0:T(1024)S(1)} copy-done((s32[16384]{0:T(1024)S(1)}, s32[16384]{0:T(1024)}, u32[]{:S(2)}) %copy-start.1) | copy-done | bytes 65560
  15.4 0.7 low.1.low_ref
  16.1 3.4 %all_gather.7.mine_ref = bf16[256,512]{1,0:T(8,128)(2,1)S(1)} all-gather(bf16[128,512]{1,0:T(8,128)(2,1)} %param.5), channel_id=1, replica_groups=mesh['z'=32,'y'=2,'c'=2,'h'=8] {'c'}, dimensions={0}, use_global_device_ids=true | all-gather | bytes 393216 | tf_op jit(solution)/shard_map/all_gather | solution.py:183
  19.5 0.0 collective-permute-done.1.refs_1_
  19.5 8.1 %collective-permute-done.refs_2_ = bf16[4,128,128]{2,1,0:T(8,128)(2,1)S(1)} collective-permute-done((bf16[4,128,128]{2,1,0:T(8,128)(2,1)S(1)}, bf16[4,128,128]{2,1,0:T(8,128)(2,1)S(1)}, u32[]{:S(2)}, u32[]{:S(2)}) %collective-permute-start) | collective-permute-done | bytes 131104 | tf_op jit(solution)/shard_map/ppermute | solution.py:38
  27.6 3.1 %collective-permute-start.2 = (bf16[256,512]{1,0:T(8,128)(2,1)S(1)}, bf16[256,512]{1,0:T(8,128)(2,1)S(1)}, u32[]{:S(2)}, u32[]{:S(2)}) collective-permute-start(bf16[256,512]{1,0:T(8,128)(2,1)S(1)} %all_gather.7.mine_ref), channel_id=1, source_target_pairs={{0,16},{16,0},{1,17},{17,1},{2,18},{18,2},{3,19},{19,3},{4,20},{20... | collective-permute-start | bytes 786440 | tf_op jit(solution)/shard_map/ppermute | solution.py:185
  30.7 3.8 %collective-permute-start.4 = (bf16[4,128,128]{2,1,0:T(8,128)(2,1)S(1)}, bf16[4,128,128]{2,1,0:T(8,128)(2,1)S(1)}, u32[]{:S(2)}, u32[]{:S(2)}) collective-permute-start(bf16[4,128,128]{2,1,0:T(8,128)(2,1)S(1)} %collective-permute-done.refs_2_), channel_id=1, source_target_pairs={{0,64},{32,96},{64,128},{96,160},{128,192},{160,224},{192,256},{22... | collective-permute-start | bytes 393224 | tf_op jit(solution)/shard_map/ppermute | solution.py:38
  34.5 4.9 %collective-permute-start.3 = (bf16[4,128,128]{2,1,0:T(8,128)(2,1)S(1)}, bf16[4,128,128]{2,1,0:T(8,128)(2,1)S(1)}, u32[]{:S(2)}, u32[]{:S(2)}) collective-permute-start(bf16[4,128,128]{2,1,0:T(8,128)(2,1)S(1)} %collective-permute-done.refs_2_), channel_id=1, source_target_pairs={{0,32},{32,64},{64,96},{96,128},{128,160},{160,192},{192,224},{224... | collective-permute-start | bytes 393224 | tf_op jit(solution)/shard_map/ppermute | solution.py:38
  39.4 0.2 collective-permute-done.2.other_ref
  39.6 3.2 %near.1 = (f32[4,128,512]{2,1,0:T(8,128)S(1)}, f32[4,8,512]{2,1,0:T(8,128)S(1)}) custom-call(s32[2]{0:T(128)S(1)} %pad_add_fusion.where_ref, bf16[256,512]{1,0:T(8,128)(2,1)S(1)} %all_gather.7.mine_ref, bf16[256,512]{1,0:T(8,128)(2,1)S(1)} %collective-permute-done.2.other_ref, s32[8,128]{1,0:T(8,128)S(1)} %low.1.low_ref, ...), custom_call_target="tpu_custom_call" | custom-call | flops 671088640 | bytes 3145728 | tf_op jit(solution)/shard_map/near/pallas_call | solution.py:122
  42.7 0.0 collective-permute-done.4.refs_1_
  42.8 4.0 %collective-permute-done.3.refs_0_ = bf16[4,128,128]{2,1,0:T(8,128)(2,1)S(1)} collective-permute-done((bf16[4,128,128]{2,1,0:T(8,128)(2,1)S(1)}, bf16[4,128,128]{2,1,0:T(8,128)(2,1)S(1)}, u32[]{:S(2)}, u32[]{:S(2)}) %collective-permute-start.3) | collective-permute-done | bytes 131104 | tf_op jit(solution)/shard_map/ppermute | solution.py:38
  46.7 2.7 %far.1 = bf16[4,144,512]{2,1,0:T(8,128)(2,1)S(1)} custom-call(s32[2]{0:T(128)S(1)} %pad_add_fusion.where_ref, bf16[256,512]{1,0:T(8,128)(2,1)S(1)} %all_gather.7.mine_ref, bf16[256,512]{1,0:T(8,128)(2,1)S(1)} %collective-permute-done.2.other_ref, s32[8,128]{1,0:T(8,128)S(1)} %low.1.low_ref, bf16[4,128,128]{2,1,0:T(8,128)(2,1)S(1)} %collective-permute-done.3.refs_0_, ...), custom_call_target="tpu_custom_call" | custom-call | flops 536870912 | bytes 3145728 | tf_op jit(solution)/shard_map/far/pallas_call | solution.py:122
  49.4 13.4 %all_to_all.10.parts_ref = bf16[4,144,512]{2,1,0:T(8,128)(2,1)S(1)} all-to-all(bf16[4,144,512]{2,1,0:T(8,128)(2,1)S(1)} %far.1), channel_id=1, replica_groups=mesh['z'=32,'y'=2,'c'=2,'h'=8] {'y','c'}, dimensions={0} | all-to-all | bytes 1179648 | tf_op jit(solution)/shard_map/all_to_all | solution.py:190
  62.9 0.3 combine.1
  63.2 19.5 %all_to_all.11.rows_ref = bf16[8,128,512]{2,1,0:T(8,128)(2,1)S(1)} all-to-all(bf16[8,128,512]{2,1,0:T(8,128)(2,1)S(1)} %combine.1), channel_id=1, replica_groups=mesh['z'=32,'y'=2,'c'=2,'h'=8] {'h'}, dimensions={0} | all-to-all | bytes 2097152 | tf_op jit(solution)/shard_map/all_to_all | solution.py:192
  82.7 0.0 copy-done
  82.7 2.0 %project.1 = bf16[128,1024]{1,0:T(8,128)(2,1)} custom-call(bf16[8,128,512]{2,1,0:T(8,128)(2,1)S(1)} %all_to_all.11.rows_ref, bf16[4096,1024]{1,0:T(8,128)(2,1)S(1)} %copy-done), custom_call_target="tpu_custom_call" | custom-call | flops 1048576 | bytes 524288 | tf_op jit(solution)/shard_map/project/pallas_call | solution.py:163
  (1 shorter events, 0.0 us)
Async XLA Ops:
  2.7 16.8 %collective-permute-start.1 = (bf16[4,128,128]{2,1,0:T(8,128)(2,1)S(1)}, bf16[4,128,128]{2,1,0:T(8,128)(2,1)S(1)}, u32[]{:S(2)}, u32[]{:S(2)}) collective-permute-start(bf16[4,128,128]{2,1,0:T(8,128)(2,1)S(1)} %all_gather.6.refs_0_), channel_id=1, source_target_pairs={{0,32},{32,64},{64,96},{96,128},{128,160},{160,192},{192,224},{224... | collective-permute-start | bytes 393224 | tf_op jit(solution)/shard_map/ppermute | solution.py:38
  6.6 21.0 %collective-permute-start = (bf16[4,128,128]{2,1,0:T(8,128)(2,1)S(1)}, bf16[4,128,128]{2,1,0:T(8,128)(2,1)S(1)}, u32[]{:S(2)}, u32[]{:S(2)}) collective-permute-start(bf16[4,128,128]{2,1,0:T(8,128)(2,1)S(1)} %all_gather.6.refs_0_), channel_id=1, source_target_pairs={{0,96},{32,128},{64,160},{96,192},{128,224},{160,256},{192,288},{2... | collective-permute-start | bytes 393224 | tf_op jit(solution)/shard_map/ppermute | solution.py:38
  14.3 68.3 %copy-start = (bf16[4096,1024]{1,0:T(8,128)(2,1)S(1)}, bf16[4096,1024]{1,0:T(8,128)(2,1)}, u32[]{:S(2)}) copy-start(bf16[4096,1024]{1,0:T(8,128)(2,1)} %weight_ref.1) | copy-start | bytes 25165828
  14.4 1.0 %copy-start.1 = (s32[16384]{0:T(1024)S(1)}, s32[16384]{0:T(1024)}, u32[]{:S(2)}) copy-start(s32[16384]{0:T(1024)} %param.8) | copy-start | bytes 196612
  27.6 12.0 %collective-permute-start.2 = (bf16[256,512]{1,0:T(8,128)(2,1)S(1)}, bf16[256,512]{1,0:T(8,128)(2,1)S(1)}, u32[]{:S(2)}, u32[]{:S(2)}) collective-permute-start(bf16[256,512]{1,0:T(8,128)(2,1)S(1)} %all_gather.7.mine_ref), channel_id=1, source_target_pairs={{0,16},{16,0},{1,17},{17,1},{2,18},{18,2},{3,19},{19,3},{4,20},{20... | collective-permute-start | bytes 786440 | tf_op jit(solution)/shard_map/ppermute | solution.py:185
  30.7 12.1 %collective-permute-start.4 = (bf16[4,128,128]{2,1,0:T(8,128)(2,1)S(1)}, bf16[4,128,128]{2,1,0:T(8,128)(2,1)S(1)}, u32[]{:S(2)}, u32[]{:S(2)}) collective-permute-start(bf16[4,128,128]{2,1,0:T(8,128)(2,1)S(1)} %collective-permute-done.refs_2_), channel_id=1, source_target_pairs={{0,64},{32,96},{64,128},{96,160},{128,192},{160,224},{192,256},{22... | collective-permute-start | bytes 393224 | tf_op jit(solution)/shard_map/ppermute | solution.py:38
  34.5 12.2 %collective-permute-start.3 = (bf16[4,128,128]{2,1,0:T(8,128)(2,1)S(1)}, bf16[4,128,128]{2,1,0:T(8,128)(2,1)S(1)}, u32[]{:S(2)}, u32[]{:S(2)}) collective-permute-start(bf16[4,128,128]{2,1,0:T(8,128)(2,1)S(1)} %collective-permute-done.refs_2_), channel_id=1, source_target_pairs={{0,32},{32,64},{64,96},{96,128},{128,160},{160,192},{192,224},{224... | collective-permute-start | bytes 393224 | tf_op jit(solution)/shard_map/ppermute | solution.py:38

commit v7 on v6

--- a/solution.py
+++ b/solution.py
@@ -30,10 +30,12 @@
 )
 
 
-def shift_by_core(block, distances):
+def shift_by_core(block, distances, crossed=False):
     planes, cores = lax.axis_size("z"), lax.axis_size("c")
     route = [
-        (z * cores + c, (z + distances[c]) * cores + c) for c in range(cores) for z in range(planes - distances[c])
+        (z * cores + c, (z + distances[c]) * cores + (cores - 1 - c if crossed else c))
+        for c in range(cores)
+        for z in range(planes - distances[c])
     ]
     return lax.ppermute(block, ("z", "c"), route)
 
@@ -62,11 +64,11 @@
         own_ref, *pairs = refs[:3]
         old, refs = (), refs[3:]
         keys, values, firsts = [own_ref[2 * core]], [own_ref[2 * core + 1]], [side_first + core * BLK]
-        distances = (1 + core, 3 + 3 * core)
+        distances = (3 - core, 4 + 2 * core)
     else:
         pairs, old, refs = refs[:2], refs[2:4], refs[4:]
         keys, values, firsts = [], [], []
-        distances = (4 + 3 * core, 5 + 3 * core)
+        distances = (5 + 2 * core, 1 + 7 * core)
     for ref, distance in zip(pairs, distances):
         for n in range(PAIR):
             keys.append(ref[2 * n])
@@ -172,20 +174,23 @@
 
 
 def on_device(queries, keys, values, segments, out_weight):
-    plane, lane = lax.axis_index("z"), lax.axis_index(("y", "c"))
+    plane, core, lane = lax.axis_index("z"), lax.axis_index("c"), lax.axis_index(("y", "c"))
     where = jnp.stack([plane, lane]).astype(jnp.int32)
-    low = small(low_kernel, "low", (8, BLK), jnp.int32, where, segments.reshape(-1, BLK), smem=1)
     is_key = lax.broadcasted_iota(jnp.int32, (2, BLK, HD), 0) == 0
     own = lax.all_gather(jnp.where(is_key, keys[None], values[None]), "c", tiled=True)
-    from36 = shift_by_core(own, (3, 6))
-    from12 = shift_by_core(own, (1, 2))
+    come = shift_by_core(own, (3, 2))
     queries, _ = lax.optimization_barrier((queries, own))
     mine = lax.all_gather(queries, "c", tiled=True)
-    from36, from12, mine, low = lax.optimization_barrier((from36, from12, mine, low))
+    come, mine, segments = lax.optimization_barrier((come, mine, segments))
+    passed = shift_by_core(come, (3, 2), crossed=True)
+    low = small(low_kernel, "low", (8, BLK), jnp.int32, where, segments.reshape(-1, BLK), smem=1)
+    mine, low = lax.optimization_barrier((mine, low))
     other = lax.ppermute(mine, "y", [(0, 1), (1, 0)])
-    one, two = shift_by_core(from36, (1, 1)), shift_by_core(from36, (2, 2))
+    passed, low = lax.optimization_barrier((passed, low))
+    one = shift_by_core(passed, (1, 1))
+    two = shift_by_core(jnp.where(core == 0, own, passed), (1, 2))
     common = (where, mine, other, low)
-    state = attend(True, *common, own, from12, from36)
+    state = attend(True, *common, own, come, passed)
     partial = attend(False, *common, one, two, *state)
     parts = lax.all_to_all(partial, ("y", "c"), 0, 0, tiled=True)
     copies = small(combine_kernel, "combine", (HEADS, BLK, GROUP * HD), jnp.bfloat16, parts)

time: 85 us -> 82 us (0.965)
  the two profiles are of different devices: /device:TPU:384 before, /device:TPU:640 now
where the time goes in v7:
time: 82 us; the launch traced here: 81.7 us
  blocking collectives  39.6 us (48%)
  waiting for transfers between devices  17 us (21%)
  starting transfers between devices  14.2 us (17%)
  Pallas kernels  8.85 us (11%)
  local copies, waits for them, and re-layouts  1 us (1%)
  other arithmetic  0.95 us (1%)
    all_to_all x1, blocking collectives, on_device(): attended = lax.all_to_all(copies, 'h', 0, 0, tiled=True)  19.6 us
    ppermute x4, waiting for transfers between devices, shift_by_core(): return lax.ppermute(block, ('z', 'c'), route)  16.4 us
    all_to_all x1, blocking collectives, on_device(): parts = lax.all_to_all(partial, ('y', 'c'), 0, 0, tiled=True)  15.9 us
    ppermute x4, starting transfers between devices, shift_by_core(): return lax.ppermute(block, ('z', 'c'), route)  9.57 us
    pallas_call x2, Pallas kernels, attend(): pl.pallas_call(functools.partial(attend_kernel, near), out_shape=out, in_...  5.88 us
    ppermute x1, starting transfers between devices, on_device(): other = lax.ppermute(mine, 'y', [(0, 1), (1, 0)])  4.59 us
    pallas_call x3, Pallas kernels, small(): pl.pallas_call(kernel, out_shape=jax.ShapeDtypeStruct(shape, dtype), in_s...  2.97 us
    all_gather x1, blocking collectives, on_device(): mine = lax.all_gather(queries, 'c', tiled=True)  2.21 us
  transfers between devices with their start and end apart: 5, of which 5 were waited for; matrix products, arithmetic and copies ran while one was open for 0% of the time, Pallas kernels for 5%

profile of v7, /device:TPU:640, one launch (start us, length us, event | category | flops | bytes accessed | tf_op | source)
XLA Modules:
  0.0 81.7 jit_solution(12051905514932134604)
XLA Ops:
  0.0 0.9 %broadcast_select_fusion.1 = bf16[2,128,128]{2,1,0:T(8,128)(2,1)S(1)} fusion(pred[2]{0:T(512)(128)(4,1)S(1)} %iota_compare_fusion, bf16[128,128]{1,0:T(8,128)(2,1)} %param.7, bf16[128,128]{1,0:T(8,128)(2,1)} %param.6), kind=kLoop, calls=%fused_computation.1 | loop fusion | flops 32768 | bytes 131074 | tf_op jit(solution)/shard_map/jit(_where)/select_n | solution.py:180
  0.9 1.9 %all_gather.6.refs_0_ = bf16[4,128,128]{2,1,0:T(8,128)(2,1)S(1)} all-gather(bf16[2,128,128]{2,1,0:T(8,128)(2,1)S(1)} %broadcast_select_fusion.1), channel_id=1, replica_groups=mesh['z'=32,'y'=2,'c'=2,'h'=8] {'c'}, dimensions={0}, use_global_device_ids=true | all-gather | bytes 196608 | tf_op jit(solution)/shard_map/all_gather | solution.py:180
  2.7 3.8 %collective-permute-start = (bf16[4,128,128]{2,1,0:T(8,128)(2,1)S(1)}, bf16[4,128,128]{2,1,0:T(8,128)(2,1)S(1)}, u32[]{:S(2)}, u32[]{:S(2)}) collective-permute-start(bf16[4,128,128]{2,1,0:T(8,128)(2,1)S(1)} %all_gather.6.refs_0_), channel_id=1, source_target_pairs={{0,96},{32,128},{64,160},{96,192},{128,224},{160,256},{192,288},{2... | collective-permute-start | bytes 393224 | tf_op jit(solution)/shard_map/ppermute | solution.py:40
  6.6 2.2 %all_gather.7.mine_ref = bf16[256,512]{1,0:T(8,128)(2,1)S(1)} all-gather(bf16[128,512]{1,0:T(8,128)(2,1)} %param.5), channel_id=1, replica_groups=mesh['z'=32,'y'=2,'c'=2,'h'=8] {'c'}, dimensions={0}, use_global_device_ids=true | all-gather | bytes 393216 | tf_op jit(solution)/shard_map/all_gather | solution.py:183
  8.8 8.0 %collective-permute-done.refs_1_ = bf16[4,128,128]{2,1,0:T(8,128)(2,1)S(1)} collective-permute-done((bf16[4,128,128]{2,1,0:T(8,128)(2,1)S(1)}, bf16[4,128,128]{2,1,0:T(8,128)(2,1)S(1)}, u32[]{:S(2)}, u32[]{:S(2)}) %collective-permute-start) | collective-permute-done | bytes 131104 | tf_op jit(solution)/shard_map/ppermute | solution.py:40
  16.8 1.9 %collective-permute-start.2 = (bf16[4,128,128]{2,1,0:T(8,128)(2,1)S(1)}, bf16[4,128,128]{2,1,0:T(8,128)(2,1)S(1)}, u32[]{:S(2)}, u32[]{:S(2)}) collective-permute-start(bf16[4,128,128]{2,1,0:T(8,128)(2,1)S(1)} %collective-permute-done.refs_1_), channel_id=1, source_target_pairs={{0,104},{32,136},{64,168},{96,200},{128,232},{160,264},{192,296},{... | collective-permute-start | bytes 393224 | tf_op jit(solution)/shard_map/ppermute | solution.py:40
  18.8 0.0 copy-start
  18.8 0.1 pad_add_fusion.where_ref
  18.8 0.0 copy-start.1
  18.8 1.0 %copy-done.1 = s32[16384]{0:T(1024)S(1)} copy-done((s32[16384]{0:T(1024)S(1)}, s32[16384]{0:T(1024)}, u32[]{:S(2)}) %copy-start.1) | copy-done | bytes 65560
  19.8 0.7 low.1.low_ref
  20.5 4.6 %collective-permute-start.1 = (bf16[256,512]{1,0:T(8,128)(2,1)S(1)}, bf16[256,512]{1,0:T(8,128)(2,1)S(1)}, u32[]{:S(2)}, u32[]{:S(2)}) collective-permute-start(bf16[256,512]{1,0:T(8,128)(2,1)S(1)} %all_gather.7.mine_ref), channel_id=1, source_target_pairs={{0,16},{16,0},{1,17},{17,1},{2,18},{18,2},{3,19},{19,3},{4,20},{20... | collective-permute-start | bytes 786440 | tf_op jit(solution)/shard_map/ppermute | solution.py:188
  25.1 3.6 %collective-permute-done.2.refs_2_ = bf16[4,128,128]{2,1,0:T(8,128)(2,1)S(1)} collective-permute-done((bf16[4,128,128]{2,1,0:T(8,128)(2,1)S(1)}, bf16[4,128,128]{2,1,0:T(8,128)(2,1)S(1)}, u32[]{:S(2)}, u32[]{:S(2)}) %collective-permute-start.2) | collective-permute-done | bytes 131104 | tf_op jit(solution)/shard_map/ppermute | solution.py:40
  28.8 1.9 %collective-permute-start.4 = (bf16[4,128,128]{2,1,0:T(8,128)(2,1)S(1)}, bf16[4,128,128]{2,1,0:T(8,128)(2,1)S(1)}, u32[]{:S(2)}, u32[]{:S(2)}) collective-permute-start(bf16[4,128,128]{2,1,0:T(8,128)(2,1)S(1)} %broadcast_select_fusion), channel_id=1, source_target_pairs={{0,32},{32,64},{64,96},{96,128},{128,160},{160,192},{192,224},{224... | collective-permute-start | bytes 393224 | tf_op jit(solution)/shard_map/ppermute | solution.py:40
  30.7 1.9 %collective-permute-start.3 = (bf16[4,128,128]{2,1,0:T(8,128)(2,1)S(1)}, bf16[4,128,128]{2,1,0:T(8,128)(2,1)S(1)}, u32[]{:S(2)}, u32[]{:S(2)}) collective-permute-start(bf16[4,128,128]{2,1,0:T(8,128)(2,1)S(1)} %collective-permute-done.2.refs_2_), channel_id=1, source_target_pairs={{0,32},{32,64},{64,96},{96,128},{128,160},{160,192},{192,224},{224... | collective-permute-start | bytes 393224 | tf_op jit(solution)/shard_map/ppermute | solution.py:40
  32.6 0.6 collective-permute-done.1.other_ref
  33.2 3.2 %near.1 = (f32[4,128,512]{2,1,0:T(8,128)S(1)}, f32[4,8,512]{2,1,0:T(8,128)S(1)}) custom-call(s32[2]{0:T(128)S(1)} %pad_add_fusion.where_ref, bf16[256,512]{1,0:T(8,128)(2,1)S(1)} %all_gather.7.mine_ref, bf16[256,512]{1,0:T(8,128)(2,1)S(1)} %collective-permute-done.1.other_ref, s32[8,128]{1,0:T(8,128)S(1)} %low.1.low_ref, ...), custom_call_target="tpu_custom_call" | custom-call | flops 671088640 | bytes 3145728 | tf_op jit(solution)/shard_map/near/pallas_call | solution.py:124
  36.4 2.1 %collective-permute-done.4.refs_1_ = bf16[4,128,128]{2,1,0:T(8,128)(2,1)S(1)} collective-permute-done((bf16[4,128,128]{2,1,0:T(8,128)(2,1)S(1)}, bf16[4,128,128]{2,1,0:T(8,128)(2,1)S(1)}, u32[]{:S(2)}, u32[]{:S(2)}) %collective-permute-start.4) | collective-permute-done | bytes 131104 | tf_op jit(solution)/shard_map/ppermute | solution.py:40
  38.5 2.6 %collective-permute-done.3.refs_0_ = bf16[4,128,128]{2,1,0:T(8,128)(2,1)S(1)} collective-permute-done((bf16[4,128,128]{2,1,0:T(8,128)(2,1)S(1)}, bf16[4,128,128]{2,1,0:T(8,128)(2,1)S(1)}, u32[]{:S(2)}, u32[]{:S(2)}) %collective-permute-start.3) | collective-permute-done | bytes 131104 | tf_op jit(solution)/shard_map/ppermute | solution.py:40
  41.1 2.7 %far.1 = bf16[4,144,512]{2,1,0:T(8,128)(2,1)S(1)} custom-call(s32[2]{0:T(128)S(1)} %pad_add_fusion.where_ref, bf16[256,512]{1,0:T(8,128)(2,1)S(1)} %all_gather.7.mine_ref, bf16[256,512]{1,0:T(8,128)(2,1)S(1)} %collective-permute-done.1.other_ref, s32[8,128]{1,0:T(8,128)S(1)} %low.1.low_ref, bf16[4,128,128]{2,1,0:T(8,128)(2,1)S(1)} %collective-permute-done.3.refs_0_, ...), custom_call_target="tpu_custom_call" | custom-call | flops 536870912 | bytes 3145728 | tf_op jit(solution)/shard_map/far/pallas_call | solution.py:124
  43.8 15.9 %all_to_all.10.parts_ref = bf16[4,144,512]{2,1,0:T(8,128)(2,1)S(1)} all-to-all(bf16[4,144,512]{2,1,0:T(8,128)(2,1)S(1)} %far.1), channel_id=1, replica_groups=mesh['z'=32,'y'=2,'c'=2,'h'=8] {'y','c'}, dimensions={0} | all-to-all | bytes 1179648 | tf_op jit(solution)/shard_map/all_to_all | solution.py:195
  59.8 0.3 combine.1
  60.1 19.6 %all_to_all.11.rows_ref = bf16[8,128,512]{2,1,0:T(8,128)(2,1)S(1)} all-to-all(bf16[8,128,512]{2,1,0:T(8,128)(2,1)S(1)} %combine.1), channel_id=1, replica_groups=mesh['z'=32,'y'=2,'c'=2,'h'=8] {'h'}, dimensions={0} | all-to-all | bytes 2097152 | tf_op jit(solution)/shard_map/all_to_all | solution.py:197
  79.7 0.0 copy-done
  79.7 2.0 %project.1 = bf16[128,1024]{1,0:T(8,128)(2,1)} custom-call(bf16[8,128,512]{2,1,0:T(8,128)(2,1)S(1)} %all_to_all.11.rows_ref, bf16[4096,1024]{1,0:T(8,128)(2,1)S(1)} %copy-done), custom_call_target="tpu_custom_call" | custom-call | flops 1048576 | bytes 524288 | tf_op jit(solution)/shard_map/project/pallas_call | solution.py:165
  (2 shorter events, 0.0 us)
Async XLA Ops:
  2.7 14.1 %collective-permute-start = (bf16[4,128,128]{2,1,0:T(8,128)(2,1)S(1)}, bf16[4,128,128]{2,1,0:T(8,128)(2,1)S(1)}, u32[]{:S(2)}, u32[]{:S(2)}) collective-permute-start(bf16[4,128,128]{2,1,0:T(8,128)(2,1)S(1)} %all_gather.6.refs_0_), channel_id=1, source_target_pairs={{0,96},{32,128},{64,160},{96,192},{128,224},{160,256},{192,288},{2... | collective-permute-start | bytes 393224 | tf_op jit(solution)/shard_map/ppermute | solution.py:40
  16.8 11.9 %collective-permute-start.2 = (bf16[4,128,128]{2,1,0:T(8,128)(2,1)S(1)}, bf16[4,128,128]{2,1,0:T(8,128)(2,1)S(1)}, u32[]{:S(2)}, u32[]{:S(2)}) collective-permute-start(bf16[4,128,128]{2,1,0:T(8,128)(2,1)S(1)} %collective-permute-done.refs_1_), channel_id=1, source_target_pairs={{0,104},{32,136},{64,168},{96,200},{128,232},{160,264},{192,296},{... | collective-permute-start | bytes 393224 | tf_op jit(solution)/shard_map/ppermute | solution.py:40
  18.8 60.9 %copy-start = (bf16[4096,1024]{1,0:T(8,128)(2,1)S(1)}, bf16[4096,1024]{1,0:T(8,128)(2,1)}, u32[]{:S(2)}) copy-start(bf16[4096,1024]{1,0:T(8,128)(2,1)} %weight_ref.1) | copy-start | bytes 25165828
  18.8 1.0 %copy-start.1 = (s32[16384]{0:T(1024)S(1)}, s32[16384]{0:T(1024)}, u32[]{:S(2)}) copy-start(s32[16384]{0:T(1024)} %param.8) | copy-start | bytes 196612
  20.5 12.7 %collective-permute-start.1 = (bf16[256,512]{1,0:T(8,128)(2,1)S(1)}, bf16[256,512]{1,0:T(8,128)(2,1)S(1)}, u32[]{:S(2)}, u32[]{:S(2)}) collective-permute-start(bf16[256,512]{1,0:T(8,128)(2,1)S(1)} %all_gather.7.mine_ref), channel_id=1, source_target_pairs={{0,16},{16,0},{1,17},{17,1},{2,18},{18,2},{3,19},{19,3},{4,20},{20... | collective-permute-start | bytes 786440 | tf_op jit(solution)/shard_map/ppermute | solution.py:188
  28.8 9.8 %collective-permute-start.4 = (bf16[4,128,128]{2,1,0:T(8,128)(2,1)S(1)}, bf16[4,128,128]{2,1,0:T(8,128)(2,1)S(1)}, u32[]{:S(2)}, u32[]{:S(2)}) collective-permute-start(bf16[4,128,128]{2,1,0:T(8,128)(2,1)S(1)} %broadcast_select_fusion), channel_id=1, source_target_pairs={{0,32},{32,64},{64,96},{96,128},{128,160},{160,192},{192,224},{224... | collective-permute-start | bytes 393224 | tf_op jit(solution)/shard_map/ppermute | solution.py:40
  30.7 10.4 %collective-permute-start.3 = (bf16[4,128,128]{2,1,0:T(8,128)(2,1)S(1)}, bf16[4,128,128]{2,1,0:T(8,128)(2,1)S(1)}, u32[]{:S(2)}, u32[]{:S(2)}) collective-permute-start(bf16[4,128,128]{2,1,0:T(8,128)(2,1)S(1)} %collective-permute-done.2.refs_2_), channel_id=1, source_target_pairs={{0,32},{32,64},{64,96},{96,128},{128,160},{160,192},{192,224},{224... | collective-permute-start | bytes 393224 | tf_op jit(solution)/shard_map/ppermute | solution.py:40

commit v8 on v6

--- a/solution.py
+++ b/solution.py
@@ -61,16 +61,17 @@
     if near:
         own_ref, *pairs = refs[:3]
         old, refs = (), refs[3:]
+        pairs = [(ref, 0) for ref in pairs]
         keys, values, firsts = [own_ref[2 * core]], [own_ref[2 * core + 1]], [side_first + core * BLK]
-        distances = (1 + core, 3 + 3 * core)
+        distances = (1 + 4 * core, 3 + 4 * core)
     else:
-        pairs, old, refs = refs[:2], refs[2:4], refs[4:]
+        pairs, old, refs = [(refs[0], 0), (refs[0], 2 * PAIR)], refs[1:3], refs[3:]
         keys, values, firsts = [], [], []
-        distances = (4 + 3 * core, 5 + 3 * core)
-    for ref, distance in zip(pairs, distances):
+        distances = (2 + 4 * core, 4 + 4 * core)
+    for (ref, at), distance in zip(pairs, distances):
         for n in range(PAIR):
-            keys.append(ref[2 * n])
-            values.append(ref[2 * n + 1])
+            keys.append(ref[at + 2 * n])
+            values.append(ref[at + 2 * n + 1])
             firsts.append(side_first + n * BLK - distance * PLANE)
     keys = jnp.concatenate(keys, axis=0)
     values_t = jnp.concatenate(values, axis=0).astype(jnp.float32).T.astype(jnp.bfloat16)
@@ -174,19 +175,21 @@
 def on_device(queries, keys, values, segments, out_weight):
     plane, lane = lax.axis_index("z"), lax.axis_index(("y", "c"))
     where = jnp.stack([plane, lane]).astype(jnp.int32)
-    low = small(low_kernel, "low", (8, BLK), jnp.int32, where, segments.reshape(-1, BLK), smem=1)
     is_key = lax.broadcasted_iota(jnp.int32, (2, BLK, HD), 0) == 0
     own = lax.all_gather(jnp.where(is_key, keys[None], values[None]), "c", tiled=True)
-    from36 = shift_by_core(own, (3, 6))
-    from12 = shift_by_core(own, (1, 2))
+    come = shift_by_core(own, (1, 5))
     queries, _ = lax.optimization_barrier((queries, own))
     mine = lax.all_gather(queries, "c", tiled=True)
-    from36, from12, mine, low = lax.optimization_barrier((from36, from12, mine, low))
+    come, mine, segments = lax.optimization_barrier((come, mine, segments))
+    passed = shift_by_core(come, (2, 2))
+    low = small(low_kernel, "low", (8, BLK), jnp.int32, where, segments.reshape(-1, BLK), smem=1)
+    mine, low = lax.optimization_barrier((mine, low))
     other = lax.ppermute(mine, "y", [(0, 1), (1, 0)])
-    one, two = shift_by_core(from36, (1, 1)), shift_by_core(from36, (2, 2))
+    passed, low = lax.optimization_barrier((passed, low))
+    last = shift_by_core(jnp.concatenate([come, passed], axis=0), (1, 1))
     common = (where, mine, other, low)
-    state = attend(True, *common, own, from12, from36)
-    partial = attend(False, *common, one, two, *state)
+    state = attend(True, *common, own, come, passed)
+    partial = attend(False, *common, last, *state)
     parts = lax.all_to_all(partial, ("y", "c"), 0, 0, tiled=True)
     copies = small(combine_kernel, "combine", (HEADS, BLK, GROUP * HD), jnp.bfloat16, parts)
     attended = lax.all_to_all(copies, "h", 0, 0, tiled=True)

time: 85 us -> 80.1 us (0.942)
  the two profiles are of different devices: /device:TPU:384 before, /device:TPU:352 now
where the time goes in v8:
time: 80.1 us; the launch traced here: 79.8 us
  blocking collectives  50.2 us (63%)
  starting transfers between devices  17.9 us (22%)
  Pallas kernels  8.85 us (11%)
  local copies, waits for them, and re-layouts  1 us (1%)
  other arithmetic  0.96 us (1%)
  waiting for transfers between devices  0.83 us (1%)
    all_to_all x1, blocking collectives, on_device(): parts = lax.all_to_all(partial, ('y', 'c'), 0, 0, tiled=True)  20.5 us
    all_to_all x1, blocking collectives, on_device(): attended = lax.all_to_all(copies, 'h', 0, 0, tiled=True)  19.5 us
    ppermute x3, starting transfers between devices, shift_by_core(): return lax.ppermute(block, ('z', 'c'), route)  12.7 us
    all_gather x1, blocking collectives, on_device(): mine = lax.all_gather(queries, 'c', tiled=True)  8.35 us
    pallas_call x2, Pallas kernels, attend(): pl.pallas_call(functools.partial(attend_kernel, near), out_shape=out, in_...  5.88 us
    ppermute x1, starting transfers between devices, on_device(): other = lax.ppermute(mine, 'y', [(0, 1), (1, 0)])  5.23 us
    pallas_call x3, Pallas kernels, small(): pl.pallas_call(kernel, out_shape=jax.ShapeDtypeStruct(shape, dtype), in_s...  2.97 us
    all_gather x1, blocking collectives, on_device(): lax.all_gather(jnp.where(is_key, keys[None], values[None]), 'c', tiled=True)  1.89 us
  transfers between devices with their start and end apart: 4, of which 2 were waited for; matrix products, arithmetic and copies ran while one was open for 0% of the time, Pallas kernels for 5%

profile of v8, /device:TPU:352, one launch (start us, length us, event | category | flops | bytes accessed | tf_op | source)
XLA Modules:
  0.0 79.8 jit_solution(12827070859133491506)
XLA Ops:
  0.0 0.9 %broadcast_select_fusion = bf16[2,128,128]{2,1,0:T(8,128)(2,1)S(1)} fusion(pred[2]{0:T(512)(128)(4,1)S(1)} %iota_compare_fusion, bf16[128,128]{1,0:T(8,128)(2,1)} %param.7, bf16[128,128]{1,0:T(8,128)(2,1)} %param.6), kind=kLoop, calls=%fused_computation.1 | loop fusion | flops 32768 | bytes 131074 | tf_op jit(solution)/shard_map/jit(_where)/select_n | solution.py:179
  0.9 1.9 %all_gather.6.refs_0_ = bf16[4,128,128]{2,1,0:T(8,128)(2,1)S(1)} all-gather(bf16[2,128,128]{2,1,0:T(8,128)(2,1)S(1)} %broadcast_select_fusion), channel_id=1, replica_groups=mesh['z'=32,'y'=2,'c'=2,'h'=8] {'c'}, dimensions={0}, use_global_device_ids=true | all-gather | bytes 196608 | tf_op jit(solution)/shard_map/all_gather | solution.py:179
  2.7 5.0 %collective-permute-start = (bf16[4,128,128]{2,1,0:T(8,128)(2,1)S(1)}, bf16[4,128,128]{2,1,0:T(8,128)(2,1)S(1)}, u32[]{:S(2)}, u32[]{:S(2)}) collective-permute-start(bf16[4,128,128]{2,1,0:T(8,128)(2,1)S(1)} %all_gather.6.refs_0_), channel_id=1, source_target_pairs={{0,32},{32,64},{64,96},{96,128},{128,160},{160,192},{192,224},{224... | collective-permute-start | bytes 393224 | tf_op jit(solution)/shard_map/ppermute | solution.py:38
  7.8 8.3 %all_gather.7.mine_ref = bf16[256,512]{1,0:T(8,128)(2,1)S(1)} all-gather(bf16[128,512]{1,0:T(8,128)(2,1)} %param.5), channel_id=1, replica_groups=mesh['z'=32,'y'=2,'c'=2,'h'=8] {'c'}, dimensions={0}, use_global_device_ids=true | all-gather | bytes 393216 | tf_op jit(solution)/shard_map/all_gather | solution.py:182
  16.1 0.0 collective-permute-done.refs_1_
  16.1 3.4 %collective-permute-start.2 = (bf16[4,128,128]{2,1,0:T(8,128)(2,1)S(1)}, bf16[4,128,128]{2,1,0:T(8,128)(2,1)S(1)}, u32[]{:S(2)}, u32[]{:S(2)}) collective-permute-start(bf16[4,128,128]{2,1,0:T(8,128)(2,1)S(1)} %collective-permute-done.refs_1_), channel_id=1, source_target_pairs={{0,64},{32,96},{64,128},{96,160},{128,192},{160,224},{192,256},{22... | collective-permute-start | bytes 393224 | tf_op jit(solution)/shard_map/ppermute | solution.py:38
  19.5 0.0 copy-start
  19.5 0.1 pad_add_fusion.where_ref
  19.6 0.0 copy-start.1
  19.6 1.0 %copy-done.1 = s32[16384]{0:T(1024)S(1)} copy-done((s32[16384]{0:T(1024)S(1)}, s32[16384]{0:T(1024)}, u32[]{:S(2)}) %copy-start.1) | copy-done | bytes 65560
  20.6 0.7 low.1.low_ref
  21.3 5.2 %collective-permute-start.1 = (bf16[256,512]{1,0:T(8,128)(2,1)S(1)}, bf16[256,512]{1,0:T(8,128)(2,1)S(1)}, u32[]{:S(2)}, u32[]{:S(2)}) collective-permute-start(bf16[256,512]{1,0:T(8,128)(2,1)S(1)} %all_gather.7.mine_ref), channel_id=1, source_target_pairs={{0,16},{16,0},{1,17},{17,1},{2,18},{18,2},{3,19},{19,3},{4,20},{20... | collective-permute-start | bytes 786440 | tf_op jit(solution)/shard_map/ppermute | solution.py:187
  26.6 0.0 collective-permute-done.2.refs_2_
  26.6 4.3 %collective-permute-start.3 = (bf16[8,128,128]{2,1,0:T(8,128)(2,1)S(1)}, bf16[8,128,128]{2,1,0:T(8,128)(2,1)S(1)}, u32[]{:S(2)}, u32[]{:S(2)}) collective-permute-start(bf16[8,128,128]{2,1,0:T(8,128)(2,1)S(1)} %pad_maximum_fusion), channel_id=1, source_target_pairs={{0,32},{32,64},{64,96},{96,128},{128,160},{160,192},{192,224},{224... | collective-permute-start | bytes 786440 | tf_op jit(solution)/shard_map/ppermute | solution.py:38
  30.9 0.3 collective-permute-done.1.other_ref
  31.2 3.2 %near.1 = (f32[4,128,512]{2,1,0:T(8,128)S(1)}, f32[4,8,512]{2,1,0:T(8,128)S(1)}) custom-call(s32[2]{0:T(128)S(1)} %pad_add_fusion.where_ref, bf16[256,512]{1,0:T(8,128)(2,1)S(1)} %all_gather.7.mine_ref, bf16[256,512]{1,0:T(8,128)(2,1)S(1)} %collective-permute-done.1.other_ref, s32[8,128]{1,0:T(8,128)S(1)} %low.1.low_ref, ...), custom_call_target="tpu_custom_call" | custom-call | flops 671088640 | bytes 3145728 | tf_op jit(solution)/shard_map/near/pallas_call | solution.py:123
  34.4 0.5 collective-permute-done.3.refs_0_
  34.9 2.7 %far.1 = bf16[4,144,512]{2,1,0:T(8,128)(2,1)S(1)} custom-call(s32[2]{0:T(128)S(1)} %pad_add_fusion.where_ref, bf16[256,512]{1,0:T(8,128)(2,1)S(1)} %all_gather.7.mine_ref, bf16[256,512]{1,0:T(8,128)(2,1)S(1)} %collective-permute-done.1.other_ref, s32[8,128]{1,0:T(8,128)S(1)} %low.1.low_ref, bf16[8,128,128]{2,1,0:T(8,128)(2,1)S(1)} %collective-permute-done.3.refs_0_, ...), custom_call_target="tpu_custom_call" | custom-call | flops 536870912 | bytes 3145728 | tf_op jit(solution)/shard_map/far/pallas_call | solution.py:123
  37.6 20.5 %all_to_all.10.parts_ref = bf16[4,144,512]{2,1,0:T(8,128)(2,1)S(1)} all-to-all(bf16[4,144,512]{2,1,0:T(8,128)(2,1)S(1)} %far.1), channel_id=1, replica_groups=mesh['z'=32,'y'=2,'c'=2,'h'=8] {'y','c'}, dimensions={0} | all-to-all | bytes 1179648 | tf_op jit(solution)/shard_map/all_to_all | solution.py:193
  58.1 0.3 combine.1
  58.4 19.5 %all_to_all.11.rows_ref = bf16[8,128,512]{2,1,0:T(8,128)(2,1)S(1)} all-to-all(bf16[8,128,512]{2,1,0:T(8,128)(2,1)S(1)} %combine.1), channel_id=1, replica_groups=mesh['z'=32,'y'=2,'c'=2,'h'=8] {'h'}, dimensions={0} | all-to-all | bytes 2097152 | tf_op jit(solution)/shard_map/all_to_all | solution.py:195
  77.8 0.0 copy-done
  77.8 2.0 %project.1 = bf16[128,1024]{1,0:T(8,128)(2,1)} custom-call(bf16[8,128,512]{2,1,0:T(8,128)(2,1)S(1)} %all_to_all.11.rows_ref, bf16[4096,1024]{1,0:T(8,128)(2,1)S(1)} %copy-done), custom_call_target="tpu_custom_call" | custom-call | flops 1048576 | bytes 524288 | tf_op jit(solution)/shard_map/project/pallas_call | solution.py:164
  (2 shorter events, 0.0 us)
Async XLA Ops:
  2.7 13.4 %collective-permute-start = (bf16[4,128,128]{2,1,0:T(8,128)(2,1)S(1)}, bf16[4,128,128]{2,1,0:T(8,128)(2,1)S(1)}, u32[]{:S(2)}, u32[]{:S(2)}) collective-permute-start(bf16[4,128,128]{2,1,0:T(8,128)(2,1)S(1)} %all_gather.6.refs_0_), channel_id=1, source_target_pairs={{0,32},{32,64},{64,96},{96,128},{128,160},{160,192},{192,224},{224... | collective-permute-start | bytes 393224 | tf_op jit(solution)/shard_map/ppermute | solution.py:38
  16.1 10.4 %collective-permute-start.2 = (bf16[4,128,128]{2,1,0:T(8,128)(2,1)S(1)}, bf16[4,128,128]{2,1,0:T(8,128)(2,1)S(1)}, u32[]{:S(2)}, u32[]{:S(2)}) collective-permute-start(bf16[4,128,128]{2,1,0:T(8,128)(2,1)S(1)} %collective-permute-done.refs_1_), channel_id=1, source_target_pairs={{0,64},{32,96},{64,128},{96,160},{128,192},{160,224},{192,256},{22... | collective-permute-start | bytes 393224 | tf_op jit(solution)/shard_map/ppermute | solution.py:38
  19.5 58.3 %copy-start = (bf16[4096,1024]{1,0:T(8,128)(2,1)S(1)}, bf16[4096,1024]{1,0:T(8,128)(2,1)}, u32[]{:S(2)}) copy-start(bf16[4096,1024]{1,0:T(8,128)(2,1)} %weight_ref.1) | copy-start | bytes 25165828
  19.6 1.0 %copy-start.1 = (s32[16384]{0:T(1024)S(1)}, s32[16384]{0:T(1024)}, u32[]{:S(2)}) copy-start(s32[16384]{0:T(1024)} %param.8) | copy-start | bytes 196612
  21.3 9.9 %collective-permute-start.1 = (bf16[256,512]{1,0:T(8,128)(2,1)S(1)}, bf16[256,512]{1,0:T(8,128)(2,1)S(1)}, u32[]{:S(2)}, u32[]{:S(2)}) collective-permute-start(bf16[256,512]{1,0:T(8,128)(2,1)S(1)} %all_gather.7.mine_ref), channel_id=1, source_target_pairs={{0,16},{16,0},{1,17},{17,1},{2,18},{18,2},{3,19},{19,3},{4,20},{20... | collective-permute-start | bytes 786440 | tf_op jit(solution)/shard_map/ppermute | solution.py:187
  26.6 8.3 %collective-permute-start.3 = (bf16[8,128,128]{2,1,0:T(8,128)(2,1)S(1)}, bf16[8,128,128]{2,1,0:T(8,128)(2,1)S(1)}, u32[]{:S(2)}, u32[]{:S(2)}) collective-permute-start(bf16[8,128,128]{2,1,0:T(8,128)(2,1)S(1)} %pad_maximum_fusion), channel_id=1, source_target_pairs={{0,32},{32,64},{64,96},{96,128},{128,160},{160,192},{192,224},{224... | collective-permute-start | bytes 786440 | tf_op jit(solution)/shard_map/ppermute | solution.py:38

commit v9 on v8

--- a/solution.py
+++ b/solution.py
@@ -20,6 +20,7 @@
 SEGMENT_VALUES = 6
 SCALE2 = float(HD**-0.5 * 1.4426950408889634)
 MASKED = -1e30
+AHEAD = 2
 VMEM = 24 * 1024 * 1024
 PARAMS = pltpu.CompilerParams(vmem_limit_bytes=VMEM)
 SMEM = pl.BlockSpec(memory_space=pltpu.SMEM)
@@ -75,21 +76,30 @@
             firsts.append(side_first + n * BLK - distance * PLANE)
     keys = jnp.concatenate(keys, axis=0)
     values_t = jnp.concatenate(values, axis=0).astype(jnp.float32).T.astype(jnp.bfloat16)
-    sub = lax.broadcasted_iota(jnp.int32, (BLK, ROWS), 0)
-    token = lax.broadcasted_iota(jnp.int32, (1, ROWS), 1) % BLK
-    for index in range(LANES):
+    sub = lax.broadcasted_iota(jnp.int32, (BLK, BLK), 0)
+    token = lax.broadcasted_iota(jnp.int32, (1, BLK), 1)
+
+    def scores_of(index):
         query_ref, of_core = (mine_ref, other_ref)[index // PAIR], index % PAIR
-        block = of_core + ((lane - core) if index < PAIR else (PAIR - lane + core))
         rows = slice(of_core * BLK, (of_core + 1) * BLK)
         queries = jnp.concatenate([query_ref[rows, g * HD : (g + 1) * HD] for g in range(GROUP)], axis=0)
-        scores = lax.dot_general(keys, queries, (((1,), (1,)), ((), ())), preferred_element_type=jnp.float32)
-        low = jnp.concatenate([low_ref[pl.ds(block, 1), :]] * GROUP, axis=1)
+        return lax.dot_general(keys, queries, (((1,), (1,)), ((), ())), preferred_element_type=jnp.float32)
+
+    ahead = [scores_of(index) for index in range(AHEAD)]
+    for index in range(LANES):
+        if index + AHEAD < LANES:
+            ahead.append(scores_of(index + AHEAD))
+        scores = ahead[index]
+        block = index % PAIR + ((lane - core) if index < PAIR else (PAIR - lane + core))
+        low = low_ref[pl.ds(block, 1), :]
         parts = []
         for n, key_first in enumerate(firsts):
             allowed = sub >= low - key_first
             if near and n == 0:
                 allowed = allowed & (sub <= plane_first + block * BLK + token - key_first)
-            parts.append(jnp.where(allowed, scores[n * BLK : (n + 1) * BLK] * SCALE2, MASKED))
+            bias = jnp.where(allowed, 0.0, MASKED)
+            bias = jnp.concatenate([bias] * GROUP, axis=1)
+            parts.append(scores[n * BLK : (n + 1) * BLK] * SCALE2 + bias)
         top = jnp.max(functools.reduce(jnp.maximum, parts), axis=0, keepdims=True)
         if not first:
             old_top = old[1][index, 0:1]

time: 80.1 us -> 79.1 us (0.988)
  Pallas kernels: 8.85 us -> 7.84 us
    pallas_call x2, Pallas kernels: 5.88 us -> 4.87 us  [attend(): pl.pallas_call(functools.partial(attend_kernel, near), out_shape=out, in_...]
  transfers between devices with their start and end apart: 4 -> 4, of which waited for: 2 -> 2; matrix products, arithmetic and copies ran while one was open for 0% -> 0% of each run, Pallas kernels for 5% -> 4%
where the time goes in v9:
time: 79.1 us; the launch traced here: 78.8 us
  blocking collectives  49.6 us (63%)
  starting transfers between devices  17.9 us (23%)
  Pallas kernels  7.84 us (10%)
  waiting for transfers between devices  1.46 us (2%)
  local copies, waits for them, and re-layouts  1 us (1%)
  other arithmetic  0.96 us (1%)
    all_to_all x1, blocking collectives, on_device(): parts = lax.all_to_all(partial, ('y', 'c'), 0, 0, tiled=True)  19.9 us
    all_to_all x1, blocking collectives, on_device(): attended = lax.all_to_all(copies, 'h', 0, 0, tiled=True)  19.5 us
    ppermute x3, starting transfers between devices, shift_by_core(): return lax.ppermute(block, ('z', 'c'), route)  12.7 us
    all_gather x1, blocking collectives, on_device(): mine = lax.all_gather(queries, 'c', tiled=True)  8.35 us
    ppermute x1, starting transfers between devices, on_device(): other = lax.ppermute(mine, 'y', [(0, 1), (1, 0)])  5.23 us
    pallas_call x2, Pallas kernels, attend(): pl.pallas_call(functools.partial(attend_kernel, near), out_shape=out, in_...  4.87 us
    pallas_call x3, Pallas kernels, small(): pl.pallas_call(kernel, out_shape=jax.ShapeDtypeStruct(shape, dtype), in_s...  2.97 us
    all_gather x1, blocking collectives, on_device(): lax.all_gather(jnp.where(is_key, keys[None], values[None]), 'c', tiled=True)  1.89 us
  transfers between devices with their start and end apart: 4, of which 2 were waited for; matrix products, arithmetic and copies ran while one was open for 0% of the time, Pallas kernels for 4%

profile of v9, /device:TPU:352, one launch (start us, length us, event | category | flops | bytes accessed | tf_op | source)
XLA Modules:
  0.0 78.8 jit_solution(15297989013325533537)
XLA Ops:
  0.0 0.9 %broadcast_select_fusion = bf16[2,128,128]{2,1,0:T(8,128)(2,1)S(1)} fusion(pred[2]{0:T(512)(128)(4,1)S(1)} %iota_compare_fusion, bf16[128,128]{1,0:T(8,128)(2,1)} %param.7, bf16[128,128]{1,0:T(8,128)(2,1)} %param.6), kind=kLoop, calls=%fused_computation.1 | loop fusion | flops 32768 | bytes 131074 | tf_op jit(solution)/shard_map/jit(_where)/select_n | solution.py:189
  0.9 1.9 %all_gather.6.refs_0_ = bf16[4,128,128]{2,1,0:T(8,128)(2,1)S(1)} all-gather(bf16[2,128,128]{2,1,0:T(8,128)(2,1)S(1)} %broadcast_select_fusion), channel_id=1, replica_groups=mesh['z'=32,'y'=2,'c'=2,'h'=8] {'c'}, dimensions={0}, use_global_device_ids=true | all-gather | bytes 196608 | tf_op jit(solution)/shard_map/all_gather | solution.py:189
  2.7 5.0 %collective-permute-start = (bf16[4,128,128]{2,1,0:T(8,128)(2,1)S(1)}, bf16[4,128,128]{2,1,0:T(8,128)(2,1)S(1)}, u32[]{:S(2)}, u32[]{:S(2)}) collective-permute-start(bf16[4,128,128]{2,1,0:T(8,128)(2,1)S(1)} %all_gather.6.refs_0_), channel_id=1, source_target_pairs={{0,32},{32,64},{64,96},{96,128},{128,160},{160,192},{192,224},{224... | collective-permute-start | bytes 393224 | tf_op jit(solution)/shard_map/ppermute | solution.py:39
  7.8 8.3 %all_gather.7.mine_ref = bf16[256,512]{1,0:T(8,128)(2,1)S(1)} all-gather(bf16[128,512]{1,0:T(8,128)(2,1)} %param.5), channel_id=1, replica_groups=mesh['z'=32,'y'=2,'c'=2,'h'=8] {'c'}, dimensions={0}, use_global_device_ids=true | all-gather | bytes 393216 | tf_op jit(solution)/shard_map/all_gather | solution.py:192
  16.1 0.0 collective-permute-done.refs_1_
  16.1 3.4 %collective-permute-start.2 = (bf16[4,128,128]{2,1,0:T(8,128)(2,1)S(1)}, bf16[4,128,128]{2,1,0:T(8,128)(2,1)S(1)}, u32[]{:S(2)}, u32[]{:S(2)}) collective-permute-start(bf16[4,128,128]{2,1,0:T(8,128)(2,1)S(1)} %collective-permute-done.refs_1_), channel_id=1, source_target_pairs={{0,64},{32,96},{64,128},{96,160},{128,192},{160,224},{192,256},{22... | collective-permute-start | bytes 393224 | tf_op jit(solution)/shard_map/ppermute | solution.py:39
  19.5 0.0 copy-start
  19.5 0.1 pad_add_fusion.where_ref
  19.6 0.0 copy-start.1
  19.6 1.0 %copy-done.1 = s32[16384]{0:T(1024)S(1)} copy-done((s32[16384]{0:T(1024)S(1)}, s32[16384]{0:T(1024)}, u32[]{:S(2)}) %copy-start.1) | copy-done | bytes 65560
  20.6 0.7 low.1.low_ref
  21.3 5.2 %collective-permute-start.1 = (bf16[256,512]{1,0:T(8,128)(2,1)S(1)}, bf16[256,512]{1,0:T(8,128)(2,1)S(1)}, u32[]{:S(2)}, u32[]{:S(2)}) collective-permute-start(bf16[256,512]{1,0:T(8,128)(2,1)S(1)} %all_gather.7.mine_ref), channel_id=1, source_target_pairs={{0,16},{16,0},{1,17},{17,1},{2,18},{18,2},{3,19},{19,3},{4,20},{20... | collective-permute-start | bytes 786440 | tf_op jit(solution)/shard_map/ppermute | solution.py:197
  26.6 0.0 collective-permute-done.2.refs_2_
  26.6 4.3 %collective-permute-start.3 = (bf16[8,128,128]{2,1,0:T(8,128)(2,1)S(1)}, bf16[8,128,128]{2,1,0:T(8,128)(2,1)S(1)}, u32[]{:S(2)}, u32[]{:S(2)}) collective-permute-start(bf16[8,128,128]{2,1,0:T(8,128)(2,1)S(1)} %pad_maximum_fusion), channel_id=1, source_target_pairs={{0,32},{32,64},{64,96},{96,128},{128,160},{160,192},{192,224},{224... | collective-permute-start | bytes 786440 | tf_op jit(solution)/shard_map/ppermute | solution.py:39
  30.9 0.3 collective-permute-done.1.other_ref
  31.2 2.5 %near.1 = (f32[4,128,512]{2,1,0:T(8,128)S(1)}, f32[4,8,512]{2,1,0:T(8,128)S(1)}) custom-call(s32[2]{0:T(128)S(1)} %pad_add_fusion.where_ref, bf16[256,512]{1,0:T(8,128)(2,1)S(1)} %all_gather.7.mine_ref, bf16[256,512]{1,0:T(8,128)(2,1)S(1)} %collective-permute-done.1.other_ref, s32[8,128]{1,0:T(8,128)S(1)} %low.1.low_ref, ...), custom_call_target="tpu_custom_call" | custom-call | flops 671088640 | bytes 3145728 | tf_op jit(solution)/shard_map/near/pallas_call | solution.py:133
  33.8 1.1 %collective-permute-done.3.refs_0_ = bf16[8,128,128]{2,1,0:T(8,128)(2,1)S(1)} collective-permute-done((bf16[8,128,128]{2,1,0:T(8,128)(2,1)S(1)}, bf16[8,128,128]{2,1,0:T(8,128)(2,1)S(1)}, u32[]{:S(2)}, u32[]{:S(2)}) %collective-permute-start.3) | collective-permute-done | bytes 262176 | tf_op jit(solution)/shard_map/ppermute | solution.py:39
  34.9 2.3 %far.1 = bf16[4,144,512]{2,1,0:T(8,128)(2,1)S(1)} custom-call(s32[2]{0:T(128)S(1)} %pad_add_fusion.where_ref, bf16[256,512]{1,0:T(8,128)(2,1)S(1)} %all_gather.7.mine_ref, bf16[256,512]{1,0:T(8,128)(2,1)S(1)} %collective-permute-done.1.other_ref, s32[8,128]{1,0:T(8,128)S(1)} %low.1.low_ref, bf16[8,128,128]{2,1,0:T(8,128)(2,1)S(1)} %collective-permute-done.3.refs_0_, ...), custom_call_target="tpu_custom_call" | custom-call | flops 536870912 | bytes 3145728 | tf_op jit(solution)/shard_map/far/pallas_call | solution.py:133
  37.2 19.9 %all_to_all.10.parts_ref = bf16[4,144,512]{2,1,0:T(8,128)(2,1)S(1)} all-to-all(bf16[4,144,512]{2,1,0:T(8,128)(2,1)S(1)} %far.1), channel_id=1, replica_groups=mesh['z'=32,'y'=2,'c'=2,'h'=8] {'y','c'}, dimensions={0} | all-to-all | bytes 1179648 | tf_op jit(solution)/shard_map/all_to_all | solution.py:203
  57.1 0.3 combine.1
  57.4 19.5 %all_to_all.11.rows_ref = bf16[8,128,512]{2,1,0:T(8,128)(2,1)S(1)} all-to-all(bf16[8,128,512]{2,1,0:T(8,128)(2,1)S(1)} %combine.1), channel_id=1, replica_groups=mesh['z'=32,'y'=2,'c'=2,'h'=8] {'h'}, dimensions={0} | all-to-all | bytes 2097152 | tf_op jit(solution)/shard_map/all_to_all | solution.py:205
  76.8 0.0 copy-done
  76.8 2.0 %project.1 = bf16[128,1024]{1,0:T(8,128)(2,1)} custom-call(bf16[8,128,512]{2,1,0:T(8,128)(2,1)S(1)} %all_to_all.11.rows_ref, bf16[4096,1024]{1,0:T(8,128)(2,1)S(1)} %copy-done), custom_call_target="tpu_custom_call" | custom-call | flops 1048576 | bytes 524288 | tf_op jit(solution)/shard_map/project/pallas_call | solution.py:174
  (2 shorter events, 0.0 us)
Async XLA Ops:
  2.7 13.4 %collective-permute-start = (bf16[4,128,128]{2,1,0:T(8,128)(2,1)S(1)}, bf16[4,128,128]{2,1,0:T(8,128)(2,1)S(1)}, u32[]{:S(2)}, u32[]{:S(2)}) collective-permute-start(bf16[4,128,128]{2,1,0:T(8,128)(2,1)S(1)} %all_gather.6.refs_0_), channel_id=1, source_target_pairs={{0,32},{32,64},{64,96},{96,128},{128,160},{160,192},{192,224},{224... | collective-permute-start | bytes 393224 | tf_op jit(solution)/shard_map/ppermute | solution.py:39
  16.1 10.4 %collective-permute-start.2 = (bf16[4,128,128]{2,1,0:T(8,128)(2,1)S(1)}, bf16[4,128,128]{2,1,0:T(8,128)(2,1)S(1)}, u32[]{:S(2)}, u32[]{:S(2)}) collective-permute-start(bf16[4,128,128]{2,1,0:T(8,128)(2,1)S(1)} %collective-permute-done.refs_1_), channel_id=1, source_target_pairs={{0,64},{32,96},{64,128},{96,160},{128,192},{160,224},{192,256},{22... | collective-permute-start | bytes 393224 | tf_op jit(solution)/shard_map/ppermute | solution.py:39
  19.5 57.3 %copy-start = (bf16[4096,1024]{1,0:T(8,128)(2,1)S(1)}, bf16[4096,1024]{1,0:T(8,128)(2,1)}, u32[]{:S(2)}) copy-start(bf16[4096,1024]{1,0:T(8,128)(2,1)} %weight_ref.1) | copy-start | bytes 25165828
  19.6 1.0 %copy-start.1 = (s32[16384]{0:T(1024)S(1)}, s32[16384]{0:T(1024)}, u32[]{:S(2)}) copy-start(s32[16384]{0:T(1024)} %param.8) | copy-start | bytes 196612
  21.3 9.9 %collective-permute-start.1 = (bf16[256,512]{1,0:T(8,128)(2,1)S(1)}, bf16[256,512]{1,0:T(8,128)(2,1)S(1)}, u32[]{:S(2)}, u32[]{:S(2)}) collective-permute-start(bf16[256,512]{1,0:T(8,128)(2,1)S(1)} %all_gather.7.mine_ref), channel_id=1, source_target_pairs={{0,16},{16,0},{1,17},{17,1},{2,18},{18,2},{3,19},{19,3},{4,20},{20... | collective-permute-start | bytes 786440 | tf_op jit(solution)/shard_map/ppermute | solution.py:197
  26.6 8.3 %collective-permute-start.3 = (bf16[8,128,128]{2,1,0:T(8,128)(2,1)S(1)}, bf16[8,128,128]{2,1,0:T(8,128)(2,1)S(1)}, u32[]{:S(2)}, u32[]{:S(2)}) collective-permute-start(bf16[8,128,128]{2,1,0:T(8,128)(2,1)S(1)} %pad_maximum_fusion), channel_id=1, source_target_pairs={{0,32},{32,64},{64,96},{96,128},{128,160},{160,192},{192,224},{224... | collective-permute-start | bytes 786440 | tf_op jit(solution)/shard_map/ppermute | solution.py:39

commit v10 on v9

--- a/solution.py
+++ b/solution.py
@@ -37,6 +37,11 @@
         (z * cores + c, (z + distances[c]) * cores + c) for c in range(cores) for z in range(planes - distances[c])
     ]
     return lax.ppermute(block, ("z", "c"), route)
+
+
+def place_kernel(place_ref, out_ref):
+    for i in range(2):
+        out_ref[i] = place_ref[i]
 
 
 def low_kernel(where_ref, segment_ref, out_ref):
@@ -170,33 +175,33 @@
     out_ref[...] = acc.astype(jnp.bfloat16)
 
 
-def small(kernel, name, shape, dtype, *args, smem=0, params=PARAMS):
+def small(kernel, name, shape, dtype, *args, smem=0, out=VREF):
     return pl.pallas_call(
         kernel,
         out_shape=jax.ShapeDtypeStruct(shape, dtype),
         in_specs=[SMEM] * smem + [VREF] * (len(args) - smem),
-        out_specs=VREF,
-        compiler_params=params,
+        out_specs=out,
+        compiler_params=PARAMS,
         cost_estimate=pl.CostEstimate(flops=1 << 20, bytes_accessed=1 << 19, transcendentals=0),
         name=name,
     )(*args)
 
 
 def on_device(queries, keys, values, segments, out_weight):
-    plane, lane = lax.axis_index("z"), lax.axis_index(("y", "c"))
-    where = jnp.stack([plane, lane]).astype(jnp.int32)
     is_key = lax.broadcasted_iota(jnp.int32, (2, BLK, HD), 0) == 0
     own = lax.all_gather(jnp.where(is_key, keys[None], values[None]), "c", tiled=True)
     come = shift_by_core(own, (1, 5))
     queries, _ = lax.optimization_barrier((queries, own))
     mine = lax.all_gather(queries, "c", tiled=True)
-    come, mine, segments = lax.optimization_barrier((come, mine, segments))
+    place = jnp.stack([lax.axis_index("z"), lax.axis_index(("y", "c"))]).astype(jnp.int32)
+    come, mine, place = lax.optimization_barrier((come, mine, place))
     passed = shift_by_core(come, (2, 2))
+    where = small(place_kernel, "place", (2,), jnp.int32, place, smem=1, out=SMEM)
+    mine, where = lax.optimization_barrier((mine, where))
+    other = lax.ppermute(mine, "y", [(0, 1), (1, 0)])
+    passed, segments, where = lax.optimization_barrier((passed, segments, where))
+    last = shift_by_core(jnp.concatenate([come, passed], axis=0), (1, 1))
     low = small(low_kernel, "low", (8, BLK), jnp.int32, where, segments.reshape(-1, BLK), smem=1)
-    mine, low = lax.optimization_barrier((mine, low))
-    other = lax.ppermute(mine, "y", [(0, 1), (1, 0)])
-    passed, low = lax.optimization_barrier((passed, low))
-    last = shift_by_core(jnp.concatenate([come, passed], axis=0), (1, 1))
     common = (where, mine, other, low)
     state = attend(True, *common, own, come, passed)
     partial = attend(False, *common, last, *state)

time: 79.1 us -> 79.5 us (level)
  the two profiles are of different devices: /device:TPU:352 before, /device:TPU:128 now
where the time goes in v10:
time: 79.5 us; the launch traced here: 79.1 us
  blocking collectives  47.6 us (60%)
  starting transfers between devices  18.5 us (23%)
  Pallas kernels  9 us (11%)
  waiting for transfers between devices  2.01 us (3%)
  other arithmetic  0.96 us (1%)
  local copies, waits for them, and re-layouts  0.84 us (1%)
    all_to_all x1, blocking collectives, on_device(): attended = lax.all_to_all(copies, 'h', 0, 0, tiled=True)  19.4 us
    all_to_all x1, blocking collectives, on_device(): parts = lax.all_to_all(partial, ('y', 'c'), 0, 0, tiled=True)  18 us
    ppermute x3, starting transfers between devices, shift_by_core(): return lax.ppermute(block, ('z', 'c'), route)  13.4 us
    all_gather x1, blocking collectives, on_device(): mine = lax.all_gather(queries, 'c', tiled=True)  8.35 us
    ppermute x1, starting transfers between devices, on_device(): other = lax.ppermute(mine, 'y', [(0, 1), (1, 0)])  5.1 us
    pallas_call x2, Pallas kernels, attend(): pl.pallas_call(functools.partial(attend_kernel, near), out_shape=out, in_...  4.89 us
    pallas_call x4, Pallas kernels, small(): pl.pallas_call(kernel, out_shape=jax.ShapeDtypeStruct(shape, dtype), in_s...  4.11 us
    ppermute x3, waiting for transfers between devices, shift_by_core(): return lax.ppermute(block, ('z', 'c'), route)  2 us
  transfers between devices with their start and end apart: 4, of which 2 were waited for; matrix products, arithmetic and copies ran while one was open for 0% of the time, Pallas kernels for 6%

profile of v10, /device:TPU:128, one launch (start us, length us, event | category | flops | bytes accessed | tf_op | source)
XLA Modules:
  0.0 79.1 jit_solution(9053141373250136372)
XLA Ops:
  0.0 0.9 %broadcast_select_fusion = bf16[2,128,128]{2,1,0:T(8,128)(2,1)S(1)} fusion(pred[2]{0:T(512)(128)(4,1)S(1)} %iota_compare_fusion, bf16[128,128]{1,0:T(8,128)(2,1)} %param.7, bf16[128,128]{1,0:T(8,128)(2,1)} %param.6), kind=kLoop, calls=%fused_computation.1 | loop fusion | flops 32768 | bytes 131074 | tf_op jit(solution)/shard_map/jit(_where)/select_n | solution.py:192
  0.9 1.9 %all_gather.6.refs_0_ = bf16[4,128,128]{2,1,0:T(8,128)(2,1)S(1)} all-gather(bf16[2,128,128]{2,1,0:T(8,128)(2,1)S(1)} %broadcast_select_fusion), channel_id=1, replica_groups=mesh['z'=32,'y'=2,'c'=2,'h'=8] {'c'}, dimensions={0}, use_global_device_ids=true | all-gather | bytes 196608 | tf_op jit(solution)/shard_map/all_gather | solution.py:192
  2.7 3.8 %collective-permute-start = (bf16[4,128,128]{2,1,0:T(8,128)(2,1)S(1)}, bf16[4,128,128]{2,1,0:T(8,128)(2,1)S(1)}, u32[]{:S(2)}, u32[]{:S(2)}) collective-permute-start(bf16[4,128,128]{2,1,0:T(8,128)(2,1)S(1)} %all_gather.6.refs_0_), channel_id=1, source_target_pairs={{0,32},{32,64},{64,96},{96,128},{128,160},{160,192},{192,224},{224... | collective-permute-start | bytes 393224 | tf_op jit(solution)/shard_map/ppermute | solution.py:39
  6.6 8.3 %all_gather.7.mine_ref = bf16[256,512]{1,0:T(8,128)(2,1)S(1)} all-gather(bf16[128,512]{1,0:T(8,128)(2,1)} %param.5), channel_id=1, replica_groups=mesh['z'=32,'y'=2,'c'=2,'h'=8] {'c'}, dimensions={0}, use_global_device_ids=true | all-gather | bytes 393216 | tf_op jit(solution)/shard_map/all_gather | solution.py:195
  14.9 0.0 copy-start
  14.9 0.1 pad_add_fusion.place_ref
  15.0 0.0 collective-permute-done.refs_1_
  15.0 5.4 %collective-permute-start.1 = (bf16[4,128,128]{2,1,0:T(8,128)(2,1)S(1)}, bf16[4,128,128]{2,1,0:T(8,128)(2,1)S(1)}, u32[]{:S(2)}, u32[]{:S(2)}) collective-permute-start(bf16[4,128,128]{2,1,0:T(8,128)(2,1)S(1)} %collective-permute-done.refs_1_), channel_id=1, source_target_pairs={{0,64},{32,96},{64,128},{96,160},{128,192},{160,224},{192,256},{22... | collective-permute-start | bytes 393224 | tf_op jit(solution)/shard_map/ppermute | solution.py:39
  20.4 1.1 %place.1.where_ref = s32[2]{0:T(128)S(1)} custom-call(s32[2]{0:T(128)S(1)} %pad_add_fusion.place_ref), custom_call_target="tpu_custom_call" | custom-call | flops 1048576 | bytes 524288 | tf_op jit(solution)/shard_map/place/pallas_call | solution.py:179
  21.6 5.1 %collective-permute-start.2 = (bf16[256,512]{1,0:T(8,128)(2,1)S(1)}, bf16[256,512]{1,0:T(8,128)(2,1)S(1)}, u32[]{:S(2)}, u32[]{:S(2)}) collective-permute-start(bf16[256,512]{1,0:T(8,128)(2,1)S(1)} %all_gather.7.mine_ref), channel_id=1, source_target_pairs={{0,16},{16,0},{1,17},{17,1},{2,18},{18,2},{3,19},{19,3},{4,20},{20... | collective-permute-start | bytes 786440 | tf_op jit(solution)/shard_map/ppermute | solution.py:201
  26.7 0.9 %collective-permute-done.1.refs_2_ = bf16[4,128,128]{2,1,0:T(8,128)(2,1)S(1)} collective-permute-done((bf16[4,128,128]{2,1,0:T(8,128)(2,1)S(1)}, bf16[4,128,128]{2,1,0:T(8,128)(2,1)S(1)}, u32[]{:S(2)}, u32[]{:S(2)}) %collective-permute-start.1) | collective-permute-done | bytes 131104 | tf_op jit(solution)/shard_map/ppermute | solution.py:39
  27.6 4.2 %collective-permute-start.3 = (bf16[8,128,128]{2,1,0:T(8,128)(2,1)S(1)}, bf16[8,128,128]{2,1,0:T(8,128)(2,1)S(1)}, u32[]{:S(2)}, u32[]{:S(2)}) collective-permute-start(bf16[8,128,128]{2,1,0:T(8,128)(2,1)S(1)} %pad_maximum_fusion), channel_id=1, source_target_pairs={{0,32},{32,64},{64,96},{96,128},{128,160},{160,192},{192,224},{224... | collective-permute-start | bytes 786440 | tf_op jit(solution)/shard_map/ppermute | solution.py:39
  31.8 0.0 copy-start.1
  31.8 0.8 %copy-done.1 = s32[16384]{0:T(1024)S(1)} copy-done((s32[16384]{0:T(1024)S(1)}, s32[16384]{0:T(1024)}, u32[]{:S(2)}) %copy-start.1) | copy-done | bytes 65560
  32.6 0.7 low.1.low_ref
  33.3 0.0 collective-permute-done.2.other_ref
  33.3 2.6 %near.1 = (f32[4,128,512]{2,1,0:T(8,128)S(1)}, f32[4,8,512]{2,1,0:T(8,128)S(1)}) custom-call(s32[2]{0:T(128)S(1)} %place.1.where_ref, bf16[256,512]{1,0:T(8,128)(2,1)S(1)} %all_gather.7.mine_ref, bf16[256,512]{1,0:T(8,128)(2,1)S(1)} %collective-permute-done.2.other_ref, s32[8,128]{1,0:T(8,128)S(1)} %low.1.low_ref, ...), custom_call_target="tpu_custom_call" | custom-call | flops 671088640 | bytes 3145728 | tf_op jit(solution)/shard_map/near/pallas_call | solution.py:138
  35.9 1.1 %collective-permute-done.3.refs_0_ = bf16[8,128,128]{2,1,0:T(8,128)(2,1)S(1)} collective-permute-done((bf16[8,128,128]{2,1,0:T(8,128)(2,1)S(1)}, bf16[8,128,128]{2,1,0:T(8,128)(2,1)S(1)}, u32[]{:S(2)}, u32[]{:S(2)}) %collective-permute-start.3) | collective-permute-done | bytes 262176 | tf_op jit(solution)/shard_map/ppermute | solution.py:39
  37.1 2.3 %far.1 = bf16[4,144,512]{2,1,0:T(8,128)(2,1)S(1)} custom-call(s32[2]{0:T(128)S(1)} %place.1.where_ref, bf16[256,512]{1,0:T(8,128)(2,1)S(1)} %all_gather.7.mine_ref, bf16[256,512]{1,0:T(8,128)(2,1)S(1)} %collective-permute-done.2.other_ref, s32[8,128]{1,0:T(8,128)S(1)} %low.1.low_ref, bf16[8,128,128]{2,1,0:T(8,128)(2,1)S(1)} %collective-permute-done.3.refs_0_, ...), custom_call_target="tpu_custom_call" | custom-call | flops 536870912 | bytes 3145728 | tf_op jit(solution)/shard_map/far/pallas_call | solution.py:138
  39.4 18.0 %all_to_all.10.parts_ref = bf16[4,144,512]{2,1,0:T(8,128)(2,1)S(1)} all-to-all(bf16[4,144,512]{2,1,0:T(8,128)(2,1)S(1)} %far.1), channel_id=1, replica_groups=mesh['z'=32,'y'=2,'c'=2,'h'=8] {'y','c'}, dimensions={0} | all-to-all | bytes 1179648 | tf_op jit(solution)/shard_map/all_to_all | solution.py:208
  57.4 0.3 combine.1
  57.7 19.4 %all_to_all.11.rows_ref = bf16[8,128,512]{2,1,0:T(8,128)(2,1)S(1)} all-to-all(bf16[8,128,512]{2,1,0:T(8,128)(2,1)S(1)} %combine.1), channel_id=1, replica_groups=mesh['z'=32,'y'=2,'c'=2,'h'=8] {'h'}, dimensions={0} | all-to-all | bytes 2097152 | tf_op jit(solution)/shard_map/all_to_all | solution.py:210
  77.1 0.0 copy-done
  77.1 2.0 %project.1 = bf16[128,1024]{1,0:T(8,128)(2,1)} custom-call(bf16[8,128,512]{2,1,0:T(8,128)(2,1)S(1)} %all_to_all.11.rows_ref, bf16[4096,1024]{1,0:T(8,128)(2,1)S(1)} %copy-done), custom_call_target="tpu_custom_call" | custom-call | flops 1048576 | bytes 524288 | tf_op jit(solution)/shard_map/project/pallas_call | solution.py:179
  (2 shorter events, 0.0 us)
Async XLA Ops:
  2.7 12.3 %collective-permute-start = (bf16[4,128,128]{2,1,0:T(8,128)(2,1)S(1)}, bf16[4,128,128]{2,1,0:T(8,128)(2,1)S(1)}, u32[]{:S(2)}, u32[]{:S(2)}) collective-permute-start(bf16[4,128,128]{2,1,0:T(8,128)(2,1)S(1)} %all_gather.6.refs_0_), channel_id=1, source_target_pairs={{0,32},{32,64},{64,96},{96,128},{128,160},{160,192},{192,224},{224... | collective-permute-start | bytes 393224 | tf_op jit(solution)/shard_map/ppermute | solution.py:39
  14.9 62.2 %copy-start = (bf16[4096,1024]{1,0:T(8,128)(2,1)S(1)}, bf16[4096,1024]{1,0:T(8,128)(2,1)}, u32[]{:S(2)}) copy-start(bf16[4096,1024]{1,0:T(8,128)(2,1)} %weight_ref.1) | copy-start | bytes 25165828
  15.0 12.6 %collective-permute-start.1 = (bf16[4,128,128]{2,1,0:T(8,128)(2,1)S(1)}, bf16[4,128,128]{2,1,0:T(8,128)(2,1)S(1)}, u32[]{:S(2)}, u32[]{:S(2)}) collective-permute-start(bf16[4,128,128]{2,1,0:T(8,128)(2,1)S(1)} %collective-permute-done.refs_1_), channel_id=1, source_target_pairs={{0,64},{32,96},{64,128},{96,160},{128,192},{160,224},{192,256},{22... | collective-permute-start | bytes 393224 | tf_op jit(solution)/shard_map/ppermute | solution.py:39
  21.6 11.8 %collective-permute-start.2 = (bf16[256,512]{1,0:T(8,128)(2,1)S(1)}, bf16[256,512]{1,0:T(8,128)(2,1)S(1)}, u32[]{:S(2)}, u32[]{:S(2)}) collective-permute-start(bf16[256,512]{1,0:T(8,128)(2,1)S(1)} %all_gather.7.mine_ref), channel_id=1, source_target_pairs={{0,16},{16,0},{1,17},{17,1},{2,18},{18,2},{3,19},{19,3},{4,20},{20... | collective-permute-start | bytes 786440 | tf_op jit(solution)/shard_map/ppermute | solution.py:201
  27.6 9.5 %collective-permute-start.3 = (bf16[8,128,128]{2,1,0:T(8,128)(2,1)S(1)}, bf16[8,128,128]{2,1,0:T(8,128)(2,1)S(1)}, u32[]{:S(2)}, u32[]{:S(2)}) collective-permute-start(bf16[8,128,128]{2,1,0:T(8,128)(2,1)S(1)} %pad_maximum_fusion), channel_id=1, source_target_pairs={{0,32},{32,64},{64,96},{96,128},{128,160},{160,192},{192,224},{224... | collective-permute-start | bytes 786440 | tf_op jit(solution)/shard_map/ppermute | solution.py:39
  31.8 0.8 %copy-start.1 = (s32[16384]{0:T(1024)S(1)}, s32[16384]{0:T(1024)}, u32[]{:S(2)}) copy-start(s32[16384]{0:T(1024)} %param.8) | copy-start | bytes 196612

commit v11 on v9

--- a/solution.py
+++ b/solution.py
@@ -39,18 +39,22 @@
     return lax.ppermute(block, ("z", "c"), route)
 
 
-def low_kernel(where_ref, segment_ref, out_ref):
+def floor_kernel(where_ref, out_ref):
+    row = lax.broadcasted_iota(jnp.int32, (8, BLK), 0)
+    token = lax.broadcasted_iota(jnp.int32, (8, BLK), 1)
+    out_ref[...] = where_ref[0] * PLANE + row * BLK + token - (WINDOW - 1)
+
+
+def low_kernel(where_ref, segment_ref, floor_ref, out_ref):
     segments = segment_ref[...]
     before = [jnp.sum((segments < v).astype(jnp.int32)) for v in range(1, SEGMENT_VALUES)]
-    token = lax.broadcasted_iota(jnp.int32, (1, BLK), 1)
     for p in range(LANES):
         own = segment_ref[pl.ds(where_ref[0] * LANES + p, 1), :]
         start = jnp.zeros((1, BLK), jnp.int32)
         for v in range(1, SEGMENT_VALUES):
             start = jnp.where(own == v, before[v - 1], start)
-        position = where_ref[0] * PLANE + p * BLK + token
-        out_ref[p : p + 1] = jnp.maximum(start, position - (WINDOW - 1))
-    out_ref[LANES:] = jnp.zeros((8 - LANES, BLK), jnp.int32)
+        out_ref[p : p + 1] = jnp.maximum(start, floor_ref[p : p + 1])
+    out_ref[LANES:] = floor_ref[LANES:]
 
 
 def attend_kernel(near, where_ref, mine_ref, other_ref, low_ref, *refs):
@@ -170,33 +174,33 @@
     out_ref[...] = acc.astype(jnp.bfloat16)
 
 
-def small(kernel, name, shape, dtype, *args, smem=0, params=PARAMS):
+def small(kernel, name, shape, dtype, *args, smem=0):
     return pl.pallas_call(
         kernel,
         out_shape=jax.ShapeDtypeStruct(shape, dtype),
         in_specs=[SMEM] * smem + [VREF] * (len(args) - smem),
         out_specs=VREF,
-        compiler_params=params,
+        compiler_params=PARAMS,
         cost_estimate=pl.CostEstimate(flops=1 << 20, bytes_accessed=1 << 19, transcendentals=0),
         name=name,
     )(*args)
 
 
 def on_device(queries, keys, values, segments, out_weight):
-    plane, lane = lax.axis_index("z"), lax.axis_index(("y", "c"))
-    where = jnp.stack([plane, lane]).astype(jnp.int32)
     is_key = lax.broadcasted_iota(jnp.int32, (2, BLK, HD), 0) == 0
     own = lax.all_gather(jnp.where(is_key, keys[None], values[None]), "c", tiled=True)
     come = shift_by_core(own, (1, 5))
     queries, _ = lax.optimization_barrier((queries, own))
     mine = lax.all_gather(queries, "c", tiled=True)
-    come, mine, segments = lax.optimization_barrier((come, mine, segments))
+    where = jnp.stack([lax.axis_index("z"), lax.axis_index(("y", "c"))]).astype(jnp.int32)
+    come, mine, where = lax.optimization_barrier((come, mine, where))
     passed = shift_by_core(come, (2, 2))
-    low = small(low_kernel, "low", (8, BLK), jnp.int32, where, segments.reshape(-1, BLK), smem=1)
-    mine, low = lax.optimization_barrier((mine, low))
+    floor = small(floor_kernel, "floor", (8, BLK), jnp.int32, where, smem=1)
+    mine, floor = lax.optimization_barrier((mine, floor))
     other = lax.ppermute(mine, "y", [(0, 1), (1, 0)])
-    passed, low = lax.optimization_barrier((passed, low))
+    passed, segments, floor = lax.optimization_barrier((passed, segments, floor))
     last = shift_by_core(jnp.concatenate([come, passed], axis=0), (1, 1))
+    low = small(low_kernel, "low", (8, BLK), jnp.int32, where, segments.reshape(-1, BLK), floor, smem=1)
     common = (where, mine, other, low)
     state = attend(True, *common, own, come, passed)
     partial = attend(False, *common, last, *state)

time: 79.1 us -> 79.5 us (level)
  the two profiles are of different devices: /device:TPU:352 before, /device:TPU:128 now
where the time goes in v11:
time: 79.5 us; the launch traced here: 79.1 us
  blocking collectives  47.1 us (59%)
  starting transfers between devices  17.9 us (23%)
  Pallas kernels  8.41 us (11%)
  waiting for transfers between devices  3.75 us (5%)
  other arithmetic  0.96 us (1%)
  local copies, waits for them, and re-layouts  0.84 us (1%)
    all_to_all x1, blocking collectives, on_device(): attended = lax.all_to_all(copies, 'h', 0, 0, tiled=True)  19.5 us
    all_to_all x1, blocking collectives, on_device(): parts = lax.all_to_all(partial, ('y', 'c'), 0, 0, tiled=True)  17.3 us
    ppermute x3, starting transfers between devices, shift_by_core(): return lax.ppermute(block, ('z', 'c'), route)  12.8 us
    all_gather x1, blocking collectives, on_device(): mine = lax.all_gather(queries, 'c', tiled=True)  8.35 us
    ppermute x1, starting transfers between devices, on_device(): other = lax.ppermute(mine, 'y', [(0, 1), (1, 0)])  5.1 us
    pallas_call x2, Pallas kernels, attend(): pl.pallas_call(functools.partial(attend_kernel, near), out_shape=out, in_...  4.9 us
    ppermute x3, waiting for transfers between devices, shift_by_core(): return lax.ppermute(block, ('z', 'c'), route)  3.75 us
    pallas_call x4, Pallas kernels, small(): pl.pallas_call(kernel, out_shape=jax.ShapeDtypeStruct(shape, dtype), in_s...  3.51 us
  transfers between devices with their start and end apart: 4, of which 2 were waited for; matrix products, arithmetic and copies ran while one was open for 0% of the time, Pallas kernels for 5%

profile of v11, /device:TPU:128, one launch (start us, length us, event | category | flops | bytes accessed | tf_op | source)
XLA Modules:
  0.0 79.1 jit_solution(16365546071834489031)
XLA Ops:
  0.0 0.9 %broadcast_select_fusion = bf16[2,128,128]{2,1,0:T(8,128)(2,1)S(1)} fusion(pred[2]{0:T(512)(128)(4,1)S(1)} %iota_compare_fusion, bf16[128,128]{1,0:T(8,128)(2,1)} %param.7, bf16[128,128]{1,0:T(8,128)(2,1)} %param.6), kind=kLoop, calls=%fused_computation.1 | loop fusion | flops 32768 | bytes 131074 | tf_op jit(solution)/shard_map/jit(_where)/select_n | solution.py:191
  0.9 1.9 %all_gather.6.refs_0_ = bf16[4,128,128]{2,1,0:T(8,128)(2,1)S(1)} all-gather(bf16[2,128,128]{2,1,0:T(8,128)(2,1)S(1)} %broadcast_select_fusion), channel_id=1, replica_groups=mesh['z'=32,'y'=2,'c'=2,'h'=8] {'c'}, dimensions={0}, use_global_device_ids=true | all-gather | bytes 196608 | tf_op jit(solution)/shard_map/all_gather | solution.py:191
  2.7 3.8 %collective-permute-start = (bf16[4,128,128]{2,1,0:T(8,128)(2,1)S(1)}, bf16[4,128,128]{2,1,0:T(8,128)(2,1)S(1)}, u32[]{:S(2)}, u32[]{:S(2)}) collective-permute-start(bf16[4,128,128]{2,1,0:T(8,128)(2,1)S(1)} %all_gather.6.refs_0_), channel_id=1, source_target_pairs={{0,32},{32,64},{64,96},{96,128},{128,160},{160,192},{192,224},{224... | collective-permute-start | bytes 393224 | tf_op jit(solution)/shard_map/ppermute | solution.py:39
  6.6 8.3 %all_gather.7.mine_ref = bf16[256,512]{1,0:T(8,128)(2,1)S(1)} all-gather(bf16[128,512]{1,0:T(8,128)(2,1)} %param.5), channel_id=1, replica_groups=mesh['z'=32,'y'=2,'c'=2,'h'=8] {'c'}, dimensions={0}, use_global_device_ids=true | all-gather | bytes 393216 | tf_op jit(solution)/shard_map/all_gather | solution.py:194
  14.9 0.0 copy-start
  14.9 0.1 pad_add_fusion.where_ref
  15.0 0.0 collective-permute-done.refs_1_
  15.0 5.4 %collective-permute-start.2 = (bf16[4,128,128]{2,1,0:T(8,128)(2,1)S(1)}, bf16[4,128,128]{2,1,0:T(8,128)(2,1)S(1)}, u32[]{:S(2)}, u32[]{:S(2)}) collective-permute-start(bf16[4,128,128]{2,1,0:T(8,128)(2,1)S(1)} %collective-permute-done.refs_1_), channel_id=1, source_target_pairs={{0,64},{32,96},{64,128},{96,160},{128,192},{160,224},{192,256},{22... | collective-permute-start | bytes 393224 | tf_op jit(solution)/shard_map/ppermute | solution.py:39
  20.4 0.5 floor.1.floor_ref
  21.0 5.1 %collective-permute-start.1 = (bf16[256,512]{1,0:T(8,128)(2,1)S(1)}, bf16[256,512]{1,0:T(8,128)(2,1)S(1)}, u32[]{:S(2)}, u32[]{:S(2)}) collective-permute-start(bf16[256,512]{1,0:T(8,128)(2,1)S(1)} %all_gather.7.mine_ref), channel_id=1, source_target_pairs={{0,16},{16,0},{1,17},{17,1},{2,18},{18,2},{3,19},{19,3},{4,20},{20... | collective-permute-start | bytes 786440 | tf_op jit(solution)/shard_map/ppermute | solution.py:200
  26.1 1.5 %collective-permute-done.2.refs_2_ = bf16[4,128,128]{2,1,0:T(8,128)(2,1)S(1)} collective-permute-done((bf16[4,128,128]{2,1,0:T(8,128)(2,1)S(1)}, bf16[4,128,128]{2,1,0:T(8,128)(2,1)S(1)}, u32[]{:S(2)}, u32[]{:S(2)}) %collective-permute-start.2) | collective-permute-done | bytes 131104 | tf_op jit(solution)/shard_map/ppermute | solution.py:39
  27.6 3.6 %collective-permute-start.3 = (bf16[8,128,128]{2,1,0:T(8,128)(2,1)S(1)}, bf16[8,128,128]{2,1,0:T(8,128)(2,1)S(1)}, u32[]{:S(2)}, u32[]{:S(2)}) collective-permute-start(bf16[8,128,128]{2,1,0:T(8,128)(2,1)S(1)} %pad_maximum_fusion), channel_id=1, source_target_pairs={{0,32},{32,64},{64,96},{96,128},{128,160},{160,192},{192,224},{224... | collective-permute-start | bytes 786440 | tf_op jit(solution)/shard_map/ppermute | solution.py:39
  31.2 0.0 copy-start.1
  31.2 0.8 %copy-done.1 = s32[16384]{0:T(1024)S(1)} copy-done((s32[16384]{0:T(1024)S(1)}, s32[16384]{0:T(1024)}, u32[]{:S(2)}) %copy-start.1) | copy-done | bytes 65560
  32.0 0.7 low.1.low_ref
  32.7 0.0 collective-permute-done.1.other_ref
  32.8 2.6 %near.1 = (f32[4,128,512]{2,1,0:T(8,128)S(1)}, f32[4,8,512]{2,1,0:T(8,128)S(1)}) custom-call(s32[2]{0:T(128)S(1)} %pad_add_fusion.where_ref, bf16[256,512]{1,0:T(8,128)(2,1)S(1)} %all_gather.7.mine_ref, bf16[256,512]{1,0:T(8,128)(2,1)S(1)} %collective-permute-done.1.other_ref, s32[8,128]{1,0:T(8,128)S(1)} %low.1.low_ref, ...), custom_call_target="tpu_custom_call" | custom-call | flops 671088640 | bytes 3145728 | tf_op jit(solution)/shard_map/near/pallas_call | solution.py:137
  35.3 2.3 %collective-permute-done.3.refs_0_ = bf16[8,128,128]{2,1,0:T(8,128)(2,1)S(1)} collective-permute-done((bf16[8,128,128]{2,1,0:T(8,128)(2,1)S(1)}, bf16[8,128,128]{2,1,0:T(8,128)(2,1)S(1)}, u32[]{:S(2)}, u32[]{:S(2)}) %collective-permute-start.3) | collective-permute-done | bytes 262176 | tf_op jit(solution)/shard_map/ppermute | solution.py:39
  37.6 2.3 %far.1 = bf16[4,144,512]{2,1,0:T(8,128)(2,1)S(1)} custom-call(s32[2]{0:T(128)S(1)} %pad_add_fusion.where_ref, bf16[256,512]{1,0:T(8,128)(2,1)S(1)} %all_gather.7.mine_ref, bf16[256,512]{1,0:T(8,128)(2,1)S(1)} %collective-permute-done.1.other_ref, s32[8,128]{1,0:T(8,128)S(1)} %low.1.low_ref, bf16[8,128,128]{2,1,0:T(8,128)(2,1)S(1)} %collective-permute-done.3.refs_0_, ...), custom_call_target="tpu_custom_call" | custom-call | flops 536870912 | bytes 3145728 | tf_op jit(solution)/shard_map/far/pallas_call | solution.py:137
  40.0 17.3 %all_to_all.10.parts_ref = bf16[4,144,512]{2,1,0:T(8,128)(2,1)S(1)} all-to-all(bf16[4,144,512]{2,1,0:T(8,128)(2,1)S(1)} %far.1), channel_id=1, replica_groups=mesh['z'=32,'y'=2,'c'=2,'h'=8] {'y','c'}, dimensions={0} | all-to-all | bytes 1179648 | tf_op jit(solution)/shard_map/all_to_all | solution.py:207
  57.3 0.3 combine.1
  57.6 19.5 %all_to_all.11.rows_ref = bf16[8,128,512]{2,1,0:T(8,128)(2,1)S(1)} all-to-all(bf16[8,128,512]{2,1,0:T(8,128)(2,1)S(1)} %combine.1), channel_id=1, replica_groups=mesh['z'=32,'y'=2,'c'=2,'h'=8] {'h'}, dimensions={0} | all-to-all | bytes 2097152 | tf_op jit(solution)/shard_map/all_to_all | solution.py:209
  77.1 0.0 copy-done
  77.1 2.0 %project.1 = bf16[128,1024]{1,0:T(8,128)(2,1)} custom-call(bf16[8,128,512]{2,1,0:T(8,128)(2,1)S(1)} %all_to_all.11.rows_ref, bf16[4096,1024]{1,0:T(8,128)(2,1)S(1)} %copy-done), custom_call_target="tpu_custom_call" | custom-call | flops 1048576 | bytes 524288 | tf_op jit(solution)/shard_map/project/pallas_call | solution.py:178
  (2 shorter events, 0.0 us)
Async XLA Ops:
  2.7 12.3 %collective-permute-start = (bf16[4,128,128]{2,1,0:T(8,128)(2,1)S(1)}, bf16[4,128,128]{2,1,0:T(8,128)(2,1)S(1)}, u32[]{:S(2)}, u32[]{:S(2)}) collective-permute-start(bf16[4,128,128]{2,1,0:T(8,128)(2,1)S(1)} %all_gather.6.refs_0_), channel_id=1, source_target_pairs={{0,32},{32,64},{64,96},{96,128},{128,160},{160,192},{192,224},{224... | collective-permute-start | bytes 393224 | tf_op jit(solution)/shard_map/ppermute | solution.py:39
  14.9 62.2 %copy-start = (bf16[4096,1024]{1,0:T(8,128)(2,1)S(1)}, bf16[4096,1024]{1,0:T(8,128)(2,1)}, u32[]{:S(2)}) copy-start(bf16[4096,1024]{1,0:T(8,128)(2,1)} %weight_ref.1) | copy-start | bytes 25165828
  15.0 12.6 %collective-permute-start.2 = (bf16[4,128,128]{2,1,0:T(8,128)(2,1)S(1)}, bf16[4,128,128]{2,1,0:T(8,128)(2,1)S(1)}, u32[]{:S(2)}, u32[]{:S(2)}) collective-permute-start(bf16[4,128,128]{2,1,0:T(8,128)(2,1)S(1)} %collective-permute-done.refs_1_), channel_id=1, source_target_pairs={{0,64},{32,96},{64,128},{96,160},{128,192},{160,224},{192,256},{22... | collective-permute-start | bytes 393224 | tf_op jit(solution)/shard_map/ppermute | solution.py:39
  21.0 11.8 %collective-permute-start.1 = (bf16[256,512]{1,0:T(8,128)(2,1)S(1)}, bf16[256,512]{1,0:T(8,128)(2,1)S(1)}, u32[]{:S(2)}, u32[]{:S(2)}) collective-permute-start(bf16[256,512]{1,0:T(8,128)(2,1)S(1)} %all_gather.7.mine_ref), channel_id=1, source_target_pairs={{0,16},{16,0},{1,17},{17,1},{2,18},{18,2},{3,19},{19,3},{4,20},{20... | collective-permute-start | bytes 786440 | tf_op jit(solution)/shard_map/ppermute | solution.py:200
  27.6 10.0 %collective-permute-start.3 = (bf16[8,128,128]{2,1,0:T(8,128)(2,1)S(1)}, bf16[8,128,128]{2,1,0:T(8,128)(2,1)S(1)}, u32[]{:S(2)}, u32[]{:S(2)}) collective-permute-start(bf16[8,128,128]{2,1,0:T(8,128)(2,1)S(1)} %pad_maximum_fusion), channel_id=1, source_target_pairs={{0,32},{32,64},{64,96},{96,128},{128,160},{160,192},{192,224},{224... | collective-permute-start | bytes 786440 | tf_op jit(solution)/shard_map/ppermute | solution.py:39
  31.2 0.8 %copy-start.1 = (s32[16384]{0:T(1024)S(1)}, s32[16384]{0:T(1024)}, u32[]{:S(2)}) copy-start(s32[16384]{0:T(1024)} %param.8) | copy-start | bytes 196612
